TPU v7x, 128 devices: a whole 4x4x4 slice. The times are simulated.
128 devices in a mesh: node: 16 (over x, z), local: 8 (over y, core).
Axes of the slice: x: 4, y: 4, z: 4, core: 2. Of those that a mesh axis runs over, the one named last changes fastest.
Arguments:
- activations: bfloat16 [16384, 2048], P(('node', 'local')), may hold values from -6 to 6
- expert_ids: int32 [16384, 8], P(('node', 'local')), may hold values from 0 to 127, as said below
- route_gates: bfloat16 [16384, 8], P(('node', 'local')), may hold values from 0.19921875 to 0.796875
- gate_proj: bfloat16 [128, 2048, 768], P(('node', 'local')), may hold values from -0.125 to 0.125
- up_proj: bfloat16 [128, 2048, 768], P(('node', 'local')), may hold values from -0.125 to 0.125
- down_proj: bfloat16 [128, 768, 2048], P(('node', 'local')), may hold values from -0.21875 to 0.21875
Outputs:
- moe_out: bfloat16 [16384, 2048], P(('node', 'local'))
Inputs may be any that keep to these rules, and one draw needn't show every extreme that they name: `expert_ids`: group k holds experts k * 8 to k * 8 + 7. Entries 2i and 2i+1 of a token's list name two different experts of one group, and a token's pairs name 4 different groups. Of the 128 tokens of one device (aligned blocks of rows), exactly 32 choose each group. Each group has one expert, its busiest, that is named by exactly 16 tokens of every device; every other expert is named by at most 8 tokens of one device, and in each block some expert of each group is named by exactly 8.
All inputs are finite; a program needn't handle non-finite values.
Results may differ from a plain program's by a relative error of at most 0.012.
Values may be sent and summed in bfloat16 or wider, within the bound.
No kernel may reach another device: no remote copies, remote signals or barrier semaphores. Data moves between devices by JAX's collectives and lax.ppermute only.
A program may use at most 128 MiB of HBM per device.

v0:
```python
import jax
import jax.numpy as jnp
from jax import lax
from jax.sharding import PartitionSpec as P


def expert_apply(row_block, gate_w, up_w, down_w):
    gate_h = jnp.dot(row_block, gate_w, preferred_element_type=jnp.float32)
    up_h = jnp.dot(row_block, up_w, preferred_element_type=jnp.float32)
    hidden_act = (jax.nn.silu(gate_h) * up_h).astype(jnp.bfloat16)
    return jnp.dot(hidden_act, down_w, preferred_element_type=jnp.float32).astype(jnp.bfloat16)


def ranks_of(label_list, label_count):
    onehot = (label_list[:, None] == jnp.arange(label_count, dtype=jnp.int32)[None, :]).astype(
        jnp.int32
    )
    return jnp.sum(jnp.cumsum(onehot, axis=0) * onehot, axis=1) - 1


def pair_sums(pair_outs, pair_gates):
    weighted = pair_gates.astype(jnp.float32)[:, :, None] * pair_outs.astype(jnp.float32)
    return jnp.sum(weighted, axis=1).astype(jnp.bfloat16)


def shards(activations, expert_ids, route_gates, gate_proj, up_proj, down_proj):
    tok_rows = activations.shape[0]
    model_width = activations.shape[1]
    top_count = expert_ids.shape[1]
    pair_count = top_count // 2
    node_count = lax.axis_size("node")
    local_count = lax.axis_size("local")
    expert_count = node_count * local_count
    node_rows = tok_rows * pair_count // node_count
    slot_cap = min(4 * node_rows // local_count, node_rows - node_rows // 4)
    gate_w = gate_proj[0]
    up_w = up_proj[0]
    down_w = down_proj[0]
    flat_ids = expert_ids.reshape(-1)
    slot_ranks = ranks_of(flat_ids, expert_count)
    token_of = jnp.arange(tok_rows * top_count, dtype=jnp.int32) // top_count
    send_buf = jnp.zeros((expert_count, slot_cap, model_width), jnp.bfloat16)
    send_buf = send_buf.at[flat_ids, slot_ranks].set(activations[token_of])
    received = lax.all_to_all(send_buf, ("node", "local"), split_axis=0, concat_axis=0, tiled=True)
    row_shape = received.shape
    flat_rows = received.reshape(-1, model_width)
    returned = lax.all_to_all(
        expert_apply(flat_rows, gate_w, up_w, down_w).reshape(row_shape),
        ("node", "local"),
        split_axis=0,
        concat_axis=0,
        tiled=True,
    )
    pair_outs = returned[flat_ids, slot_ranks].reshape(tok_rows * pair_count, 2, model_width)
    pair_vals = pair_sums(pair_outs, route_gates.reshape(tok_rows * pair_count, 2))
    summed = jnp.sum(
        pair_vals.reshape(tok_rows, pair_count, model_width).astype(jnp.float32), axis=1
    )
    return summed.astype(jnp.bfloat16)


def solution(mesh):
    in_specs = (
        P(("node", "local"), None),
        P(("node", "local"), None),
        P(("node", "local"), None),
        P(("node", "local"), None, None),
        P(("node", "local"), None, None),
        P(("node", "local"), None, None),
    )
    out_specs = P(("node", "local"), None)
    return jax.shard_map(shards, mesh=mesh, in_specs=in_specs, out_specs=out_specs, check_vma=False)
```

profile of v0, /device:TPU:2, one launch (start us, length us, event | category | flops | bytes accessed | tf_op | source)
XLA Modules:
  0.0 343.2 jit_solution(15250470700888117549)
XLA Ops:
  0.0 0.9 copy.20
  1.1 0.1 reshape.131
  1.2 0.1 copy.23
  1.3 0.2 fusion.10
  1.6 0.8 copy-done.3
  2.4 1.1 broadcast_add_fusion
  3.5 0.1 copy.24
  3.6 0.4 fusion.9
  4.0 0.7 multiply_reduce_fusion.1
  4.7 0.8 and_reduce_fusion
  5.5 25.4 %scatter_custom_fusion = bf16[2048,2048]{1,0:T(8,128)(2,1)} fusion(s32[1024]{0:T(1024)S(1)} %get-tuple-element.11, bf16[128,2048]{1,0:T(8,128)(2,1)} %param.6, s32[1024]{0:T(1024)S(1)} %get-tuple-element.10, bf16[]{:T(256)} %constant.29.clone.1), kind=kCustom, calls=%fused_computation.6 | custom fusion | bytes 8389120
  30.8 108.1 %all_to_all.10 = bf16[128,16,2048]{2,1,0:T(8,128)(2,1)S(1)} all-to-all(bf16[128,16,2048]{2,1,0:T(8,128)(2,1)} %bitcast.28), channel_id=1, replica_groups=mesh['node'=16,'local'=8] {'node','local'}, dimensions={0} | all-to-all | bytes 16777216 | tf_op jit(solution)/shard_map/all_to_all | solution.py:44
  139.0 3.2 copy-done.2
  142.2 8.5 %fusion.6 = f32[2048,768]{1,0:T(8,128)} fusion(bf16[2048,2048]{1,0:T(8,128)(2,1)S(1)} %bitcast.30, bf16[1,2048,768]{2,1,0:T(8,128)(2,1)S(1)} %copy-done.5), kind=kOutput, calls=%fused_computation.11 | convolution fusion | flops 6442450944 | bytes 17825792 | tf_op jit(solution)/shard_map/dot_general | solution.py:8
  150.7 21.3 %convolution_convert_fusion = bf16[2048,2048]{1,0:T(8,128)(2,1)} fusion(f32[2048,768]{1,0:T(8,128)} %fusion.6, bf16[2048,2048]{1,0:T(8,128)(2,1)} %bitcast.31, bf16[1,768,2048]{2,1,0:T(8,128)(2,1)S(1)} %copy-done, bf16[1,2048,768]{2,1,0:T(8,128)(2,1)} %param.10), kind=kOutput, calls=%fused_computation.4 | convolution fusion | flops 12898533376 | bytes 29360128 | tf_op jit(solution)/shard_map/dot_general | solution.py:11
  172.0 9.0 %all-to-all-start.1 = ((bf16[128,16,2048]{2,1,0:T(8,128)(2,1)}), bf16[128,16,2048]{2,1,0:T(8,128)(2,1)}, u32[]{:S(2)}, u32[]{:S(2)}) async-start(bf16[128,16,2048]{2,1,0:T(8,128)(2,1)} %bitcast.29), calls=%async_computation.1 | async-start | bytes 16777216 | tf_op jit(solution)/shard_map/all_to_all | solution.py:47
  180.9 0.1 copy.19
  181.1 0.1 reshape.139
  181.2 102.6 %all-to-all-done.1 = bf16[128,16,2048]{2,1,0:T(8,128)(2,1)} async-done(((bf16[128,16,2048]{2,1,0:T(8,128)(2,1)}), bf16[128,16,2048]{2,1,0:T(8,128)(2,1)}, u32[]{:S(2)}, u32[]{:S(2)}) %all-to-all-start.1) | async-done | bytes 8388640 | tf_op jit(solution)/shard_map/all_to_all | solution.py:47
  283.8 25.5 %gather_fusion = bf16[1024,2048]{1,0:T(8,128)(2,1)} fusion(bf16[128,16,2048]{2,1,0:T(8,128)(2,1)} %all-to-all-done.1, s32[1024]{0:T(1024)S(1)} %bitcast.27), kind=kCustom, calls=%fused_computation.1 | custom fusion | bytes 8396800 | tf_op jit(solution)/shard_map/gather | solution.py:54
  309.3 9.8 %reshape.140 = f32[512,2,2048]{2,1,0:T(2,128)} reshape(bf16[1024,2048]{1,0:T(8,128)(2,1)} %gather_fusion) | data formatting | bytes 12582912 | tf_op jit(solution)/shard_map/convert_element_type | solution.py:22
  319.1 15.1 %multiply_reduce_fusion = bf16[512,2048]{1,0:T(8,128)(2,1)} fusion(f32[512,2,2048]{2,1,0:T(2,128)} %reshape.140, f32[512,2]{1,0:T(8,128)S(1)} %reshape.139), kind=kLoop, calls=%fused_computation.3 | loop fusion | flops 3145728 | bytes 10489856 | tf_op jit(solution)/shard_map/reduce_sum | solution.py:23
  334.1 4.1 %convert_element_type.44 = bf16[128,4,2048]{2,1,0:T(4,128)(2,1)} reshape(bf16[512,2048]{1,0:T(8,128)(2,1)} %multiply_reduce_fusion) | data formatting | bytes 4194304 | tf_op jit(solution)/shard_map/convert_element_type | solution.py:23
  338.3 5.0 %reduce_sum.32 = bf16[128,2048]{1,0:T(8,128)(2,1)} reduce(bf16[128,4,2048]{2,1,0:T(4,128)(2,1)} %convert_element_type.44, bf16[]{:T(256)} %constant.29.clone.1), dimensions={1}, to_apply=%region_5.6 | reduce | flops 786432 | bytes 2621442 | tf_op jit(solution)/shard_map/reduce_sum | solution.py:56
  (19 shorter events, 0.3 us)
Async XLA Ops:
  0.0 150.7 %copy-start = (bf16[1,768,2048]{2,1,0:T(8,128)(2,1)S(1)}, bf16[1,768,2048]{2,1,0:T(8,128)(2,1)}, u32[]{:S(2)}) copy-start(bf16[1,768,2048]{2,1,0:T(8,128)(2,1)} %param.11) | copy-start | bytes 9437188
  1.5 0.8 copy-start.3
  30.8 111.3 %copy-start.5 = (bf16[1,2048,768]{2,1,0:T(8,128)(2,1)S(1)}, bf16[1,2048,768]{2,1,0:T(8,128)(2,1)}, u32[]{:S(2)}) copy-start(bf16[1,2048,768]{2,1,0:T(8,128)(2,1)} %param.9) | copy-start | bytes 9437188
  138.9 3.2 copy-start.2
  172.0 9.0 %copy-start.4 = (bf16[128,8]{0,1:T(8,128)(2,1)S(1)}, bf16[128,8]{0,1:T(8,128)(2,1)}, u32[]{:S(2)}) copy-start(bf16[128,8]{0,1:T(8,128)(2,1)} %param.8) | copy-start | bytes 6148
  172.0 111.8 %all-to-all-start.1 = ((bf16[128,16,2048]{2,1,0:T(8,128)(2,1)}), bf16[128,16,2048]{2,1,0:T(8,128)(2,1)}, u32[]{:S(2)}, u32[]{:S(2)}) async-start(bf16[128,16,2048]{2,1,0:T(8,128)(2,1)} %bitcast.29), calls=%async_computation.1 | async-start | bytes 16777216 | tf_op jit(solution)/shard_map/all_to_all | solution.py:47
  309.3 34.0 %copy-start.1 = (bf16[1,768,2048]{2,1,0:T(8,128)(2,1)S(1)}, bf16[1,768,2048]{2,1,0:T(8,128)(2,1)}, u32[]{:S(2)}) copy-start(bf16[1,768,2048]{2,1,0:T(8,128)(2,1)} %param.11) | copy-start | bytes 9437188
where the time goes:
time: 349 us; the launch traced here: 343 us
  blocking collectives  108 us (31%)
  waiting for transfers between devices  103 us (30%)
  local copies, waits for them, and re-layouts  70.4 us (20%)
  matrix products  29.8 us (9%)
  other arithmetic  23.3 us (7%)
  starting transfers between devices  8.96 us (3%)
    all_to_all x1, blocking collectives, shards(): lax.all_to_all(send_buf, ('node', 'local'), split_axis=0, concat_axis=0,...  108 us
    all_to_all x1, waiting for transfers between devices, shards(): lax.all_to_all(expert_apply(flat_rows, gate_w, up_w, down_w).reshape(row_...  103 us
    unnamed x14, local copies, waits for them, and re-layouts  30.3 us
    gather x1, local copies, waits for them, and re-layouts, shards(): returned[flat_ids, slot_ranks]  25.5 us
    dot_general x1, matrix products, expert_apply(): jnp.dot(hidden_act, down_w, preferred_element_type=jnp.float32)  21.3 us
    reduce_sum x1, other arithmetic, pair_sums(): return jnp.sum(weighted, axis=1).astype(jnp.bfloat16)  15.1 us
    convert_element_type x1, local copies, waits for them, and re-layouts, pair_sums(): pair_outs.astype(jnp.float32)  9.8 us
    all_to_all x1, starting transfers between devices, shards(): lax.all_to_all(expert_apply(flat_rows, gate_w, up_w, down_w).reshape(row_...  8.96 us
  transfers between devices with their start and end apart: 1, of which 1 were waited for; matrix products, arithmetic and copies ran while one was open for 0% of the time, Pallas kernels for 0%

commit v1 on v0

v1 whole, which is shorter than its diff:
```python
import functools

import jax
import jax.numpy as jnp
from jax import lax
from jax.experimental import pallas as pl
from jax.experimental.pallas import tpu as pltpu
from jax.sharding import PartitionSpec as P

SLOTS = 8
SHIFT = 3
BF16 = jnp.bfloat16
F32 = jnp.float32
VMEM_BYTES = 48 * 1024 * 1024


def iota(shape, dim):
    return lax.broadcasted_iota(jnp.int32, shape, dim)


def indicator(mask):
    return jnp.where(mask, 1.0, 0.0).astype(F32)


def dot(left, right):
    return jnp.dot(left, right, preferred_element_type=F32)


def ranks_of(named):
    tokens = named.shape[1]
    earlier = indicator(iota((tokens, tokens), 0) < iota((tokens, tokens), 1))
    return dot(named.astype(BF16), earlier.astype(BF16))


def spread(values, slots):
    labels = values.shape[0]
    picks = indicator((iota((labels * slots, labels), 0) >> SHIFT) == iota((labels * slots, labels), 1))
    return dot(picks.astype(BF16), values.astype(BF16))


def group_sums(values, groups):
    experts = values.shape[0]
    per_group = experts // groups
    shape = (groups * SLOTS, experts)
    same = indicator((iota(shape, 0) >> SHIFT) == (iota(shape, 1) // per_group))
    return dot(same.astype(BF16), values.astype(BF16))


def marks_of(ids_ref, labels):
    total = indicator(labels == ids_ref[0:1, :])
    for entry in range(1, ids_ref.shape[0]):
        total = total + indicator(labels == ids_ref[entry : entry + 1, :])
    return total


def spill_codes(named, ranks):
    return named * jnp.maximum(ranks - (SLOTS - 1), 0.0)


def spill_kernel(groups, experts, ids_ref, acts_ref, out_ref):
    tokens = ids_ref.shape[1]
    named = marks_of(ids_ref, iota((experts, tokens), 0))
    codes = group_sums(spill_codes(named, ranks_of(named)), groups)
    slot = (iota(codes.shape, 0) & (SLOTS - 1)).astype(F32)
    out_ref[...] = dot(indicator(codes == slot + 1.0).astype(BF16), acts_ref[...]).astype(BF16)


def weight_kernel(groups, experts, ids_ref, gates_ref, main_ref, spill_ref):
    tokens = ids_ref.shape[1]
    labels = iota((experts, tokens), 0)
    named = marks_of(ids_ref, labels)
    gates = jnp.zeros((experts, tokens), F32)
    for entry in range(ids_ref.shape[0]):
        value = gates_ref[entry : entry + 1, :].astype(F32)
        gates = gates + jnp.where(labels == ids_ref[entry : entry + 1, :], value, 0.0)
    ranks = ranks_of(named)
    rank_rows = spread(jnp.where(named > 0.0, ranks, 99.0), SLOTS)
    gate_rows = spread(gates, SLOTS)
    slot = (iota(rank_rows.shape, 0) & (SLOTS - 1)).astype(F32)
    main_ref[...] = jnp.where(rank_rows == slot, gate_rows, 0.0).astype(BF16)
    codes = spill_codes(named, ranks)
    code_rows = group_sums(codes, groups)
    spill_rows = group_sums(jnp.where(codes > 0.0, gates, 0.0), groups)
    spill_slot = (iota(code_rows.shape, 0) & (SLOTS - 1)).astype(F32)
    spill_ref[...] = jnp.where(code_rows == spill_slot + 1.0, spill_rows, 0.0).astype(BF16)


def gather_kernel(groups, per_group, my_ref, ids_ref, acts_ref, out_ref):
    tokens = ids_ref.shape[1]
    named = marks_of(ids_ref, iota((groups, tokens), 0) * per_group + my_ref[0])
    rank_rows = spread(jnp.where(named > 0.0, ranks_of(named), 99.0), SLOTS)
    slot = (iota(rank_rows.shape, 0) & (SLOTS - 1)).astype(F32)
    rows = dot(indicator(rank_rows == slot).astype(BF16), acts_ref[...])
    out_ref[...] = rows.reshape(groups, 1, SLOTS, rows.shape[1]).astype(BF16)


def expert_kernel(on_ref, rows_ref, gate_hbm, up_hbm, down_hbm, out_ref, gate_w, up_w, down_w, sems):
    step = pl.program_id(0)
    busy = on_ref[0] != 0
    copies = [
        pltpu.make_async_copy(source.at[0], target, sems.at[place])
        for place, (source, target) in enumerate(((gate_hbm, gate_w), (up_hbm, up_w), (down_hbm, down_w)))
    ]

    @pl.when(busy & (step == 0))
    def _():
        for copy in copies:
            copy.start()

    def arrived(place):
        @pl.when(step == 0)
        def _():
            copies[place].wait()

    @pl.when(busy)
    def _():
        rows = rows_ref[...]
        arrived(0)
        gate_h = dot(rows, gate_w[...])
        arrived(1)
        up_h = dot(rows, up_w[...])
        hidden = (gate_h / (1.0 + jnp.exp(-gate_h)) * up_h).astype(BF16)
        arrived(2)
        out_ref[...] = dot(hidden, down_w[...]).astype(BF16)

    @pl.when(jnp.logical_not(busy))
    def _():
        out_ref[...] = jnp.zeros(out_ref.shape, BF16)


def combine_kernel(main_w_ref, spill_w_ref, main_ref, spill_ref, out_ref):
    over_rows = (((0,), (0,)), ((), ()))
    total = lax.dot_general(main_w_ref[...], main_ref[...], over_rows, preferred_element_type=F32)
    total += lax.dot_general(spill_w_ref[...], spill_ref[...], over_rows, preferred_element_type=F32)
    out_ref[...] = total.astype(BF16)


def params():
    return pltpu.CompilerParams(vmem_limit_bytes=VMEM_BYTES)


def whole():
    return pl.BlockSpec(memory_space=pltpu.VMEM)


def scalar():
    return pl.BlockSpec(memory_space=pltpu.SMEM)


def apply_expert(on, rows, gate_proj, up_proj, down_proj):
    count, width = rows.shape
    hidden = gate_proj.shape[2]
    block = min(256, count)
    anywhere = pl.BlockSpec(memory_space=pl.ANY)
    return pl.pallas_call(
        expert_kernel,
        grid=(count // block,),
        in_specs=[scalar(), pl.BlockSpec((block, width), lambda i: (i, 0)), anywhere, anywhere, anywhere],
        out_specs=pl.BlockSpec((block, width), lambda i: (i, 0)),
        out_shape=jax.ShapeDtypeStruct((count, width), BF16),
        scratch_shapes=[
            pltpu.VMEM((width, hidden), BF16),
            pltpu.VMEM((width, hidden), BF16),
            pltpu.VMEM((hidden, width), BF16),
            pltpu.SemaphoreType.DMA((3,)),
        ],
        compiler_params=params(),
        cost_estimate=pl.CostEstimate(
            flops=6 * count * width * hidden,
            bytes_accessed=4 * count * width + 6 * width * hidden,
            transcendentals=count * hidden,
        ),
        name="expert",
    )(on, rows, gate_proj, up_proj, down_proj)


def shards(activations, expert_ids, route_gates, gate_proj, up_proj, down_proj):
    tokens, width = activations.shape
    top = expert_ids.shape[1]
    groups = lax.axis_size("node")
    per_group = lax.axis_size("local")
    experts = groups * per_group
    my_local = lax.axis_index("local").astype(jnp.int32)
    my_expert = lax.axis_index("node").astype(jnp.int32) * per_group + my_local
    id_rows = expert_ids.T
    gate_rows = route_gates.T

    acts_all = lax.all_gather(activations, "local", tiled=True)
    ids_all = lax.all_gather(id_rows, "local", tiled=True)

    spill = pl.pallas_call(
        functools.partial(spill_kernel, groups, experts),
        in_specs=[whole(), whole()],
        out_specs=whole(),
        out_shape=jax.ShapeDtypeStruct((groups * SLOTS, width), BF16),
        compiler_params=params(),
        name="spill_rows",
    )(id_rows, activations)
    spill_in = lax.all_to_all(spill.reshape(groups, SLOTS, width), "node", split_axis=0, concat_axis=0, tiled=True)
    spill_all = lax.all_gather(spill_in.reshape(groups * SLOTS, width), "local", tiled=True)

    main_w, spill_w = pl.pallas_call(
        functools.partial(weight_kernel, groups, experts),
        in_specs=[whole(), whole()],
        out_specs=[whole(), whole()],
        out_shape=[
            jax.ShapeDtypeStruct((experts * SLOTS, tokens), BF16),
            jax.ShapeDtypeStruct((groups * SLOTS, tokens), BF16),
        ],
        compiler_params=params(),
        name="combine_weights",
    )(id_rows, gate_rows)

    main = pl.pallas_call(
        functools.partial(gather_kernel, groups, per_group),
        grid=(per_group,),
        in_specs=[
            scalar(),
            pl.BlockSpec((top, tokens), lambda i: (i, 0)),
            pl.BlockSpec((tokens, width), lambda i: (i, 0)),
        ],
        out_specs=pl.BlockSpec((groups, 1, SLOTS, width), lambda i: (0, i, 0, 0)),
        out_shape=jax.ShapeDtypeStruct((groups, per_group, SLOTS, width), BF16),
        compiler_params=params(),
        name="main_rows",
    )(my_local.reshape(1), ids_all, acts_all)
    main_in = lax.all_to_all(
        main.reshape(groups, per_group * SLOTS, width), "node", split_axis=0, concat_axis=0, tiled=True
    )

    busiest = (jnp.sum((expert_ids == my_expert).astype(jnp.int32)) > SLOTS).astype(jnp.int32).reshape(1)
    spill_out = apply_expert(busiest, spill_all, gate_proj, up_proj, down_proj)
    spill_back = lax.psum_scatter(spill_out, "local", tiled=True)

    always = jnp.ones((1,), jnp.int32)
    main_out = apply_expert(always, main_in.reshape(experts * SLOTS, width), gate_proj, up_proj, down_proj)
    main_back = lax.all_to_all(
        main_out.reshape(experts, SLOTS, width), ("node", "local"), split_axis=0, concat_axis=0, tiled=True
    )
    spill_home = lax.all_to_all(
        spill_back.reshape(groups, SLOTS, width), "node", split_axis=0, concat_axis=0, tiled=True
    )

    columns = min(512, width)
    return pl.pallas_call(
        combine_kernel,
        grid=(width // columns,),
        in_specs=[
            pl.BlockSpec((experts * SLOTS, tokens), lambda i: (0, 0)),
            pl.BlockSpec((groups * SLOTS, tokens), lambda i: (0, 0)),
            pl.BlockSpec((experts * SLOTS, columns), lambda i: (0, i)),
            pl.BlockSpec((groups * SLOTS, columns), lambda i: (0, i)),
        ],
        out_specs=pl.BlockSpec((tokens, columns), lambda i: (0, i)),
        out_shape=jax.ShapeDtypeStruct((tokens, width), BF16),
        compiler_params=params(),
        name="combine",
    )(main_w, spill_w, main_back.reshape(experts * SLOTS, width), spill_home.reshape(groups * SLOTS, width))


def solution(mesh):
    rows = P(("node", "local"), None)
    stacks = P(("node", "local"), None, None)
    return jax.shard_map(
        shards, mesh=mesh, in_specs=(rows, rows, rows, stacks, stacks, stacks), out_specs=rows, check_vma=False
    )
```

time: 349 us -> 230 us (0.66)
  local copies, waits for them, and re-layouts: 70.4 us -> 5.84 us
  waiting for transfers between devices: 103 us -> 60.5 us
  Pallas kernels: 0 us -> 33 us
  matrix products: 29.8 us -> 0 us
  other arithmetic: 23.3 us -> 1.34 us
  between operations: 0.1 us -> 13.8 us
  blocking collectives: 108 us -> 99.5 us
  starting transfers between devices: 8.96 us -> 13.1 us
    all_to_all x1 -> x2, waiting for transfers between devices: 103 us -> 41.5 us  [the longest x1 32.9 us: shards(): lax.all_to_all(main.reshape(groups, per_group * SLOTS, width), 'node', sp...]
    pallas_call x0 -> x6, Pallas kernels: none -> 33 us  [the longest x2 22.2 us: apply_expert(): pl.pallas_call(expert_kernel, grid=(count // block,), in_specs=[scalar(),...]
    dot_general x2 -> x0, matrix products: 29.8 us -> none  [the longest x1 21.3 us: expert_apply(): jnp.dot(hidden_act, down_w, preferred_element_type=jnp.float32)]
    gather x1 -> x0, local copies, waits for them, and re-layouts: 25.5 us -> none  [shards(): returned[flat_ids, slot_ranks]]
    unnamed x14, local copies, waits for them, and re-layouts: 30.3 us -> 5.84 us
    all_to_all x1 -> x2, blocking collectives: 108 us -> 86 us  [the longest x1 68.4 us: shards(): lax.all_to_all(main_out.reshape(experts, SLOTS, width), ('node', 'local')...]
    reduce_sum x3 -> x1, other arithmetic: 20.4 us -> 1.34 us  [shards(): jnp.sum((expert_ids == my_expert).astype(jnp.int32)) > SLOTS]
    all_gather x0 -> x2, waiting for transfers between devices: none -> 18.3 us  [the longest x1 17.1 us: shards(): lax.all_gather(spill_in.reshape(groups * SLOTS, width), 'local', tiled=True)]
  transfers between devices with their start and end apart: 1 -> 5, of which waited for: 1 -> 4; matrix products, arithmetic and copies ran while one was open for 0% -> 1% of each run, Pallas kernels for 0% -> 13%
where the time goes in v1:
time: 230 us; the launch traced here: 227 us
  blocking collectives  99.5 us (43%)
  waiting for transfers between devices  60.5 us (26%)
  Pallas kernels  33 us (14%)
  between operations  13.8 us (6%)
  starting transfers between devices  13.1 us (6%)
  local copies, waits for them, and re-layouts  5.84 us (3%)
    all_to_all x1, blocking collectives, shards(): lax.all_to_all(main_out.reshape(experts, SLOTS, width), ('node', 'local')...  68.4 us
    all_to_all x1, waiting for transfers between devices, shards(): lax.all_to_all(main.reshape(groups, per_group * SLOTS, width), 'node', sp...  32.9 us
    pallas_call x2, Pallas kernels, apply_expert(): pl.pallas_call(expert_kernel, grid=(count // block,), in_specs=[scalar(),...  22.2 us
    all_to_all x1, blocking collectives, shards(): lax.all_to_all(spill.reshape(groups, SLOTS, width), 'node', split_axis=0,...  17.5 us
    all_gather x1, waiting for transfers between devices, shards(): lax.all_gather(spill_in.reshape(groups * SLOTS, width), 'local', tiled=True)  17.1 us
    all_gather x1, blocking collectives, shards(): ids_all = lax.all_gather(id_rows, 'local', tiled=True)  13.5 us
    all_to_all x1, waiting for transfers between devices, shards(): lax.all_to_all(spill_back.reshape(groups, SLOTS, width), 'node', split_ax...  8.57 us
    all_to_all x1, starting transfers between devices, shards(): lax.all_to_all(main.reshape(groups, per_group * SLOTS, width), 'node', sp...  7.67 us
  transfers between devices with their start and end apart: 5, of which 4 were waited for; matrix products, arithmetic and copies ran while one was open for 1% of the time, Pallas kernels for 13%

profile of v1, /device:TPU:2, one launch (start us, length us, event | category | flops | bytes accessed | tf_op | source)
XLA Modules:
  0.0 227.0 jit_solution(9867845193441051414)
XLA Ops:
  6.5 0.7 all-gather.3.cloned.1.call-update
  7.3 0.0 all-gather.5.cloned.1.call-start
  7.3 1.0 copy-done.2
  8.3 0.7 copy-done.3
  9.0 0.6 spill_rows.1
  9.6 17.5 %all_to_all.20 = bf16[16,8,2048]{2,1,0:T(8,128)(2,1)} all-to-all(bf16[16,8,2048]{2,1,0:T(8,128)(2,1)S(1)} %bitcast.14), channel_id=1, replica_groups=mesh['node'=16,'local'=8] {'node'}, dimensions={0} | all-to-all | bytes 1048576 | tf_op jit(solution)/shard_map/all_to_all | solution.py:199
  27.1 0.0 all-gather.5.cloned.1.call-update
  27.2 1.3 convert_reduce_fusion
  29.1 13.5 %all_gather.9.ids_ref = s32[64,128]{1,0:T(8,128)S(1)} all-gather(s32[8,128]{1,0:T(8,128)} %bitcast.16), channel_id=1, replica_groups=mesh['node'=16,'local'=8] {'local'}, dimensions={0}, use_global_device_ids=true | all-gather | bytes 36864 | tf_op jit(solution)/shard_map/all_gather | solution.py:189
  42.6 1.1 all-gather.3.cloned.1.call-done.acts_ref
  43.7 7.0 %main_rows.1 = bf16[16,8,8,2048]{3,2,1,0:T(8,128)(2,1)S(1)} custom-call(s32[1]{0:T(128)} %bitcast.2.my_ref, s32[64,128]{1,0:T(8,128)S(1)} %all_gather.9.ids_ref, bf16[1024,2048]{1,0:T(8,128)(2,1)} %all-gather.3.cloned.1.call-done.acts_ref), custom_call_target="tpu_custom_call" | custom-call | tf_op jit(solution)/shard_map/main_rows/pallas_call | solution.py:214
  50.8 1.9 copy-done
  52.7 7.7 %all-to-all-start = ((bf16[16,64,2048]{2,1,0:T(8,128)(2,1)}), bf16[16,64,2048]{2,1,0:T(8,128)(2,1)}, u32[]{:S(2)}, u32[]{:S(2)}) async-start(bf16[16,64,2048]{2,1,0:T(8,128)(2,1)} %bitcast.12), calls=%async_computation | async-start | bytes 8388608 | tf_op jit(solution)/shard_map/all_to_all | solution.py:227
  60.4 0.0 reduce-scatter.2.cloned.1.call-start
  60.4 17.1 %all-gather.5.cloned.1.call-done.rows_ref = bf16[1024,2048]{1,0:T(8,128)(2,1)} async-done(((bf16[128,2048]{1,0:T(8,128)(2,1)}), bf16[1024,2048]{1,0:T(8,128)(2,1)}) %all-gather.5.cloned.1.call-update) | async-done | bytes 4194320 | tf_op jit(solution)/shard_map/all_gather | solution.py:200
  77.5 4.8 %expert.3 = bf16[1024,2048]{1,0:T(8,128)(2,1)} custom-call(s32[1]{0:T(128)} %bitcast.7.on_ref, bf16[1024,2048]{1,0:T(8,128)(2,1)} %all-gather.5.cloned.1.call-done.rows_ref, bf16[1,2048,768]{2,1,0:T(8,128)(2,1)S(1)} %copy-done.6, bf16[1,2048,768]{2,1,0:T(8,128)(2,1)} %up_hbm.3, bf16[1,768,2048]{2,1,0:T(8,128)(2,1)} %down_hbm.3), custom_call_target="tpu_custom_call" | custom-call | flops 9663676416 | bytes 17825792 | tf_op jit(solution)/shard_map/expert/pallas_call | solution.py:155
  82.4 32.9 %all-to-all-done = bf16[16,64,2048]{2,1,0:T(8,128)(2,1)} async-done(((bf16[16,64,2048]{2,1,0:T(8,128)(2,1)}), bf16[16,64,2048]{2,1,0:T(8,128)(2,1)}, u32[]{:S(2)}, u32[]{:S(2)}) %all-to-all-start) | async-done | bytes 4194336 | tf_op jit(solution)/shard_map/all_to_all | solution.py:227
  115.3 17.4 %expert.2 = bf16[1024,2048]{1,0:T(8,128)(2,1)} custom-call(s32[1]{0:T(128)} %constant.3.clone.1.on_ref, bf16[1024,2048]{1,0:T(8,128)(2,1)} %bitcast.4.rows_ref, bf16[1,2048,768]{2,1,0:T(8,128)(2,1)S(1)} %copy-done.6, bf16[1,2048,768]{2,1,0:T(8,128)(2,1)} %up_hbm.3, bf16[1,768,2048]{2,1,0:T(8,128)(2,1)} %down_hbm.3), custom_call_target="tpu_custom_call" | custom-call | flops 9663676416 | bytes 17825792 | tf_op jit(solution)/shard_map/expert/pallas_call | solution.py:155
  132.7 68.4 %all_to_all.21 = bf16[128,8,2048]{2,1,0:T(8,128)(2,1)} all-to-all(bf16[128,8,2048]{2,1,0:T(8,128)(2,1)} %bitcast.20), channel_id=1, replica_groups=mesh['node'=16,'local'=8] {'node','local'}, dimensions={0} | all-to-all | bytes 8388608 | tf_op jit(solution)/shard_map/all_to_all | solution.py:237
  201.1 5.3 %all-to-all-start.3 = ((bf16[16,8,2048]{2,1,0:T(8,128)(2,1)}), bf16[16,8,2048]{2,1,0:T(8,128)(2,1)S(1)}, u32[]{:S(2)}, u32[]{:S(2)}) async-start(bf16[16,8,2048]{2,1,0:T(8,128)(2,1)} %bitcast.22), calls=%async_computation.4 | async-start | bytes 1048576 | tf_op jit(solution)/shard_map/all_to_all | solution.py:240
  206.5 0.5 combine_weights.1
  207.0 8.6 %all-to-all-done.3 = bf16[16,8,2048]{2,1,0:T(8,128)(2,1)S(1)} async-done(((bf16[16,8,2048]{2,1,0:T(8,128)(2,1)}), bf16[16,8,2048]{2,1,0:T(8,128)(2,1)S(1)}, u32[]{:S(2)}, u32[]{:S(2)}) %all-to-all-start.3) | async-done | bytes 524320 | tf_op jit(solution)/shard_map/all_to_all | solution.py:240
  215.5 2.2 copy-done.1
  217.7 2.8 %combine.1 = bf16[128,2048]{1,0:T(8,128)(2,1)} custom-call(bf16[1024,128]{1,0:T(8,128)(2,1)S(1)} %get-tuple-element.7.main_w_ref, bf16[128,128]{1,0:T(8,128)(2,1)S(1)} %get-tuple-element.8.spill_w_ref, bf16[1024,2048]{1,0:T(8,128)(2,1)S(1)} %bitcast.13, bf16[128,2048]{1,0:T(8,128)(2,1)S(1)} %bitcast.15), custom_call_target="tpu_custom_call" | custom-call | tf_op jit(solution)/shard_map/combine/pallas_call | solution.py:245
  (13 shorter events, 0.0 us)
Async XLA Ops:
  6.5 37.2 %all-gather.3.cloned.1.call-start = ((), (), s32[]{:S(2)}) async-start(), calls=%async_computation.5 | async-start | bytes 4718592 | tf_op jit(solution)/shard_map/all_gather | solution.py:188
  7.3 70.3 %all-gather.5.cloned.1.call-start = ((), (), s32[]{:S(2)}) async-start(), calls=%async_computation.6 | async-start | bytes 4718592 | tf_op jit(solution)/shard_map/all_gather | solution.py:200
  7.3 1.0 copy-start.2
  8.3 0.7 copy-start.3
  50.8 1.9 copy-start
  52.7 24.8 %copy-start.6 = (bf16[1,2048,768]{2,1,0:T(8,128)(2,1)S(1)}, bf16[1,2048,768]{2,1,0:T(8,128)(2,1)}, u32[]{:S(2)}) copy-start(bf16[1,2048,768]{2,1,0:T(8,128)(2,1)} %gate_hbm.3) | copy-start | bytes 9437188
  52.7 62.5 %all-to-all-start = ((bf16[16,64,2048]{2,1,0:T(8,128)(2,1)}), bf16[16,64,2048]{2,1,0:T(8,128)(2,1)}, u32[]{:S(2)}, u32[]{:S(2)}) async-start(bf16[16,64,2048]{2,1,0:T(8,128)(2,1)} %bitcast.12), calls=%async_computation | async-start | bytes 8388608 | tf_op jit(solution)/shard_map/all_to_all | solution.py:227
  60.4 140.7 %reduce-scatter.2.cloned.1.call-start = ((), (), s32[]{:S(2)}) async-start(), calls=%async_computation.7 | async-start | bytes 4718592 | tf_op jit(solution)/shard_map/reduce_scatter | solution.py:233
  132.6 73.8 %copy-start.4 = (s32[128,8]{0,1:T(8,128)S(1)}, s32[128,8]{0,1:T(8,128)}, u32[]{:S(2)}) copy-start(s32[128,8]{0,1:T(8,128)} %param.7) | copy-start | bytes 12292
  132.7 73.8 %copy-start.5 = (bf16[128,8]{0,1:T(8,128)(2,1)S(1)}, bf16[128,8]{0,1:T(8,128)(2,1)}, u32[]{:S(2)}) copy-start(bf16[128,8]{0,1:T(8,128)(2,1)} %param.8) | copy-start | bytes 6148
  201.1 14.4 %all-to-all-start.3 = ((bf16[16,8,2048]{2,1,0:T(8,128)(2,1)}), bf16[16,8,2048]{2,1,0:T(8,128)(2,1)S(1)}, u32[]{:S(2)}, u32[]{:S(2)}) async-start(bf16[16,8,2048]{2,1,0:T(8,128)(2,1)} %bitcast.22), calls=%async_computation.4 | async-start | bytes 1048576 | tf_op jit(solution)/shard_map/all_to_all | solution.py:240
  215.5 2.2 copy-start.1
Sparse Core Ops, SparseCore 0:
  9.1 34.6 all-gather.2
  45.4 32.0 all-gather.4
  82.5 50.3 reduce-scatter.1

commit v2 on v1

v2 whole, which is shorter than its diff:
```python
import functools

import jax
import jax.numpy as jnp
from jax import lax
from jax.experimental import pallas as pl
from jax.experimental.pallas import tpu as pltpu
from jax.sharding import PartitionSpec as P

SLOTS = 8
SHIFT = 3
BF16 = jnp.bfloat16
F32 = jnp.float32


def iota(shape, dim):
    return lax.broadcasted_iota(jnp.int32, shape, dim)


def indicator(mask):
    return jnp.where(mask, 1.0, 0.0).astype(F32)


def dot(left, right):
    return jnp.dot(left, right, preferred_element_type=F32)


def ranks_of(named):
    tokens = named.shape[1]
    earlier = indicator(iota((tokens, tokens), 0) < iota((tokens, tokens), 1))
    return dot(named.astype(BF16), earlier.astype(BF16))


def spread(values, slots):
    labels = values.shape[0]
    picks = indicator((iota((labels * slots, labels), 0) >> SHIFT) == iota((labels * slots, labels), 1))
    return dot(picks.astype(BF16), values.astype(BF16))


def group_sums(values, groups):
    experts = values.shape[0]
    per_group = experts // groups
    shape = (groups * SLOTS, experts)
    same = indicator((iota(shape, 0) >> SHIFT) == (iota(shape, 1) // per_group))
    return dot(same.astype(BF16), values.astype(BF16))


def marks_of(ids_ref, labels):
    total = indicator(labels == ids_ref[0:1, :])
    for entry in range(1, ids_ref.shape[0]):
        total = total + indicator(labels == ids_ref[entry : entry + 1, :])
    return total


def spill_codes(named, ranks):
    return named * jnp.maximum(ranks - (SLOTS - 1), 0.0)


def pack_kernel(groups, experts, ids_ref, acts_ref, packed_ref, spill_ref):
    tokens, width = acts_ref.shape
    entries = ids_ref.shape[0]
    packed_ref[:, :width] = acts_ref[...]
    ids = ids_ref[...].astype(F32)
    filler = jnp.zeros((tokens - entries, tokens), F32)
    packed_ref[:, width:] = jnp.concatenate([ids, filler], axis=0).astype(BF16)
    named = marks_of(ids_ref, iota((experts, tokens), 0))
    codes = group_sums(spill_codes(named, ranks_of(named)), groups)
    slot = (iota(codes.shape, 0) & (SLOTS - 1)).astype(F32)
    spill_ref[...] = dot(indicator(codes == slot + 1.0).astype(BF16), acts_ref[...]).astype(BF16)


def weight_kernel(groups, experts, ids_ref, gates_ref, main_ref, spill_ref):
    tokens = ids_ref.shape[1]
    labels = iota((experts, tokens), 0)
    named = marks_of(ids_ref, labels)
    gates = jnp.zeros((experts, tokens), F32)
    for entry in range(ids_ref.shape[0]):
        value = gates_ref[entry : entry + 1, :].astype(F32)
        gates = gates + jnp.where(labels == ids_ref[entry : entry + 1, :], value, 0.0)
    ranks = ranks_of(named)
    rank_rows = spread(jnp.where(named > 0.0, ranks, 99.0), SLOTS)
    gate_rows = spread(gates, SLOTS)
    slot = (iota(rank_rows.shape, 0) & (SLOTS - 1)).astype(F32)
    main_ref[...] = jnp.where(rank_rows == slot, gate_rows, 0.0).astype(BF16)
    codes = spill_codes(named, ranks)
    code_rows = group_sums(codes, groups)
    spill_rows = group_sums(jnp.where(codes > 0.0, gates, 0.0), groups)
    spill_slot = (iota(code_rows.shape, 0) & (SLOTS - 1)).astype(F32)
    spill_ref[...] = jnp.where(code_rows == spill_slot + 1.0, spill_rows, 0.0).astype(BF16)


def gather_kernel(groups, per_group, parts, count, my_ref, *refs):
    out_ref = refs[-1]
    width = out_ref.shape[-1]
    mine = my_ref[0]
    core = my_ref[1]
    for place in range(count // parts):
        pieces = refs[place * parts : (place + 1) * parts]
        ids = pieces[0][0:16, width:].astype(F32)[0:8].astype(jnp.int32)
        tokens = ids.shape[1]
        labels = iota((groups, tokens), 0) * per_group + mine
        named = indicator(labels == ids[0:1, :])
        for entry in range(1, ids.shape[0]):
            named = named + indicator(labels == ids[entry : entry + 1, :])
        rank_rows = spread(jnp.where(named > 0.0, ranks_of(named), 99.0), SLOTS)
        slot = (iota(rank_rows.shape, 0) & (SLOTS - 1)).astype(F32)
        picks = indicator(rank_rows == slot).astype(BF16)
        step = tokens // parts
        rows = dot(picks[:, :step], pieces[0][:, :width])
        for part in range(1, parts):
            rows = rows + dot(picks[:, part * step : (part + 1) * step], pieces[part][:, :width])
        rows = rows.reshape(groups, 1, 1, SLOTS, width).astype(BF16)
        side = core if place % 2 == 0 else 1 - core
        out_ref[:, place // 2 : place // 2 + 1, pl.ds(side, 1)] = rows


def expert_rows(blocks, weights, arrive):
    gate_w, up_w, down_w = weights
    arrive(0)
    gates = [dot(rows(), gate_w[...]) for rows in blocks]
    arrive(1)
    ups = [dot(rows(), up_w[...]) for rows in blocks]
    hidden = [(g / (1.0 + jnp.exp(-g)) * u).astype(BF16) for g, u in zip(gates, ups)]
    arrive(2)
    return [dot(rows, down_w[...]).astype(BF16) for rows in hidden]


def weight_copies(sources, weights, sems):
    return [
        pltpu.make_async_copy(source.at[0], weight, sems.at[place])
        for place, (source, weight) in enumerate(zip(sources, weights))
    ]


def main_kernel(first, chips_ref, rows_hbm, gate_hbm, up_hbm, down_hbm, *refs):
    out_hbm, held, done, gate_w, up_w, down_w, row_sems, sems, out_sems = refs[-9:]
    chips, groups, slots, width = held.shape
    weights = (gate_w, up_w, down_w)
    loads = weight_copies((gate_hbm, up_hbm, down_hbm), weights, sems)
    rows = [
        pltpu.make_async_copy(rows_hbm.at[:, chip], held.at[chip], row_sems.at[chip]) for chip in range(chips)
    ]
    for copy in rows + loads:
        copy.start()
    for copy in rows:
        copy.wait()
    blocks = [lambda chip=chip: held[chip].reshape(groups * slots, width) for chip in range(chips)]
    results = expert_rows(blocks, weights, lambda place: loads[place].wait())
    stores = [
        pltpu.make_async_copy(done.at[chip], out_hbm.at[:, chips_ref[first + chip]], out_sems.at[chip])
        for chip in range(chips)
    ]
    for chip in range(chips):
        done[chip] = results[chip].reshape(groups, slots, width)
        stores[chip].start()
    for store in stores:
        store.wait()


def spill_kernel(on_ref, *refs):
    pieces = refs[:10]
    gate_hbm, up_hbm, down_hbm = refs[10:13]
    same_hbm, other_hbm, held, done, gate_w, up_w, down_w, row_sems, sems, out_sems = refs[-10:]
    chips, both, width = held.shape
    tokens = both // 2
    half = tokens // 2
    weights = (gate_w, up_w, down_w)
    places = [(chip, side * tokens, tokens) for chip in range(chips - 1) for side in range(2)]
    places += [(chips - 1, quarter * half, half) for quarter in range(4)]
    loads = weight_copies((gate_hbm, up_hbm, down_hbm), weights, sems)
    rows = [
        pltpu.make_async_copy(piece, held.at[chip, pl.ds(start, count)], row_sems.at[place])
        for place, (piece, (chip, start, count)) in enumerate(zip(pieces, places))
    ]
    stores = [
        pltpu.make_async_copy(done.at[chip, pl.ds(side * tokens, tokens)], out.at[chip], out_sems.at[chip, side])
        for chip in range(chips)
        for side, out in enumerate((same_hbm, other_hbm))
    ]

    @pl.when(on_ref[0] != 0)
    def _():
        for copy in rows + loads:
            copy.start()
        for copy in rows:
            copy.wait()
        for pair in range(chips // 2):
            blocks = [lambda chip=chip: held[chip] for chip in (2 * pair, 2 * pair + 1)]
            results = expert_rows(blocks, weights, lambda place: loads[place].wait() if pair == 0 else None)
            for chip, result in zip((2 * pair, 2 * pair + 1), results):
                done[chip] = result
                stores[2 * chip].start()
                stores[2 * chip + 1].start()

    @pl.when(on_ref[0] == 0)
    def _():
        done[...] = jnp.zeros(done.shape, BF16)
        for store in stores:
            store.start()

    for store in stores:
        store.wait()


def combine_kernel(main_w_ref, spill_w_ref, main_ref, spill_ref, out_ref):
    over_rows = (((0,), (0,)), ((), ()))
    total = lax.dot_general(main_w_ref[...], main_ref[...], over_rows, preferred_element_type=F32)
    total += lax.dot_general(spill_w_ref[...], spill_ref[...], over_rows, preferred_element_type=F32)
    out_ref[...] = total.astype(BF16)


def params(megabytes=48):
    return pltpu.CompilerParams(vmem_limit_bytes=megabytes * 1024 * 1024)


def whole():
    return pl.BlockSpec(memory_space=pltpu.VMEM)


def scalar():
    return pl.BlockSpec(memory_space=pltpu.SMEM)


def anywhere():
    return pl.BlockSpec(memory_space=pl.ANY)


def expert_cost(count, width, hidden):
    return pl.CostEstimate(
        flops=6 * count * width * hidden,
        bytes_accessed=4 * count * width + 6 * width * hidden,
        transcendentals=count * hidden,
    )


def swap_cores(value):
    size = lax.axis_size("local")
    return lax.ppermute(value, "local", [(i, i ^ 1) for i in range(size)])


def next_chip(value, hops):
    size = lax.axis_size("local")
    return lax.ppermute(value, "local", [(i, (i + 2 * hops) % size) for i in range(size)])


def around(value):
    half = value.shape[0] // 2
    before = next_chip(value, 1)
    after = next_chip(value, -1)
    beside = swap_cores(value)
    far_top = next_chip(before[:half], 1)
    far_low = next_chip(after[half:], -1)
    before_beside = swap_cores(before)
    after_beside = swap_cores(after)
    far = [far_top, far_low, swap_cores(far_top), swap_cores(far_low)]
    return [value, beside], [before, before_beside, after, after_beside], far


def order_kernel(value_ref, *refs):
    pass


def after(value, *earlier):
    return pl.pallas_call(
        order_kernel,
        in_specs=[anywhere()] * (1 + len(earlier)),
        out_specs=anywhere(),
        out_shape=jax.ShapeDtypeStruct(value.shape, value.dtype),
        input_output_aliases={0: 0},
        compiler_params=params(60),
        name="order",
    )(value, *earlier)


def back_home(same, other):
    half = same.shape[1] // 2
    total = same + swap_cores(other)
    far = total[3]
    from_before = next_chip(far[:half], 1)
    from_after = next_chip(far[half:], -1)
    to_after = jnp.concatenate([total[2][:half] + from_before, total[2][half:]], axis=0)
    to_before = jnp.concatenate([total[1][:half], total[1][half:] + from_after], axis=0)
    return total[0] + next_chip(to_after, 1) + next_chip(to_before, -1)


def shards(activations, expert_ids, route_gates, gate_proj, up_proj, down_proj):
    tokens, width = activations.shape
    hidden = gate_proj.shape[2]
    groups = lax.axis_size("node")
    per_group = lax.axis_size("local")
    experts = groups * per_group
    chips = per_group // 2
    my_local = lax.axis_index("local").astype(jnp.int32)
    my_expert = lax.axis_index("node").astype(jnp.int32) * per_group + my_local
    my_chip = my_local >> 1
    place = jnp.stack([my_local, my_local & 1])
    order = jnp.stack([my_chip, (my_chip + 3) % chips, (my_chip + 1) % chips, (my_chip + 2) % chips])
    id_rows = expert_ids.T
    gate_rows = route_gates.T

    packed, spill = pl.pallas_call(
        functools.partial(pack_kernel, groups, experts),
        in_specs=[whole(), whole()],
        out_specs=[whole(), whole()],
        out_shape=[
            jax.ShapeDtypeStruct((tokens, width + tokens), BF16),
            jax.ShapeDtypeStruct((groups * SLOTS, width), BF16),
        ],
        compiler_params=params(16),
        name="pack_rows",
    )(id_rows, activations)
    spill_in = lax.all_to_all(spill.reshape(groups, SLOTS, width), "node", split_axis=0, concat_axis=0, tiled=True)

    def pick(pieces, parts):
        return pl.pallas_call(
            functools.partial(gather_kernel, groups, per_group, parts, len(pieces)),
            in_specs=[scalar()] + [whole()] * len(pieces),
            out_specs=whole(),
            out_shape=jax.ShapeDtypeStruct((groups, len(pieces) // parts // 2, 2, SLOTS, width), BF16),
            compiler_params=params(24),
            name="main_rows",
        )(place, *pieces)

    def send(rows):
        count = rows.shape[1]
        sent = rows.reshape(groups, count * 2 * SLOTS, width)
        sent = lax.all_to_all(sent, "node", split_axis=0, concat_axis=0, tiled=True)
        return sent.reshape(groups, count, 2 * SLOTS, width)

    own, near, far = around(packed)
    spill_own, spill_near, spill_far = around(spill_in.reshape(groups * SLOTS, width))
    own_in = send(after(pick(own, 1), spill_in))
    near_rows = pick(near, 1)
    near_in = send(after(near_rows, own_in, spill_near[0], spill_near[2]))
    far_rows = pick(far, 2)

    busiest = (jnp.sum((expert_ids == my_expert).astype(jnp.int32)) > SLOTS).astype(jnp.int32).reshape(1)
    weight_space = [
        pltpu.VMEM((width, hidden), BF16),
        pltpu.VMEM((width, hidden), BF16),
        pltpu.VMEM((hidden, width), BF16),
    ]
    earlier = [own_in]
    spill_same, spill_other = pl.pallas_call(
        spill_kernel,
        in_specs=[scalar()] + [anywhere()] * (13 + len(earlier)),
        out_specs=[anywhere(), anywhere()],
        out_shape=[jax.ShapeDtypeStruct((chips, groups * SLOTS, width), BF16)] * 2,
        scratch_shapes=[pltpu.VMEM((chips, 2 * groups * SLOTS, width), BF16)] * 2
        + weight_space
        + [pltpu.SemaphoreType.DMA((10,)), pltpu.SemaphoreType.DMA((3,)), pltpu.SemaphoreType.DMA((chips, 2))],
        compiler_params=params(60),
        cost_estimate=expert_cost(per_group * groups * SLOTS, width, hidden),
        name="spill_expert",
    )(busiest, *spill_own, *spill_near, *spill_far, gate_proj, up_proj, down_proj, *earlier)
    far_in = send(after(far_rows, near_in, spill_same))
    spill_back = back_home(spill_same, after(spill_other, near_in))

    main_out = spill_same
    first = 0
    for arrival in (own_in, near_in, far_in):
        count = arrival.shape[1]
        main_out = pl.pallas_call(
            functools.partial(main_kernel, first),
            in_specs=[scalar()] + [anywhere()] * 5,
            out_specs=anywhere(),
            out_shape=jax.ShapeDtypeStruct((groups, chips, 2 * SLOTS, width), BF16),
            scratch_shapes=[pltpu.VMEM((count, groups, 2 * SLOTS, width), BF16)] * 2
            + weight_space
            + [pltpu.SemaphoreType.DMA((count,)), pltpu.SemaphoreType.DMA((3,)), pltpu.SemaphoreType.DMA((count,))],
            input_output_aliases={5: 0} if first else {},
            compiler_params=params(60),
            cost_estimate=expert_cost(count * 2 * groups * SLOTS, width, hidden),
            name="main_expert",
        )(order, arrival, gate_proj, up_proj, down_proj, main_out)
        first += count

    main_w, spill_w = pl.pallas_call(
        functools.partial(weight_kernel, groups, experts),
        in_specs=[whole(), whole()],
        out_specs=[whole(), whole()],
        out_shape=[
            jax.ShapeDtypeStruct((experts * SLOTS, tokens), BF16),
            jax.ShapeDtypeStruct((groups * SLOTS, tokens), BF16),
        ],
        compiler_params=params(16),
        name="combine_weights",
    )(id_rows, gate_rows)
    main_back = lax.all_to_all(
        main_out.reshape(experts, SLOTS, width), ("node", "local"), split_axis=0, concat_axis=0, tiled=True
    )
    spill_home = lax.all_to_all(
        after(spill_back, main_back).reshape(groups, SLOTS, width), "node", split_axis=0, concat_axis=0, tiled=True
    )

    columns = min(1024, width)
    return pl.pallas_call(
        combine_kernel,
        grid=(width // columns,),
        in_specs=[
            pl.BlockSpec((experts * SLOTS, tokens), lambda i: (0, 0)),
            pl.BlockSpec((groups * SLOTS, tokens), lambda i: (0, 0)),
            pl.BlockSpec((experts * SLOTS, columns), lambda i: (0, i)),
            pl.BlockSpec((groups * SLOTS, columns), lambda i: (0, i)),
        ],
        out_specs=pl.BlockSpec((tokens, columns), lambda i: (0, i)),
        out_shape=jax.ShapeDtypeStruct((tokens, width), BF16),
        compiler_params=params(60),
        name="combine",
    )(main_w, spill_w, main_back.reshape(experts * SLOTS, width), spill_home.reshape(groups * SLOTS, width))


def solution(mesh):
    rows = P(("node", "local"), None)
    stacks = P(("node", "local"), None, None)
    return jax.shard_map(
        shards, mesh=mesh, in_specs=(rows, rows, rows, stacks, stacks, stacks), out_specs=rows, check_vma=False
    )
```

time: 230 us -> 227 us (0.987)
  blocking collectives: 99.5 us -> 0 us
  starting transfers between devices: 13.1 us -> 69.6 us
  waiting for transfers between devices: 60.5 us -> 93.5 us
  between operations: 13.8 us -> 0.96 us
  local copies, waits for them, and re-layouts: 5.84 us -> 14.7 us
  Pallas kernels: 33 us -> 40.7 us
  other arithmetic: 1.34 us -> 4.76 us
    all_to_all x2 -> x0, blocking collectives: 86 us -> none  [the longest x1 68.4 us: shards(): lax.all_to_all(main_out.reshape(experts, SLOTS, width), ('node', 'local')...]
    ppermute x0 -> x23, waiting for transfers between devices: none -> 77.7 us  [the longest x12 77.7 us: next_chip(): lax.ppermute(value, 'local', [(i, (i + 2 * hops) % size) for i in range(s...]
    all_to_all x2 -> x6, starting transfers between devices: 13 us -> 44.1 us  [the longest x3 20.2 us: send(): sent = lax.all_to_all(sent, 'node', split_axis=0, concat_axis=0, tiled=True)]
    all_to_all x2 -> x6, waiting for transfers between devices: 41.5 us -> 15.8 us  [the longest x1 6.21 us: shards(): lax.all_to_all(after(spill_back, main_back).reshape(groups, SLOTS, width)...]
    ppermute x0 -> x23, starting transfers between devices: none -> 25.5 us  [the longest x12 15.8 us: next_chip(): lax.ppermute(value, 'local', [(i, (i + 2 * hops) % size) for i in range(s...]
    all_gather x2 -> x0, waiting for transfers between devices: 18.3 us -> none  [the longest x1 17.1 us: shards(): lax.all_gather(spill_in.reshape(groups * SLOTS, width), 'local', tiled=True)]
    all_gather x1 -> x0, blocking collectives: 13.5 us -> none  [shards(): ids_all = lax.all_gather(id_rows, 'local', tiled=True)]
    pallas_call x4 -> x13, Pallas kernels: 29.8 us -> 36.6 us  [the longest x3 27 us: shards(): pl.pallas_call(functools.partial(main_kernel, first), in_specs=[scalar()]...]
  transfers between devices with their start and end apart: 5 -> 29, of which waited for: 4 -> 11; matrix products, arithmetic and copies ran while one was open for 1% -> 3% of each run, Pallas kernels for 13% -> 16%
where the time goes in v2:
time: 227 us; the launch traced here: 224 us
  waiting for transfers between devices  93.5 us (41%)
  starting transfers between devices  69.6 us (31%)
  Pallas kernels  40.7 us (18%)
  local copies, waits for them, and re-layouts  14.7 us (6%)
  other arithmetic  4.76 us (2%)
    ppermute x12, waiting for transfers between devices, next_chip(): lax.ppermute(value, 'local', [(i, (i + 2 * hops) % size) for i in range(s...  77.7 us
    pallas_call x3, Pallas kernels, shards(): pl.pallas_call(functools.partial(main_kernel, first), in_specs=[scalar()]...  27 us
    all_to_all x3, starting transfers between devices, send(): sent = lax.all_to_all(sent, 'node', split_axis=0, concat_axis=0, tiled=True)  20.2 us
    ppermute x12, starting transfers between devices, next_chip(): lax.ppermute(value, 'local', [(i, (i + 2 * hops) % size) for i in range(s...  15.8 us
    unnamed x36, local copies, waits for them, and re-layouts  12 us
    ppermute x11, starting transfers between devices, swap_cores(): return lax.ppermute(value, 'local', [(i, i ^ 1) for i in range(size)])  9.67 us
    all_to_all x1, starting transfers between devices, shards(): lax.all_to_all(after(spill_back, main_back).reshape(groups, SLOTS, width)...  8.32 us
    all_to_all x1, starting transfers between devices, shards(): lax.all_to_all(spill.reshape(groups, SLOTS, width), 'node', split_axis=0,...  8.31 us
  transfers between devices with their start and end apart: 29, of which 11 were waited for; matrix products, arithmetic and copies ran while one was open for 3% of the time, Pallas kernels for 16%

profile of v2, /device:TPU:2, one launch (start us, length us, event | category | flops | bytes accessed | tf_op | source)
XLA Modules:
  0.0 224.3 jit_solution(4527710922682198109)
XLA Ops:
  3.1 8.3 %all-to-all-start = ((bf16[16,8,2048]{2,1,0:T(8,128)(2,1)}), bf16[16,8,2048]{2,1,0:T(8,128)(2,1)S(1)}, u32[]{:S(2)}, u32[]{:S(2)}) async-start(bf16[16,8,2048]{2,1,0:T(8,128)(2,1)} %bitcast.8), calls=%async_computation | async-start | bytes 1048576 | tf_op jit(solution)/shard_map/all_to_all | solution.py:312
  11.4 3.0 %collective-permute-start.2 = (bf16[128,2176]{1,0:T(8,128)(2,1)S(1)}, bf16[128,2176]{1,0:T(8,128)(2,1)S(1)}, u32[]{:S(2)}, u32[]{:S(2)}) collective-permute-start(bf16[128,2176]{1,0:T(8,128)(2,1)S(1)} %get-tuple-element.13.refs_0_), channel_id=1, source_target_pairs={{0,6},{1,7},{2,0},{3,1},{4,2},{5,3},{6,4},{7,5},{8,14},{9,15},{10,... | collective-permute-start | bytes 1671176 | tf_op jit(solution)/shard_map/ppermute | solution.py:243
  17.0 4.4 %all-to-all-done.refs_0_ = bf16[16,8,2048]{2,1,0:T(8,128)(2,1)S(1)} async-done(((bf16[16,8,2048]{2,1,0:T(8,128)(2,1)}), bf16[16,8,2048]{2,1,0:T(8,128)(2,1)S(1)}, u32[]{:S(2)}, u32[]{:S(2)}) %all-to-all-start) | async-done | bytes 524320 | tf_op jit(solution)/shard_map/all_to_all | solution.py:312
  22.1 6.0 %all-to-all-start.1 = ((bf16[16,16,2048]{2,1,0:T(8,128)(2,1)}), bf16[16,16,2048]{2,1,0:T(8,128)(2,1)S(1)}, u32[]{:S(2)}, u32[]{:S(2)}) async-start(bf16[16,16,2048]{2,1,0:T(8,128)(2,1)} %bitcast.44), calls=%async_computation.1 | async-start | bytes 2097152 | tf_op jit(solution)/shard_map/all_to_all | solution.py:327
  32.6 3.0 %collective-permute-start.3 = (bf16[64,2176]{1,0:T(8,128)(2,1)}, bf16[64,2176]{1,0:T(8,128)(2,1)S(1)}, u32[]{:S(2)}, u32[]{:S(2)}) collective-permute-start(bf16[64,2176]{1,0:T(8,128)(2,1)} %slice.80), channel_id=1, source_target_pairs={{0,6},{1,7},{2,0},{3,1},{4,2},{5,3},{6,4},{7,5},{8,14},{9,15},{10,... | collective-permute-start | bytes 835592 | tf_op jit(solution)/shard_map/ppermute | solution.py:243
  39.4 5.2 %collective-permute-done.10.refs_2_.refs_4_ = bf16[128,2048]{1,0:T(8,128)(2,1)S(1)} collective-permute-done((bf16[128,2048]{1,0:T(8,128)(2,1)S(1)}, bf16[128,2048]{1,0:T(8,128)(2,1)S(1)}, u32[]{:S(2)}, u32[]{:S(2)}) %collective-permute-start.10) | collective-permute-done | bytes 524320 | tf_op jit(solution)/shard_map/ppermute | solution.py:243
  45.4 2.4 %collective-permute-done.9.refs_1_.refs_2_ = bf16[128,2048]{1,0:T(8,128)(2,1)} collective-permute-done((bf16[128,2048]{1,0:T(8,128)(2,1)S(1)}, bf16[128,2048]{1,0:T(8,128)(2,1)}, u32[]{:S(2)}, u32[]{:S(2)}) %collective-permute-start.9) | collective-permute-done | bytes 524320 | tf_op jit(solution)/shard_map/ppermute | solution.py:243
  48.8 7.4 %all-to-all-start.2 = ((bf16[16,32,2048]{2,1,0:T(8,128)(2,1)}), bf16[16,32,2048]{2,1,0:T(8,128)(2,1)S(1)}, u32[]{:S(2)}, u32[]{:S(2)}) async-start(bf16[16,32,2048]{2,1,0:T(8,128)(2,1)} %bitcast.43), calls=%async_computation.2 | async-start | bytes 4194304 | tf_op jit(solution)/shard_map/all_to_all | solution.py:327
  61.5 5.1 %collective-permute-done.15.refs_7_ = bf16[64,2048]{1,0:T(8,128)(2,1)S(1)} collective-permute-done((bf16[64,2048]{1,0:T(8,128)(2,1)S(1)}, bf16[64,2048]{1,0:T(8,128)(2,1)S(1)}, u32[]{:S(2)}, u32[]{:S(2)}) %collective-permute-start.15) | collective-permute-done | bytes 262176 | tf_op jit(solution)/shard_map/ppermute | solution.py:243
  66.6 2.7 %collective-permute-done.14.refs_6_ = bf16[64,2048]{1,0:T(8,128)(2,1)} collective-permute-done((bf16[64,2048]{1,0:T(8,128)(2,1)S(1)}, bf16[64,2048]{1,0:T(8,128)(2,1)}, u32[]{:S(2)}, u32[]{:S(2)}) %collective-permute-start.14) | collective-permute-done | bytes 262176 | tf_op jit(solution)/shard_map/ppermute | solution.py:243
  73.6 2.7 %spill_expert.1 = (bf16[4,128,2048]{2,1,0:T(8,128)(2,1)}, bf16[4,128,2048]{2,1,0:T(8,128)(2,1)}) custom-call(s32[1]{0:T(128)} %bitcast.14.on_ref, bf16[128,2048]{1,0:T(8,128)(2,1)} %bitcast.59, bf16[128,2048]{1,0:T(8,128)(2,1)} %collective-permute-done.11.refs_1_, bf16[128,2048]{1,0:T(8,128)(2,1)} %collective-permute-done.9.refs_1_.refs_2_, ...), custom_call_target="tpu_custom_call" | custom-call | flops 9663676416 | bytes 17825792 | tf_op jit(solution)/shard_map/spill_expert/pallas_call | solution.py:344
  76.3 5.2 %all-to-all-done.2 = bf16[16,32,2048]{2,1,0:T(8,128)(2,1)S(1)} async-done(((bf16[16,32,2048]{2,1,0:T(8,128)(2,1)}), bf16[16,32,2048]{2,1,0:T(8,128)(2,1)S(1)}, u32[]{:S(2)}, u32[]{:S(2)}) %all-to-all-start.2) | async-done | bytes 2097184 | tf_op jit(solution)/shard_map/all_to_all | solution.py:327
  82.8 6.8 %all-to-all-start.3 = ((bf16[16,16,2048]{2,1,0:T(8,128)(2,1)}), bf16[16,16,2048]{2,1,0:T(8,128)(2,1)S(1)}, u32[]{:S(2)}, u32[]{:S(2)}) async-start(bf16[16,16,2048]{2,1,0:T(8,128)(2,1)} %bitcast.45), calls=%async_computation.3 | async-start | bytes 2097152 | tf_op jit(solution)/shard_map/all_to_all | solution.py:327
  90.2 8.2 %main_expert.3.refs_0_ = bf16[16,4,16,2048]{3,2,1,0:T(8,128)(2,1)} custom-call(s32[4]{0:T(128)} %pad_add_fusion.chips_ref, bf16[16,1,16,2048]{3,2,1,0:T(8,128)(2,1)} %bitcast.55, bf16[1,2048,768]{2,1,0:T(8,128)(2,1)} %gate_hbm.5, bf16[1,2048,768]{2,1,0:T(8,128)(2,1)} %up_hbm.5, bf16[1,768,2048]{2,1,0:T(8,128)(2,1)} %down_hbm.5, ...), custom_call_target="tpu_custom_call" | custom-call | flops 2415919104 | bytes 11534336 | tf_op jit(solution)/shard_map/main_expert/pallas_call | solution.py:363
  98.5 8.4 %collective-permute-start.18 = (bf16[4,128,2048]{2,1,0:T(8,128)(2,1)}, bf16[4,128,2048]{2,1,0:T(8,128)(2,1)}, u32[]{:S(2)}, u32[]{:S(2)}) collective-permute-start(bf16[4,128,2048]{2,1,0:T(8,128)(2,1)} %order.8), channel_id=1, source_target_pairs={{0,1},{1,0},{2,3},{3,2},{4,5},{5,4},{6,7},{7,6},{8,9},{9,8},{10,11... | collective-permute-start | bytes 6291464 | tf_op jit(solution)/shard_map/ppermute | solution.py:238
  106.9 10.5 %main_expert.4.refs_0_ = bf16[16,4,16,2048]{3,2,1,0:T(8,128)(2,1)} custom-call(s32[4]{0:T(128)} %pad_add_fusion.chips_ref, bf16[16,2,16,2048]{3,2,1,0:T(8,128)(2,1)} %bitcast.52, bf16[1,2048,768]{2,1,0:T(8,128)(2,1)} %gate_hbm.5, bf16[1,2048,768]{2,1,0:T(8,128)(2,1)} %up_hbm.5, bf16[1,768,2048]{2,1,0:T(8,128)(2,1)} %down_hbm.5, ...), custom_call_target="tpu_custom_call", output_to_operand_aliasing={{}: (5, {})} | custom-call | flops 4831838208 | bytes 13631488 | tf_op jit(solution)/shard_map/main_expert/pallas_call | solution.py:363
  118.4 8.2 %main_expert.5 = bf16[16,4,16,2048]{3,2,1,0:T(8,128)(2,1)} custom-call(s32[4]{0:T(128)} %pad_add_fusion.chips_ref, bf16[16,1,16,2048]{3,2,1,0:T(8,128)(2,1)} %bitcast.57, bf16[1,2048,768]{2,1,0:T(8,128)(2,1)} %gate_hbm.5, bf16[1,2048,768]{2,1,0:T(8,128)(2,1)} %up_hbm.5, bf16[1,768,2048]{2,1,0:T(8,128)(2,1)} %down_hbm.5, ...), custom_call_target="tpu_custom_call", output_to_operand_aliasing={{}: (5, {})} | custom-call | flops 2415919104 | bytes 11534336 | tf_op jit(solution)/shard_map/main_expert/pallas_call | solution.py:363
  126.7 7.3 %all-to-all-start.4 = ((bf16[128,8,2048]{2,1,0:T(8,128)(2,1)}), bf16[128,8,2048]{2,1,0:T(8,128)(2,1)}, u32[]{:S(2)}, u32[]{:S(2)}) async-start(bf16[128,8,2048]{2,1,0:T(8,128)(2,1)} %bitcast.49), calls=%async_computation.4 | async-start | bytes 8388608 | tf_op jit(solution)/shard_map/all_to_all | solution.py:389
  134.0 2.4 %add.44 = bf16[4,128,2048]{2,1,0:T(8,128)(2,1)S(1)} add(bf16[4,128,2048]{2,1,0:T(8,128)(2,1)S(1)} %copy-done.10, bf16[4,128,2048]{2,1,0:T(8,128)(2,1)} %collective-permute-done.18) | non-fusion elementwise | flops 1048576 | bytes 6291456 | tf_op jit(solution)/shard_map/add | solution.py:277
  139.8 47.9 %collective-permute-done.19 = bf16[64,2048]{1,0:T(8,128)(2,1)S(1)} collective-permute-done((bf16[64,2048]{1,0:T(8,128)(2,1)S(1)}, bf16[64,2048]{1,0:T(8,128)(2,1)S(1)}, u32[]{:S(2)}, u32[]{:S(2)}) %collective-permute-start.19) | collective-permute-done | bytes 262176 | tf_op jit(solution)/shard_map/ppermute | solution.py:243
  190.0 11.3 %collective-permute-done.22 = bf16[128,2048]{1,0:T(8,128)(2,1)S(1)} collective-permute-done((bf16[128,2048]{1,0:T(8,128)(2,1)S(1)}, bf16[128,2048]{1,0:T(8,128)(2,1)S(1)}, u32[]{:S(2)}, u32[]{:S(2)}) %collective-permute-start.22) | collective-permute-done | bytes 524320 | tf_op jit(solution)/shard_map/ppermute | solution.py:243
  203.5 8.3 %all-to-all-start.5 = ((bf16[16,8,2048]{2,1,0:T(8,128)(2,1)}), bf16[16,8,2048]{2,1,0:T(8,128)(2,1)S(1)}, u32[]{:S(2)}, u32[]{:S(2)}) async-start(bf16[16,8,2048]{2,1,0:T(8,128)(2,1)} %bitcast.56), calls=%async_computation.5 | async-start | bytes 1048576 | tf_op jit(solution)/shard_map/all_to_all | solution.py:392
  213.6 6.2 %all-to-all-done.5 = bf16[16,8,2048]{2,1,0:T(8,128)(2,1)S(1)} async-done(((bf16[16,8,2048]{2,1,0:T(8,128)(2,1)}), bf16[16,8,2048]{2,1,0:T(8,128)(2,1)S(1)}, u32[]{:S(2)}, u32[]{:S(2)}) %all-to-all-start.5) | async-done | bytes 524320 | tf_op jit(solution)/shard_map/all_to_all | solution.py:392
  220.6 3.6 %combine.1 = bf16[128,2048]{1,0:T(8,128)(2,1)} custom-call(bf16[1024,128]{1,0:T(8,128)(2,1)} %copy-done.4, bf16[128,128]{1,0:T(8,128)(2,1)} %copy-done.7, bf16[1024,2048]{1,0:T(8,128)(2,1)} %bitcast.18.main_ref, bf16[128,2048]{1,0:T(8,128)(2,1)} %bitcast.62), custom_call_target="tpu_custom_call" | custom-call | tf_op jit(solution)/shard_map/combine/pallas_call | solution.py:397
  (98 shorter events, 38.6 us)
Async XLA Ops:
  3.1 11.4 %collective-permute-start.8 = (bf16[128,2176]{1,0:T(8,128)(2,1)S(1)}, bf16[128,2176]{1,0:T(8,128)(2,1)S(1)}, u32[]{:S(2)}, u32[]{:S(2)}) collective-permute-start(bf16[128,2176]{1,0:T(8,128)(2,1)S(1)} %get-tuple-element.13.refs_0_), channel_id=1, source_target_pairs={{0,1},{1,0},{2,3},{3,2},{4,5},{5,4},{6,7},{7,6},{8,9},{9,8},{10,11... | collective-permute-start | bytes 1671176 | tf_op jit(solution)/shard_map/ppermute | solution.py:238
  3.1 18.2 %all-to-all-start = ((bf16[16,8,2048]{2,1,0:T(8,128)(2,1)}), bf16[16,8,2048]{2,1,0:T(8,128)(2,1)S(1)}, u32[]{:S(2)}, u32[]{:S(2)}) async-start(bf16[16,8,2048]{2,1,0:T(8,128)(2,1)} %bitcast.8), calls=%async_computation | async-start | bytes 1048576 | tf_op jit(solution)/shard_map/all_to_all | solution.py:312
  11.4 16.7 %collective-permute-start.2 = (bf16[128,2176]{1,0:T(8,128)(2,1)S(1)}, bf16[128,2176]{1,0:T(8,128)(2,1)S(1)}, u32[]{:S(2)}, u32[]{:S(2)}) collective-permute-start(bf16[128,2176]{1,0:T(8,128)(2,1)S(1)} %get-tuple-element.13.refs_0_), channel_id=1, source_target_pairs={{0,6},{1,7},{2,0},{3,1},{4,2},{5,3},{6,4},{7,5},{8,14},{9,15},{10,... | collective-permute-start | bytes 1671176 | tf_op jit(solution)/shard_map/ppermute | solution.py:243
  14.5 15.4 %collective-permute-start = (bf16[128,2176]{1,0:T(8,128)(2,1)S(1)}, bf16[128,2176]{1,0:T(8,128)(2,1)S(1)}, u32[]{:S(2)}, u32[]{:S(2)}) collective-permute-start(bf16[128,2176]{1,0:T(8,128)(2,1)S(1)} %get-tuple-element.13.refs_0_), channel_id=1, source_target_pairs={{0,2},{1,3},{2,4},{3,5},{4,6},{5,7},{6,0},{7,1},{8,10},{9,11},{10,... | collective-permute-start | bytes 1671176 | tf_op jit(solution)/shard_map/ppermute | solution.py:243
  22.1 25.7 %all-to-all-start.1 = ((bf16[16,16,2048]{2,1,0:T(8,128)(2,1)}), bf16[16,16,2048]{2,1,0:T(8,128)(2,1)S(1)}, u32[]{:S(2)}, u32[]{:S(2)}) async-start(bf16[16,16,2048]{2,1,0:T(8,128)(2,1)} %bitcast.44), calls=%async_computation.1 | async-start | bytes 2097152 | tf_op jit(solution)/shard_map/all_to_all | solution.py:327
  28.1 7.6 %collective-permute-start.7 = (bf16[128,2176]{1,0:T(8,128)(2,1)S(1)}, bf16[128,2176]{1,0:T(8,128)(2,1)S(1)}, u32[]{:S(2)}, u32[]{:S(2)}) collective-permute-start(bf16[128,2176]{1,0:T(8,128)(2,1)S(1)} %collective-permute-done.2.refs_2_), channel_id=1, source_target_pairs={{0,1},{1,0},{2,3},{3,2},{4,5},{5,4},{6,7},{7,6},{8,9},{9,8},{10,11... | collective-permute-start | bytes 1671176 | tf_op jit(solution)/shard_map/ppermute | solution.py:238
  29.9 14.7 %collective-permute-start.10 = (bf16[128,2048]{1,0:T(8,128)(2,1)S(1)}, bf16[128,2048]{1,0:T(8,128)(2,1)S(1)}, u32[]{:S(2)}, u32[]{:S(2)}) collective-permute-start(bf16[128,2048]{1,0:T(8,128)(2,1)S(1)} %bitcast.60), channel_id=1, source_target_pairs={{0,6},{1,7},{2,0},{3,1},{4,2},{5,3},{6,4},{7,5},{8,14},{9,15},{10,... | collective-permute-start | bytes 1572872 | tf_op jit(solution)/shard_map/ppermute | solution.py:243
  31.7 16.1 %collective-permute-start.9 = (bf16[128,2048]{1,0:T(8,128)(2,1)S(1)}, bf16[128,2048]{1,0:T(8,128)(2,1)}, u32[]{:S(2)}, u32[]{:S(2)}) collective-permute-start(bf16[128,2048]{1,0:T(8,128)(2,1)S(1)} %bitcast.61), channel_id=1, source_target_pairs={{0,2},{1,3},{2,4},{3,5},{4,6},{5,7},{6,0},{7,1},{8,10},{9,11},{10,... | collective-permute-start | bytes 1572872 | tf_op jit(solution)/shard_map/ppermute | solution.py:243
  32.6 23.6 %collective-permute-start.3 = (bf16[64,2176]{1,0:T(8,128)(2,1)}, bf16[64,2176]{1,0:T(8,128)(2,1)S(1)}, u32[]{:S(2)}, u32[]{:S(2)}) collective-permute-start(bf16[64,2176]{1,0:T(8,128)(2,1)} %slice.80), channel_id=1, source_target_pairs={{0,6},{1,7},{2,0},{3,1},{4,2},{5,3},{6,4},{7,5},{8,14},{9,15},{10,... | collective-permute-start | bytes 835592 | tf_op jit(solution)/shard_map/ppermute | solution.py:243
  35.7 20.6 %collective-permute-start.1 = (bf16[64,2176]{1,0:T(8,128)(2,1)S(1)}, bf16[64,2176]{1,0:T(8,128)(2,1)S(1)}, u32[]{:S(2)}, u32[]{:S(2)}) collective-permute-start(bf16[64,2176]{1,0:T(8,128)(2,1)S(1)} %slice.79), channel_id=1, source_target_pairs={{0,2},{1,3},{2,4},{3,5},{4,6},{5,7},{6,0},{7,1},{8,10},{9,11},{10,... | collective-permute-start | bytes 835592 | tf_op jit(solution)/shard_map/ppermute | solution.py:243
  48.8 32.6 %all-to-all-start.2 = ((bf16[16,32,2048]{2,1,0:T(8,128)(2,1)}), bf16[16,32,2048]{2,1,0:T(8,128)(2,1)S(1)}, u32[]{:S(2)}, u32[]{:S(2)}) async-start(bf16[16,32,2048]{2,1,0:T(8,128)(2,1)} %bitcast.43), calls=%async_computation.2 | async-start | bytes 4194304 | tf_op jit(solution)/shard_map/all_to_all | solution.py:327
  56.8 16.7 %collective-permute-start.11 = (bf16[128,2048]{1,0:T(8,128)(2,1)}, bf16[128,2048]{1,0:T(8,128)(2,1)}, u32[]{:S(2)}, u32[]{:S(2)}) collective-permute-start(bf16[128,2048]{1,0:T(8,128)(2,1)} %bitcast.58), channel_id=1, source_target_pairs={{0,1},{1,0},{2,3},{3,2},{4,5},{5,4},{6,7},{7,6},{8,9},{9,8},{10,11... | collective-permute-start | bytes 1572872 | tf_op jit(solution)/shard_map/ppermute | solution.py:238
  57.9 8.7 %collective-permute-start.15 = (bf16[64,2048]{1,0:T(8,128)(2,1)S(1)}, bf16[64,2048]{1,0:T(8,128)(2,1)S(1)}, u32[]{:S(2)}, u32[]{:S(2)}) collective-permute-start(bf16[64,2048]{1,0:T(8,128)(2,1)S(1)} %slice.82), channel_id=1, source_target_pairs={{0,6},{1,7},{2,0},{3,1},{4,2},{5,3},{6,4},{7,5},{8,14},{9,15},{10,... | collective-permute-start | bytes 786440 | tf_op jit(solution)/shard_map/ppermute | solution.py:243
  59.6 9.7 %collective-permute-start.14 = (bf16[64,2048]{1,0:T(8,128)(2,1)S(1)}, bf16[64,2048]{1,0:T(8,128)(2,1)}, u32[]{:S(2)}, u32[]{:S(2)}) collective-permute-start(bf16[64,2048]{1,0:T(8,128)(2,1)S(1)} %slice.81), channel_id=1, source_target_pairs={{0,2},{1,3},{2,4},{3,5},{4,6},{5,7},{6,0},{7,1},{8,10},{9,11},{10,... | collective-permute-start | bytes 786440 | tf_op jit(solution)/shard_map/ppermute | solution.py:243
  61.0 12.5 %collective-permute-start.13 = (bf16[128,2048]{1,0:T(8,128)(2,1)}, bf16[128,2048]{1,0:T(8,128)(2,1)}, u32[]{:S(2)}, u32[]{:S(2)}) collective-permute-start(bf16[128,2048]{1,0:T(8,128)(2,1)} %copy-done.16), channel_id=1, source_target_pairs={{0,1},{1,0},{2,3},{3,2},{4,5},{5,4},{6,7},{7,6},{8,9},{9,8},{10,11... | collective-permute-start | bytes 1572872 | tf_op jit(solution)/shard_map/ppermute | solution.py:238
  61.0 12.5 %collective-permute-start.12 = (bf16[128,2048]{1,0:T(8,128)(2,1)}, bf16[128,2048]{1,0:T(8,128)(2,1)}, u32[]{:S(2)}, u32[]{:S(2)}) collective-permute-start(bf16[128,2048]{1,0:T(8,128)(2,1)} %collective-permute-done.9.refs_1_.refs_2_), channel_id=1, source_target_pairs={{0,1},{1,0},{2,3},{3,2},{4,5},{5,4},{6,7},{7,6},{8,9},{9,8},{10,11... | collective-permute-start | bytes 1572872 | tf_op jit(solution)/shard_map/ppermute | solution.py:238
  82.8 34.6 %all-to-all-start.3 = ((bf16[16,16,2048]{2,1,0:T(8,128)(2,1)}), bf16[16,16,2048]{2,1,0:T(8,128)(2,1)S(1)}, u32[]{:S(2)}, u32[]{:S(2)}) async-start(bf16[16,16,2048]{2,1,0:T(8,128)(2,1)} %bitcast.45), calls=%async_computation.3 | async-start | bytes 2097152 | tf_op jit(solution)/shard_map/all_to_all | solution.py:327
  98.5 35.5 %collective-permute-start.18 = (bf16[4,128,2048]{2,1,0:T(8,128)(2,1)}, bf16[4,128,2048]{2,1,0:T(8,128)(2,1)}, u32[]{:S(2)}, u32[]{:S(2)}) collective-permute-start(bf16[4,128,2048]{2,1,0:T(8,128)(2,1)} %order.8), channel_id=1, source_target_pairs={{0,1},{1,0},{2,3},{3,2},{4,5},{5,4},{6,7},{7,6},{8,9},{9,8},{10,11... | collective-permute-start | bytes 6291464 | tf_op jit(solution)/shard_map/ppermute | solution.py:238
  126.7 76.8 %all-to-all-start.4 = ((bf16[128,8,2048]{2,1,0:T(8,128)(2,1)}), bf16[128,8,2048]{2,1,0:T(8,128)(2,1)}, u32[]{:S(2)}, u32[]{:S(2)}) async-start(bf16[128,8,2048]{2,1,0:T(8,128)(2,1)} %bitcast.49), calls=%async_computation.4 | async-start | bytes 8388608 | tf_op jit(solution)/shard_map/all_to_all | solution.py:389
  136.5 51.2 %collective-permute-start.19 = (bf16[64,2048]{1,0:T(8,128)(2,1)S(1)}, bf16[64,2048]{1,0:T(8,128)(2,1)S(1)}, u32[]{:S(2)}, u32[]{:S(2)}) collective-permute-start(bf16[64,2048]{1,0:T(8,128)(2,1)S(1)} %get-tuple-element.19), channel_id=1, source_target_pairs={{0,2},{1,3},{2,4},{3,5},{4,6},{5,7},{6,0},{7,1},{8,10},{9,11},{10,... | collective-permute-start | bytes 786440 | tf_op jit(solution)/shard_map/ppermute | solution.py:243
  138.0 49.7 %collective-permute-start.21 = (bf16[64,2048]{1,0:T(8,128)(2,1)S(1)}, bf16[64,2048]{1,0:T(8,128)(2,1)S(1)}, u32[]{:S(2)}, u32[]{:S(2)}) collective-permute-start(bf16[64,2048]{1,0:T(8,128)(2,1)S(1)} %get-tuple-element.20), channel_id=1, source_target_pairs={{0,6},{1,7},{2,0},{3,1},{4,2},{5,3},{6,4},{7,5},{8,14},{9,15},{10,... | collective-permute-start | bytes 786440 | tf_op jit(solution)/shard_map/ppermute | solution.py:243
  187.8 13.5 %collective-permute-start.22 = (bf16[128,2048]{1,0:T(8,128)(2,1)S(1)}, bf16[128,2048]{1,0:T(8,128)(2,1)S(1)}, u32[]{:S(2)}, u32[]{:S(2)}) collective-permute-start(bf16[128,2048]{1,0:T(8,128)(2,1)S(1)} %pad_maximum_fusion.1), channel_id=1, source_target_pairs={{0,6},{1,7},{2,0},{3,1},{4,2},{5,3},{6,4},{7,5},{8,14},{9,15},{10,... | collective-permute-start | bytes 1572872 | tf_op jit(solution)/shard_map/ppermute | solution.py:243
  188.2 14.5 %collective-permute-start.20 = (bf16[128,2048]{1,0:T(8,128)(2,1)S(1)}, bf16[128,2048]{1,0:T(8,128)(2,1)S(1)}, u32[]{:S(2)}, u32[]{:S(2)}) collective-permute-start(bf16[128,2048]{1,0:T(8,128)(2,1)S(1)} %pad_maximum_fusion), channel_id=1, source_target_pairs={{0,2},{1,3},{2,4},{3,5},{4,6},{5,7},{6,0},{7,1},{8,10},{9,11},{10,... | collective-permute-start | bytes 1572872 | tf_op jit(solution)/shard_map/ppermute | solution.py:243
  203.5 16.3 %all-to-all-start.5 = ((bf16[16,8,2048]{2,1,0:T(8,128)(2,1)}), bf16[16,8,2048]{2,1,0:T(8,128)(2,1)S(1)}, u32[]{:S(2)}, u32[]{:S(2)}) async-start(bf16[16,8,2048]{2,1,0:T(8,128)(2,1)} %bitcast.56), calls=%async_computation.5 | async-start | bytes 1048576 | tf_op jit(solution)/shard_map/all_to_all | solution.py:392
  (23 other events, 89.4 us)

commit v3 on v2

--- a/solution.py
+++ b/solution.py
@@ -56,17 +56,13 @@
     return named * jnp.maximum(ranks - (SLOTS - 1), 0.0)
 
 
-def pack_kernel(groups, experts, ids_ref, acts_ref, packed_ref, spill_ref):
+def pack_kernel(ids_ref, acts_ref, packed_ref):
     tokens, width = acts_ref.shape
     entries = ids_ref.shape[0]
     packed_ref[:, :width] = acts_ref[...]
     ids = ids_ref[...].astype(F32)
     filler = jnp.zeros((tokens - entries, tokens), F32)
     packed_ref[:, width:] = jnp.concatenate([ids, filler], axis=0).astype(BF16)
-    named = marks_of(ids_ref, iota((experts, tokens), 0))
-    codes = group_sums(spill_codes(named, ranks_of(named)), groups)
-    slot = (iota(codes.shape, 0) & (SLOTS - 1)).astype(F32)
-    spill_ref[...] = dot(indicator(codes == slot + 1.0).astype(BF16), acts_ref[...]).astype(BF16)
 
 
 def weight_kernel(groups, experts, ids_ref, gates_ref, main_ref, spill_ref):
@@ -89,63 +85,100 @@
     spill_ref[...] = jnp.where(code_rows == spill_slot + 1.0, spill_rows, 0.0).astype(BF16)
 
 
-def gather_kernel(groups, per_group, parts, count, my_ref, *refs):
-    out_ref = refs[-1]
-    width = out_ref.shape[-1]
-    mine = my_ref[0]
+def ids_of(packed_ref, width):
+    return packed_ref[0:16, width:].astype(F32)[0:8].astype(jnp.int32)
+
+
+def picks_for(ids, groups, per_group, mine):
+    named = marks_of(ids, iota((groups, ids.shape[1]), 0) * per_group + mine)
+    rank_rows = spread(jnp.where(named > 0.0, ranks_of(named), 99.0), SLOTS)
+    slot = (iota(rank_rows.shape, 0) & (SLOTS - 1)).astype(F32)
+    return indicator(rank_rows == slot).astype(BF16)
+
+
+def gather_kernel(groups, per_group, parts, with_spill, my_ref, *refs):
+    out_hbm, held, sem = refs[-3:]
+    pieces = refs[:-3]
+    width = held.shape[-1]
     core = my_ref[1]
-    for place in range(count // parts):
-        pieces = refs[place * parts : (place + 1) * parts]
-        ids = pieces[0][0:16, width:].astype(F32)[0:8].astype(jnp.int32)
-        tokens = ids.shape[1]
-        labels = iota((groups, tokens), 0) * per_group + mine
-        named = indicator(labels == ids[0:1, :])
-        for entry in range(1, ids.shape[0]):
-            named = named + indicator(labels == ids[entry : entry + 1, :])
-        rank_rows = spread(jnp.where(named > 0.0, ranks_of(named), 99.0), SLOTS)
-        slot = (iota(rank_rows.shape, 0) & (SLOTS - 1)).astype(F32)
-        picks = indicator(rank_rows == slot).astype(BF16)
-        step = tokens // parts
-        rows = dot(picks[:, :step], pieces[0][:, :width])
+    for place in range(len(pieces) // parts):
+        block = pieces[place * parts : (place + 1) * parts]
+        picks = picks_for(ids_of(block[0], width), groups, per_group, my_ref[0])
+        step = picks.shape[1] // parts
+        rows = dot(picks[:, :step], block[0][:, :width])
         for part in range(1, parts):
-            rows = rows + dot(picks[:, part * step : (part + 1) * step], pieces[part][:, :width])
-        rows = rows.reshape(groups, 1, 1, SLOTS, width).astype(BF16)
+            rows = rows + dot(picks[:, part * step : (part + 1) * step], block[part][:, :width])
         side = core if place % 2 == 0 else 1 - core
-        out_ref[:, place // 2 : place // 2 + 1, pl.ds(side, 1)] = rows
-
-
-def expert_rows(blocks, weights, arrive):
+        held[:, pl.ds(2 * (place // 2) + side, 1)] = rows.reshape(groups, 1, SLOTS, width).astype(BF16)
+    if with_spill:
+        ids = ids_of(pieces[0], width)
+        named = marks_of(ids, iota((groups * per_group, ids.shape[1]), 0))
+        codes = group_sums(spill_codes(named, ranks_of(named)), groups)
+        slot = (iota(codes.shape, 0) & (SLOTS - 1)).astype(F32)
+        rows = dot(indicator(codes == slot + 1.0).astype(BF16), pieces[0][:, :width])
+        held[:, held.shape[1] - 1] = rows.reshape(groups, SLOTS, width).astype(BF16)
+    copy = pltpu.make_async_copy(held, out_hbm, sem)
+    copy.start()
+    copy.wait()
+
+
+SLICES = 3
+
+
+def expert_loads(sources, weights, sems):
+    gate_hbm, up_hbm, down_hbm = sources
     gate_w, up_w, down_w = weights
-    arrive(0)
-    gates = [dot(rows(), gate_w[...]) for rows in blocks]
-    arrive(1)
-    ups = [dot(rows(), up_w[...]) for rows in blocks]
-    hidden = [(g / (1.0 + jnp.exp(-g)) * u).astype(BF16) for g, u in zip(gates, ups)]
-    arrive(2)
-    return [dot(rows, down_w[...]).astype(BF16) for rows in hidden]
-
-
-def weight_copies(sources, weights, sems):
-    return [
-        pltpu.make_async_copy(source.at[0], weight, sems.at[place])
-        for place, (source, weight) in enumerate(zip(sources, weights))
-    ]
+    step = gate_w.shape[2]
+    loads = []
+    for part in range(SLICES):
+        units = pl.ds(part * step, step)
+        loads.append(
+            (
+                pltpu.make_async_copy(gate_hbm.at[0, :, units], gate_w.at[part], sems.at[part, 0]),
+                pltpu.make_async_copy(up_hbm.at[0, :, units], up_w.at[part], sems.at[part, 1]),
+                pltpu.make_async_copy(down_hbm.at[0, units], down_w.at[part], sems.at[part, 2]),
+            )
+        )
+    return loads
+
+
+def expert_rows(blocks, weights, loads, fresh=True):
+    gate_w, up_w, down_w = weights
+    totals = [None] * len(blocks)
+    for part in range(SLICES):
+        if fresh:
+            loads[part][0].wait()
+            loads[part][2].start()
+            if part + 1 < SLICES:
+                loads[part + 1][0].start()
+                loads[part + 1][1].start()
+        gates = [dot(rows(), gate_w[part]) for rows in blocks]
+        if fresh:
+            loads[part][1].wait()
+        ups = [dot(rows(), up_w[part]) for rows in blocks]
+        hidden = [(g / (1.0 + jnp.exp(-g)) * u).astype(BF16) for g, u in zip(gates, ups)]
+        if fresh:
+            loads[part][2].wait()
+        outs = [dot(rows, down_w[part]) for rows in hidden]
+        totals = [out if total is None else total + out for total, out in zip(totals, outs)]
+    return [total.astype(BF16) for total in totals]
 
 
 def main_kernel(first, chips_ref, rows_hbm, gate_hbm, up_hbm, down_hbm, *refs):
     out_hbm, held, done, gate_w, up_w, down_w, row_sems, sems, out_sems = refs[-9:]
     chips, groups, slots, width = held.shape
     weights = (gate_w, up_w, down_w)
-    loads = weight_copies((gate_hbm, up_hbm, down_hbm), weights, sems)
+    loads = expert_loads((gate_hbm, up_hbm, down_hbm), weights, sems)
     rows = [
-        pltpu.make_async_copy(rows_hbm.at[:, chip], held.at[chip], row_sems.at[chip]) for chip in range(chips)
+        pltpu.make_async_copy(rows_hbm.at[:, pl.ds(chip * slots, slots)], held.at[chip], row_sems.at[chip])
+        for chip in range(chips)
     ]
-    for copy in rows + loads:
+    for copy in [*rows, loads[0][0], loads[0][1]]:
         copy.start()
     for copy in rows:
         copy.wait()
     blocks = [lambda chip=chip: held[chip].reshape(groups * slots, width) for chip in range(chips)]
-    results = expert_rows(blocks, weights, lambda place: loads[place].wait())
+    results = expert_rows(blocks, weights, loads)
     stores = [
         pltpu.make_async_copy(done.at[chip], out_hbm.at[:, chips_ref[first + chip]], out_sems.at[chip])
         for chip in range(chips)
@@ -167,7 +200,7 @@
     weights = (gate_w, up_w, down_w)
     places = [(chip, side * tokens, tokens) for chip in range(chips - 1) for side in range(2)]
     places += [(chips - 1, quarter * half, half) for quarter in range(4)]
-    loads = weight_copies((gate_hbm, up_hbm, down_hbm), weights, sems)
+    loads = expert_loads((gate_hbm, up_hbm, down_hbm), weights, sems)
     rows = [
         pltpu.make_async_copy(piece, held.at[chip, pl.ds(start, count)], row_sems.at[place])
         for place, (piece, (chip, start, count)) in enumerate(zip(pieces, places))
@@ -180,13 +213,13 @@
 
     @pl.when(on_ref[0] != 0)
     def _():
-        for copy in rows + loads:
+        for copy in [*rows, loads[0][0], loads[0][1]]:
             copy.start()
         for copy in rows:
             copy.wait()
         for pair in range(chips // 2):
             blocks = [lambda chip=chip: held[chip] for chip in (2 * pair, 2 * pair + 1)]
-            results = expert_rows(blocks, weights, lambda place: loads[place].wait() if pair == 0 else None)
+            results = expert_rows(blocks, weights, loads, pair == 0)
             for chip, result in zip((2 * pair, 2 * pair + 1), results):
                 done[chip] = result
                 stores[2 * chip].start()
@@ -219,6 +252,10 @@
 
 def scalar():
     return pl.BlockSpec(memory_space=pltpu.SMEM)
+
+
+def hbm():
+    return pl.BlockSpec(memory_space=pltpu.HBM)
 
 
 def anywhere():
@@ -263,24 +300,13 @@
 def after(value, *earlier):
     return pl.pallas_call(
         order_kernel,
-        in_specs=[anywhere()] * (1 + len(earlier)),
-        out_specs=anywhere(),
+        in_specs=[hbm()] + [anywhere()] * len(earlier),
+        out_specs=hbm(),
         out_shape=jax.ShapeDtypeStruct(value.shape, value.dtype),
         input_output_aliases={0: 0},
         compiler_params=params(60),
         name="order",
     )(value, *earlier)
-
-
-def back_home(same, other):
-    half = same.shape[1] // 2
-    total = same + swap_cores(other)
-    far = total[3]
-    from_before = next_chip(far[:half], 1)
-    from_after = next_chip(far[half:], -1)
-    to_after = jnp.concatenate([total[2][:half] + from_before, total[2][half:]], axis=0)
-    to_before = jnp.concatenate([total[1][:half], total[1][half:] + from_after], axis=0)
-    return total[0] + next_chip(to_after, 1) + next_chip(to_before, -1)
 
 
 def shards(activations, expert_ids, route_gates, gate_proj, up_proj, down_proj):
@@ -298,82 +324,84 @@
     id_rows = expert_ids.T
     gate_rows = route_gates.T
 
-    packed, spill = pl.pallas_call(
-        functools.partial(pack_kernel, groups, experts),
+    packed = pl.pallas_call(
+        pack_kernel,
         in_specs=[whole(), whole()],
-        out_specs=[whole(), whole()],
-        out_shape=[
-            jax.ShapeDtypeStruct((tokens, width + tokens), BF16),
-            jax.ShapeDtypeStruct((groups * SLOTS, width), BF16),
-        ],
+        out_specs=whole(),
+        out_shape=jax.ShapeDtypeStruct((tokens, width + tokens), BF16),
         compiler_params=params(16),
         name="pack_rows",
     )(id_rows, activations)
-    spill_in = lax.all_to_all(spill.reshape(groups, SLOTS, width), "node", split_axis=0, concat_axis=0, tiled=True)
-
-    def pick(pieces, parts):
+
+    def pick(pieces, parts, with_spill):
+        count = len(pieces) // parts + with_spill
         return pl.pallas_call(
-            functools.partial(gather_kernel, groups, per_group, parts, len(pieces)),
+            functools.partial(gather_kernel, groups, per_group, parts, with_spill),
             in_specs=[scalar()] + [whole()] * len(pieces),
-            out_specs=whole(),
-            out_shape=jax.ShapeDtypeStruct((groups, len(pieces) // parts // 2, 2, SLOTS, width), BF16),
+            out_specs=hbm(),
+            out_shape=jax.ShapeDtypeStruct((groups, count, SLOTS, width), BF16),
+            scratch_shapes=[pltpu.VMEM((groups, count, SLOTS, width), BF16), pltpu.SemaphoreType.DMA],
             compiler_params=params(24),
             name="main_rows",
         )(place, *pieces)
 
     def send(rows):
-        count = rows.shape[1]
-        sent = rows.reshape(groups, count * 2 * SLOTS, width)
-        sent = lax.all_to_all(sent, "node", split_axis=0, concat_axis=0, tiled=True)
-        return sent.reshape(groups, count, 2 * SLOTS, width)
+        sent = rows.reshape(groups, rows.shape[1] * SLOTS, width)
+        return lax.all_to_all(sent, "node", split_axis=0, concat_axis=0, tiled=True)
 
     own, near, far = around(packed)
-    spill_own, spill_near, spill_far = around(spill_in.reshape(groups * SLOTS, width))
-    own_in = send(after(pick(own, 1), spill_in))
-    near_rows = pick(near, 1)
-    near_in = send(after(near_rows, own_in, spill_near[0], spill_near[2]))
-    far_rows = pick(far, 2)
+    own_in = send(pick(own, 1, True))
+    near_rows = pick(near, 1, False)
+    near_in = send(after(near_rows, own_in))
+    spill_in = own_in[:, 2 * SLOTS :].reshape(groups * SLOTS, width)
+    spill_own, spill_near, spill_far = around(spill_in)
 
     busiest = (jnp.sum((expert_ids == my_expert).astype(jnp.int32)) > SLOTS).astype(jnp.int32).reshape(1)
+    step = hidden // SLICES
     weight_space = [
-        pltpu.VMEM((width, hidden), BF16),
-        pltpu.VMEM((width, hidden), BF16),
-        pltpu.VMEM((hidden, width), BF16),
+        pltpu.VMEM((SLICES, width, step), BF16),
+        pltpu.VMEM((SLICES, width, step), BF16),
+        pltpu.VMEM((SLICES, step, width), BF16),
     ]
-    earlier = [own_in]
     spill_same, spill_other = pl.pallas_call(
         spill_kernel,
-        in_specs=[scalar()] + [anywhere()] * (13 + len(earlier)),
-        out_specs=[anywhere(), anywhere()],
+        in_specs=[scalar()] + [anywhere()] * 15,
+        out_specs=[hbm(), hbm()],
         out_shape=[jax.ShapeDtypeStruct((chips, groups * SLOTS, width), BF16)] * 2,
         scratch_shapes=[pltpu.VMEM((chips, 2 * groups * SLOTS, width), BF16)] * 2
         + weight_space
-        + [pltpu.SemaphoreType.DMA((10,)), pltpu.SemaphoreType.DMA((3,)), pltpu.SemaphoreType.DMA((chips, 2))],
+        + [pltpu.SemaphoreType.DMA((10,)), pltpu.SemaphoreType.DMA((SLICES, 3)), pltpu.SemaphoreType.DMA((chips, 2))],
         compiler_params=params(60),
         cost_estimate=expert_cost(per_group * groups * SLOTS, width, hidden),
         name="spill_expert",
-    )(busiest, *spill_own, *spill_near, *spill_far, gate_proj, up_proj, down_proj, *earlier)
-    far_in = send(after(far_rows, near_in, spill_same))
-    spill_back = back_home(spill_same, after(spill_other, near_in))
-
-    main_out = spill_same
-    first = 0
-    for arrival in (own_in, near_in, far_in):
-        count = arrival.shape[1]
-        main_out = pl.pallas_call(
+    )(busiest, *spill_own, *spill_near, *spill_far, gate_proj, up_proj, down_proj, far[2], far[3])
+    far_in = send(after(pick(far, 2, False), near_in, spill_same))
+
+    def main_expert(arrival, first, count, main_out, *earlier):
+        return pl.pallas_call(
             functools.partial(main_kernel, first),
-            in_specs=[scalar()] + [anywhere()] * 5,
-            out_specs=anywhere(),
+            in_specs=[scalar()] + [anywhere()] * (5 + len(earlier)),
+            out_specs=hbm(),
             out_shape=jax.ShapeDtypeStruct((groups, chips, 2 * SLOTS, width), BF16),
             scratch_shapes=[pltpu.VMEM((count, groups, 2 * SLOTS, width), BF16)] * 2
             + weight_space
-            + [pltpu.SemaphoreType.DMA((count,)), pltpu.SemaphoreType.DMA((3,)), pltpu.SemaphoreType.DMA((count,))],
+            + [pltpu.SemaphoreType.DMA((count,)), pltpu.SemaphoreType.DMA((SLICES, 3)), pltpu.SemaphoreType.DMA((count,))],
             input_output_aliases={5: 0} if first else {},
             compiler_params=params(60),
             cost_estimate=expert_cost(count * 2 * groups * SLOTS, width, hidden),
             name="main_expert",
-        )(order, arrival, gate_proj, up_proj, down_proj, main_out)
-        first += count
+        )(order, arrival, gate_proj, up_proj, down_proj, main_out, *earlier)
+
+    main_out = main_expert(own_in, 0, 1, spill_same, near_in)
+    half = groups * SLOTS // 2
+    total = spill_same + swap_cores(after(spill_other, near_in))
+    from_before = next_chip(total[3, :half], 1)
+    from_after = next_chip(total[3, half:], -1)
+    main_out = main_expert(near_in, 1, 2, main_out, total)
+    to_after = jnp.concatenate([total[2, :half] + from_before, total[2, half:]], axis=0)
+    to_before = jnp.concatenate([total[1, :half], total[1, half:] + from_after], axis=0)
+    main_out = main_expert(far_in, 3, 1, main_out, to_after, to_before)
+    spill_back = total[0] + next_chip(to_after, 1) + next_chip(to_before, -1)
 
     main_w, spill_w = pl.pallas_call(
         functools.partial(weight_kernel, groups, experts),

time: 227 us -> 235 us (1.035)
  waiting for transfers between devices: 93.5 us -> 98.9 us
  other arithmetic: 4.76 us -> 9.19 us
    ppermute x12, waiting for transfers between devices: 77.7 us -> 89 us  [next_chip(): lax.ppermute(value, 'local', [(i, (i + 2 * hops) % size) for i in range(s...]
    all_to_all x4 -> x3, waiting for transfers between devices: 9.6 us -> 0.01 us  [send(): return lax.all_to_all(sent, 'node', split_axis=0, concat_axis=0, tiled=True)]
    ppermute x11, starting transfers between devices: 9.67 us -> 1.39 us  [swap_cores(): return lax.ppermute(value, 'local', [(i, i ^ 1) for i in range(size)])]
    all_to_all x4 -> x3, starting transfers between devices: 28.5 us -> 35 us  [send(): return lax.all_to_all(sent, 'node', split_axis=0, concat_axis=0, tiled=True)]
    unnamed x36 -> x38, local copies, waits for them, and re-layouts: 12 us -> 8.92 us
    add x3, other arithmetic: 3.32 us -> 6.11 us  [the longest x1 3.01 us: shards(): total = spill_same + swap_cores(after(spill_other, near_in))]
    ppermute x11, waiting for transfers between devices: 0.03 us -> 2.42 us  [swap_cores(): return lax.ppermute(value, 'local', [(i, i ^ 1) for i in range(size)])]
    pallas_call x10 -> x9, Pallas kernels: 31.1 us -> 30.5 us  [the longest x3 27.7 us: main_expert(): pl.pallas_call(functools.partial(main_kernel, first), in_specs=[scalar()]...]
  transfers between devices with their start and end apart: 29 -> 28, of which waited for: 11 -> 9; matrix products, arithmetic and copies ran while one was open for 3% -> 6% of each run, Pallas kernels for 16% -> 11%
where the time goes in v3:
time: 235 us; the launch traced here: 232 us
  waiting for transfers between devices  98.9 us (42%)
  starting transfers between devices  67.7 us (29%)
  Pallas kernels  42 us (18%)
  local copies, waits for them, and re-layouts  13.6 us (6%)
  other arithmetic  9.19 us (4%)
    ppermute x12, waiting for transfers between devices, next_chip(): lax.ppermute(value, 'local', [(i, (i + 2 * hops) % size) for i in range(s...  89 us
    all_to_all x3, starting transfers between devices, send(): return lax.all_to_all(sent, 'node', split_axis=0, concat_axis=0, tiled=True)  35 us
    pallas_call x3, Pallas kernels, main_expert(): pl.pallas_call(functools.partial(main_kernel, first), in_specs=[scalar()]...  27.7 us
    ppermute x12, starting transfers between devices, next_chip(): lax.ppermute(value, 'local', [(i, (i + 2 * hops) % size) for i in range(s...  15.4 us
    unnamed x38, local copies, waits for them, and re-layouts  8.92 us
    all_to_all x1, starting transfers between devices, shards(): lax.all_to_all(main_out.reshape(experts, SLOTS, width), ('node', 'local')...  8.21 us
    all_to_all x1, starting transfers between devices, shards(): lax.all_to_all(after(spill_back, main_back).reshape(groups, SLOTS, width)...  7.75 us
    all_to_all x1, waiting for transfers between devices, shards(): lax.all_to_all(after(spill_back, main_back).reshape(groups, SLOTS, width)...  7.49 us
  transfers between devices with their start and end apart: 28, of which 9 were waited for; matrix products, arithmetic and copies ran while one was open for 6% of the time, Pallas kernels for 11%

profile of v3, /device:TPU:2, one launch (start us, length us, event | category | flops | bytes accessed | tf_op | source)
XLA Modules:
  0.0 232.4 jit_solution(13573019861261001048)
XLA Ops:
  3.8 3.0 %main_rows.5 = bf16[16,3,8,2048]{3,2,1,0:T(8,128)(2,1)} custom-call(s32[2]{0:T(128)S(1)} %pad_add_fusion.1.my_ref, bf16[128,2176]{1,0:T(8,128)(2,1)S(1)} %pack_rows.1.refs_0_, bf16[128,2176]{1,0:T(8,128)(2,1)S(1)} %collective-permute-done.8.refs_1_), custom_call_target="tpu_custom_call" | custom-call | tf_op jit(solution)/shard_map/main_rows/pallas_call | solution.py:338
  6.9 8.3 %all-to-all-start = ((bf16[16,24,2048]{2,1,0:T(8,128)(2,1)}), bf16[16,24,2048]{2,1,0:T(8,128)(2,1)S(1)}, u32[]{:S(2)}, u32[]{:S(2)}) async-start(bf16[16,24,2048]{2,1,0:T(8,128)(2,1)} %bitcast.8), calls=%async_computation | async-start | bytes 3145728 | tf_op jit(solution)/shard_map/all_to_all | solution.py:350
  15.2 3.0 %collective-permute-start.2 = (bf16[128,2176]{1,0:T(8,128)(2,1)S(1)}, bf16[128,2176]{1,0:T(8,128)(2,1)S(1)}, u32[]{:S(2)}, u32[]{:S(2)}) collective-permute-start(bf16[128,2176]{1,0:T(8,128)(2,1)S(1)} %pack_rows.1.refs_0_), channel_id=1, source_target_pairs={{0,6},{1,7},{2,0},{3,1},{4,2},{5,3},{6,4},{7,5},{8,14},{9,15},{10,... | collective-permute-start | bytes 1671176 | tf_op jit(solution)/shard_map/ppermute | solution.py:280
  18.2 11.6 %collective-permute-done.2.refs_2_ = bf16[128,2176]{1,0:T(8,128)(2,1)S(1)} collective-permute-done((bf16[128,2176]{1,0:T(8,128)(2,1)S(1)}, bf16[128,2176]{1,0:T(8,128)(2,1)S(1)}, u32[]{:S(2)}, u32[]{:S(2)}) %collective-permute-start.2) | collective-permute-done | bytes 557088 | tf_op jit(solution)/shard_map/ppermute | solution.py:280
  29.8 3.4 %collective-permute-done.refs_0_ = bf16[128,2176]{1,0:T(8,128)(2,1)S(1)} collective-permute-done((bf16[128,2176]{1,0:T(8,128)(2,1)S(1)}, bf16[128,2176]{1,0:T(8,128)(2,1)S(1)}, u32[]{:S(2)}, u32[]{:S(2)}) %collective-permute-start) | collective-permute-done | bytes 557088 | tf_op jit(solution)/shard_map/ppermute | solution.py:280
  36.1 2.4 %main_rows.4.value_ref = bf16[16,4,8,2048]{3,2,1,0:T(8,128)(2,1)S(1)} custom-call(s32[2]{0:T(128)S(1)} %pad_add_fusion.1.my_ref, bf16[128,2176]{1,0:T(8,128)(2,1)S(1)} %collective-permute-done.refs_0_, bf16[128,2176]{1,0:T(8,128)(2,1)S(1)} %collective-permute-done.6.refs_1_, bf16[128,2176]{1,0:T(8,128)(2,1)S(1)} %collective-permute-done.2.refs_2_, ...), custom_call_target="tpu_custom_call" | custom-call | tf_op jit(solution)/shard_map/main_rows/pallas_call | solution.py:338
  41.0 7.2 %all-to-all-start.1 = ((bf16[16,32,2048]{2,1,0:T(8,128)(2,1)}), bf16[16,32,2048]{2,1,0:T(8,128)(2,1)S(1)}, u32[]{:S(2)}, u32[]{:S(2)}) async-start(bf16[16,32,2048]{2,1,0:T(8,128)(2,1)} %bitcast.40), calls=%async_computation.1 | async-start | bytes 4194304 | tf_op jit(solution)/shard_map/all_to_all | solution.py:350
  50.1 2.0 collective-permute-start.12
  52.8 10.9 %collective-permute-done.12.refs_4_ = bf16[128,2048]{1,0:T(8,128)(2,1)} collective-permute-done((bf16[128,2048]{1,0:T(8,128)(2,1)}, bf16[128,2048]{1,0:T(8,128)(2,1)}, u32[]{:S(2)}, u32[]{:S(2)}) %collective-permute-start.12) | collective-permute-done | bytes 524320 | tf_op jit(solution)/shard_map/ppermute | solution.py:280
  64.6 2.8 %collective-permute-start.15 = (bf16[64,2048]{1,0:T(8,128)(2,1)S(1)}, bf16[64,2048]{1,0:T(8,128)(2,1)S(1)}, u32[]{:S(2)}, u32[]{:S(2)}) collective-permute-start(bf16[64,2048]{1,0:T(8,128)(2,1)S(1)} %slice.52), channel_id=1, source_target_pairs={{0,6},{1,7},{2,0},{3,1},{4,2},{5,3},{6,4},{7,5},{8,14},{9,15},{10,... | collective-permute-start | bytes 786440 | tf_op jit(solution)/shard_map/ppermute | solution.py:280
  69.1 2.3 %collective-permute-done.15.refs_7_ = bf16[64,2048]{1,0:T(8,128)(2,1)S(1)} collective-permute-done((bf16[64,2048]{1,0:T(8,128)(2,1)S(1)}, bf16[64,2048]{1,0:T(8,128)(2,1)S(1)}, u32[]{:S(2)}, u32[]{:S(2)}) %collective-permute-start.15) | collective-permute-done | bytes 262176 | tf_op jit(solution)/shard_map/ppermute | solution.py:280
  71.4 4.7 %collective-permute-done.14.refs_6_ = bf16[64,2048]{1,0:T(8,128)(2,1)} collective-permute-done((bf16[64,2048]{1,0:T(8,128)(2,1)S(1)}, bf16[64,2048]{1,0:T(8,128)(2,1)}, u32[]{:S(2)}, u32[]{:S(2)}) %collective-permute-start.14) | collective-permute-done | bytes 262176 | tf_op jit(solution)/shard_map/ppermute | solution.py:280
  78.0 2.7 %spill_expert.1 = (bf16[4,128,2048]{2,1,0:T(8,128)(2,1)}, bf16[4,128,2048]{2,1,0:T(8,128)(2,1)}) custom-call(s32[1]{0:T(128)} %bitcast.10.on_ref, bf16[128,2048]{1,0:T(8,128)(2,1)} %slice_bitcast_fusion.1.refs_0_, bf16[128,2048]{1,0:T(8,128)(2,1)} %collective-permute-done.9.refs_1_, bf16[128,2048]{1,0:T(8,128)(2,1)} %collective-permute-done.10.refs_2_, ...), custom_call_target="tpu_custom_call" | custom-call | flops 9663676416 | bytes 17825792 | tf_op jit(solution)/shard_map/spill_expert/pallas_call | solution.py:366
  86.2 19.4 %all-to-all-start.2 = ((bf16[16,16,2048]{2,1,0:T(8,128)(2,1)}), bf16[16,16,2048]{2,1,0:T(8,128)(2,1)}, u32[]{:S(2)}, u32[]{:S(2)}) async-start(bf16[16,16,2048]{2,1,0:T(8,128)(2,1)} %bitcast.41), calls=%async_computation.2 | async-start | bytes 2097152 | tf_op jit(solution)/shard_map/all_to_all | solution.py:350
  105.6 8.8 %main_expert.3.refs_0_ = bf16[16,4,16,2048]{3,2,1,0:T(8,128)(2,1)} custom-call(s32[4]{0:T(128)} %pad_add_fusion.chips_ref, bf16[16,24,2048]{2,1,0:T(8,128)(2,1)} %copy-done.14, bf16[1,2048,768]{2,1,0:T(8,128)(2,1)} %gate_hbm.5, bf16[1,2048,768]{2,1,0:T(8,128)(2,1)} %up_hbm.5, bf16[1,768,2048]{2,1,0:T(8,128)(2,1)} %down_hbm.5, ...), custom_call_target="tpu_custom_call" | custom-call | flops 2415919104 | bytes 11534336 | tf_op jit(solution)/shard_map/main_expert/pallas_call | solution.py:381
  114.4 3.0 %add.44.refs_1_ = bf16[4,128,2048]{2,1,0:T(8,128)(2,1)S(1)} add(bf16[4,128,2048]{2,1,0:T(8,128)(2,1)} %get-tuple-element.11.refs_1_.refs_0_, bf16[4,128,2048]{2,1,0:T(8,128)(2,1)} %collective-permute-done.18) | non-fusion elementwise | flops 1048576 | bytes 6291456 | tf_op jit(solution)/shard_map/add | solution.py:397
  117.6 2.0 collective-permute-start.19
  119.6 10.2 %main_expert.4.refs_0_ = bf16[16,4,16,2048]{3,2,1,0:T(8,128)(2,1)} custom-call(s32[4]{0:T(128)} %pad_add_fusion.chips_ref, bf16[16,32,2048]{2,1,0:T(8,128)(2,1)} %copy-done.12, bf16[1,2048,768]{2,1,0:T(8,128)(2,1)} %gate_hbm.5, bf16[1,2048,768]{2,1,0:T(8,128)(2,1)} %up_hbm.5, bf16[1,768,2048]{2,1,0:T(8,128)(2,1)} %down_hbm.5, ...), custom_call_target="tpu_custom_call", output_to_operand_aliasing={{}: (5, {})} | custom-call | flops 4831838208 | bytes 13631488 | tf_op jit(solution)/shard_map/main_expert/pallas_call | solution.py:381
  132.6 8.8 %main_expert.5 = bf16[16,4,16,2048]{3,2,1,0:T(8,128)(2,1)} custom-call(s32[4]{0:T(128)} %pad_add_fusion.chips_ref, bf16[16,16,2048]{2,1,0:T(8,128)(2,1)} %all-to-all-done.2.rows_hbm, bf16[1,2048,768]{2,1,0:T(8,128)(2,1)} %gate_hbm.5, bf16[1,2048,768]{2,1,0:T(8,128)(2,1)} %up_hbm.5, bf16[1,768,2048]{2,1,0:T(8,128)(2,1)} %down_hbm.5, ...), custom_call_target="tpu_custom_call", output_to_operand_aliasing={{}: (5, {})} | custom-call | flops 2415919104 | bytes 11534336 | tf_op jit(solution)/shard_map/main_expert/pallas_call | solution.py:381
  141.4 8.2 %all-to-all-start.3 = ((bf16[128,8,2048]{2,1,0:T(8,128)(2,1)}), bf16[128,8,2048]{2,1,0:T(8,128)(2,1)}, u32[]{:S(2)}, u32[]{:S(2)}) async-start(bf16[128,8,2048]{2,1,0:T(8,128)(2,1)} %bitcast.45), calls=%async_computation.3 | async-start | bytes 8388608 | tf_op jit(solution)/shard_map/all_to_all | solution.py:417
  152.9 56.0 %collective-permute-done.21 = bf16[128,2048]{1,0:T(8,128)(2,1)S(1)} collective-permute-done((bf16[128,2048]{1,0:T(8,128)(2,1)S(1)}, bf16[128,2048]{1,0:T(8,128)(2,1)S(1)}, u32[]{:S(2)}, u32[]{:S(2)}) %collective-permute-start.21) | collective-permute-done | bytes 524320 | tf_op jit(solution)/shard_map/ppermute | solution.py:280
  210.9 7.8 %all-to-all-start.4 = ((bf16[16,8,2048]{2,1,0:T(8,128)(2,1)}), bf16[16,8,2048]{2,1,0:T(8,128)(2,1)S(1)}, u32[]{:S(2)}, u32[]{:S(2)}) async-start(bf16[16,8,2048]{2,1,0:T(8,128)(2,1)} %bitcast.46), calls=%async_computation.4 | async-start | bytes 1048576 | tf_op jit(solution)/shard_map/all_to_all | solution.py:420
  220.5 7.5 %all-to-all-done.4 = bf16[16,8,2048]{2,1,0:T(8,128)(2,1)S(1)} async-done(((bf16[16,8,2048]{2,1,0:T(8,128)(2,1)}), bf16[16,8,2048]{2,1,0:T(8,128)(2,1)S(1)}, u32[]{:S(2)}, u32[]{:S(2)}) %all-to-all-start.4) | async-done | bytes 524320 | tf_op jit(solution)/shard_map/all_to_all | solution.py:420
  228.7 3.6 %combine.1 = bf16[128,2048]{1,0:T(8,128)(2,1)} custom-call(bf16[1024,128]{1,0:T(8,128)(2,1)} %copy-done.7, bf16[128,128]{1,0:T(8,128)(2,1)} %copy-done.10, bf16[1024,2048]{1,0:T(8,128)(2,1)} %bitcast.20.main_ref, bf16[128,2048]{1,0:T(8,128)(2,1)} %bitcast.47), custom_call_target="tpu_custom_call" | custom-call | tf_op jit(solution)/shard_map/combine/pallas_call | solution.py:425
  (98 shorter events, 31.7 us)
Async XLA Ops:
  6.9 33.0 %all-to-all-start = ((bf16[16,24,2048]{2,1,0:T(8,128)(2,1)}), bf16[16,24,2048]{2,1,0:T(8,128)(2,1)S(1)}, u32[]{:S(2)}, u32[]{:S(2)}) async-start(bf16[16,24,2048]{2,1,0:T(8,128)(2,1)} %bitcast.8), calls=%async_computation | async-start | bytes 3145728 | tf_op jit(solution)/shard_map/all_to_all | solution.py:350
  15.2 14.6 %collective-permute-start.2 = (bf16[128,2176]{1,0:T(8,128)(2,1)S(1)}, bf16[128,2176]{1,0:T(8,128)(2,1)S(1)}, u32[]{:S(2)}, u32[]{:S(2)}) collective-permute-start(bf16[128,2176]{1,0:T(8,128)(2,1)S(1)} %pack_rows.1.refs_0_), channel_id=1, source_target_pairs={{0,6},{1,7},{2,0},{3,1},{4,2},{5,3},{6,4},{7,5},{8,14},{9,15},{10,... | collective-permute-start | bytes 1671176 | tf_op jit(solution)/shard_map/ppermute | solution.py:280
  18.2 15.0 %collective-permute-start = (bf16[128,2176]{1,0:T(8,128)(2,1)S(1)}, bf16[128,2176]{1,0:T(8,128)(2,1)S(1)}, u32[]{:S(2)}, u32[]{:S(2)}) collective-permute-start(bf16[128,2176]{1,0:T(8,128)(2,1)S(1)} %pack_rows.1.refs_0_), channel_id=1, source_target_pairs={{0,2},{1,3},{2,4},{3,5},{4,6},{5,7},{6,0},{7,1},{8,10},{9,11},{10,... | collective-permute-start | bytes 1671176 | tf_op jit(solution)/shard_map/ppermute | solution.py:280
  29.8 6.3 %collective-permute-start.7 = (bf16[128,2176]{1,0:T(8,128)(2,1)S(1)}, bf16[128,2176]{1,0:T(8,128)(2,1)S(1)}, u32[]{:S(2)}, u32[]{:S(2)}) collective-permute-start(bf16[128,2176]{1,0:T(8,128)(2,1)S(1)} %collective-permute-done.2.refs_2_), channel_id=1, source_target_pairs={{0,1},{1,0},{2,3},{3,2},{4,5},{5,4},{6,7},{7,6},{8,9},{9,8},{10,11... | collective-permute-start | bytes 1671176 | tf_op jit(solution)/shard_map/ppermute | solution.py:275
  34.0 18.2 %collective-permute-start.3 = (bf16[64,2176]{1,0:T(8,128)(2,1)}, bf16[64,2176]{1,0:T(8,128)(2,1)S(1)}, u32[]{:S(2)}, u32[]{:S(2)}) collective-permute-start(bf16[64,2176]{1,0:T(8,128)(2,1)} %slice.49), channel_id=1, source_target_pairs={{0,6},{1,7},{2,0},{3,1},{4,2},{5,3},{6,4},{7,5},{8,14},{9,15},{10,... | collective-permute-start | bytes 835592 | tf_op jit(solution)/shard_map/ppermute | solution.py:280
  34.8 17.4 %collective-permute-start.1 = (bf16[64,2176]{1,0:T(8,128)(2,1)S(1)}, bf16[64,2176]{1,0:T(8,128)(2,1)S(1)}, u32[]{:S(2)}, u32[]{:S(2)}) collective-permute-start(bf16[64,2176]{1,0:T(8,128)(2,1)S(1)} %slice.48), channel_id=1, source_target_pairs={{0,2},{1,3},{2,4},{3,5},{4,6},{5,7},{6,0},{7,1},{8,10},{9,11},{10,... | collective-permute-start | bytes 835592 | tf_op jit(solution)/shard_map/ppermute | solution.py:280
  41.0 39.8 %all-to-all-start.1 = ((bf16[16,32,2048]{2,1,0:T(8,128)(2,1)}), bf16[16,32,2048]{2,1,0:T(8,128)(2,1)S(1)}, u32[]{:S(2)}, u32[]{:S(2)}) async-start(bf16[16,32,2048]{2,1,0:T(8,128)(2,1)} %bitcast.40), calls=%async_computation.1 | async-start | bytes 4194304 | tf_op jit(solution)/shard_map/all_to_all | solution.py:350
  50.1 13.5 %collective-permute-start.12 = (bf16[128,2048]{1,0:T(8,128)(2,1)}, bf16[128,2048]{1,0:T(8,128)(2,1)}, u32[]{:S(2)}, u32[]{:S(2)}) collective-permute-start(bf16[128,2048]{1,0:T(8,128)(2,1)} %slice_bitcast_fusion.1.refs_0_), channel_id=1, source_target_pairs={{0,6},{1,7},{2,0},{3,1},{4,2},{5,3},{6,4},{7,5},{8,14},{9,15},{10,... | collective-permute-start | bytes 1572872 | tf_op jit(solution)/shard_map/ppermute | solution.py:280
  52.1 15.3 %collective-permute-start.10 = (bf16[128,2048]{1,0:T(8,128)(2,1)}, bf16[128,2048]{1,0:T(8,128)(2,1)}, u32[]{:S(2)}, u32[]{:S(2)}) collective-permute-start(bf16[128,2048]{1,0:T(8,128)(2,1)} %slice_bitcast_fusion.1.refs_0_), channel_id=1, source_target_pairs={{0,2},{1,3},{2,4},{3,5},{4,6},{5,7},{6,0},{7,1},{8,10},{9,11},{10,... | collective-permute-start | bytes 1572872 | tf_op jit(solution)/shard_map/ppermute | solution.py:280
  52.2 16.3 %collective-permute-start.5 = (bf16[64,2176]{1,0:T(8,128)(2,1)S(1)}, bf16[64,2176]{1,0:T(8,128)(2,1)S(1)}, u32[]{:S(2)}, u32[]{:S(2)}) collective-permute-start(bf16[64,2176]{1,0:T(8,128)(2,1)S(1)} %collective-permute-done.3.refs_1_), channel_id=1, source_target_pairs={{0,1},{1,0},{2,3},{3,2},{4,5},{5,4},{6,7},{7,6},{8,9},{9,8},{10,11... | collective-permute-start | bytes 835592 | tf_op jit(solution)/shard_map/ppermute | solution.py:275
  52.2 16.4 %collective-permute-start.4 = (bf16[64,2176]{1,0:T(8,128)(2,1)S(1)}, bf16[64,2176]{1,0:T(8,128)(2,1)S(1)}, u32[]{:S(2)}, u32[]{:S(2)}) collective-permute-start(bf16[64,2176]{1,0:T(8,128)(2,1)S(1)} %collective-permute-done.1.refs_0_), channel_id=1, source_target_pairs={{0,1},{1,0},{2,3},{3,2},{4,5},{5,4},{6,7},{7,6},{8,9},{9,8},{10,11... | collective-permute-start | bytes 835592 | tf_op jit(solution)/shard_map/ppermute | solution.py:275
  52.7 24.8 %collective-permute-start.9 = (bf16[128,2048]{1,0:T(8,128)(2,1)}, bf16[128,2048]{1,0:T(8,128)(2,1)}, u32[]{:S(2)}, u32[]{:S(2)}) collective-permute-start(bf16[128,2048]{1,0:T(8,128)(2,1)} %slice_bitcast_fusion.1.refs_0_), channel_id=1, source_target_pairs={{0,1},{1,0},{2,3},{3,2},{4,5},{5,4},{6,7},{7,6},{8,9},{9,8},{10,11... | collective-permute-start | bytes 1572872 | tf_op jit(solution)/shard_map/ppermute | solution.py:275
  64.6 6.8 %collective-permute-start.15 = (bf16[64,2048]{1,0:T(8,128)(2,1)S(1)}, bf16[64,2048]{1,0:T(8,128)(2,1)S(1)}, u32[]{:S(2)}, u32[]{:S(2)}) collective-permute-start(bf16[64,2048]{1,0:T(8,128)(2,1)S(1)} %slice.52), channel_id=1, source_target_pairs={{0,6},{1,7},{2,0},{3,1},{4,2},{5,3},{6,4},{7,5},{8,14},{9,15},{10,... | collective-permute-start | bytes 786440 | tf_op jit(solution)/shard_map/ppermute | solution.py:280
  68.4 7.8 %collective-permute-start.14 = (bf16[64,2048]{1,0:T(8,128)(2,1)S(1)}, bf16[64,2048]{1,0:T(8,128)(2,1)}, u32[]{:S(2)}, u32[]{:S(2)}) collective-permute-start(bf16[64,2048]{1,0:T(8,128)(2,1)S(1)} %slice.51), channel_id=1, source_target_pairs={{0,2},{1,3},{2,4},{3,5},{4,6},{5,7},{6,0},{7,1},{8,10},{9,11},{10,... | collective-permute-start | bytes 786440 | tf_op jit(solution)/shard_map/ppermute | solution.py:280
  68.5 9.5 %collective-permute-start.13 = (bf16[128,2048]{1,0:T(8,128)(2,1)}, bf16[128,2048]{1,0:T(8,128)(2,1)}, u32[]{:S(2)}, u32[]{:S(2)}) collective-permute-start(bf16[128,2048]{1,0:T(8,128)(2,1)} %collective-permute-done.12.refs_4_), channel_id=1, source_target_pairs={{0,1},{1,0},{2,3},{3,2},{4,5},{5,4},{6,7},{7,6},{8,9},{9,8},{10,11... | collective-permute-start | bytes 1572872 | tf_op jit(solution)/shard_map/ppermute | solution.py:275
  68.6 9.4 %collective-permute-start.11 = (bf16[128,2048]{1,0:T(8,128)(2,1)}, bf16[128,2048]{1,0:T(8,128)(2,1)}, u32[]{:S(2)}, u32[]{:S(2)}) collective-permute-start(bf16[128,2048]{1,0:T(8,128)(2,1)} %collective-permute-done.10.refs_2_), channel_id=1, source_target_pairs={{0,1},{1,0},{2,3},{3,2},{4,5},{5,4},{6,7},{7,6},{8,9},{9,8},{10,11... | collective-permute-start | bytes 1572872 | tf_op jit(solution)/shard_map/ppermute | solution.py:275
  82.2 32.2 %collective-permute-start.18 = (bf16[4,128,2048]{2,1,0:T(8,128)(2,1)}, bf16[4,128,2048]{2,1,0:T(8,128)(2,1)}, u32[]{:S(2)}, u32[]{:S(2)}) collective-permute-start(bf16[4,128,2048]{2,1,0:T(8,128)(2,1)} %order.6), channel_id=1, source_target_pairs={{0,1},{1,0},{2,3},{3,2},{4,5},{5,4},{6,7},{7,6},{8,9},{9,8},{10,11... | collective-permute-start | bytes 6291464 | tf_op jit(solution)/shard_map/ppermute | solution.py:275
  86.2 46.4 %all-to-all-start.2 = ((bf16[16,16,2048]{2,1,0:T(8,128)(2,1)}), bf16[16,16,2048]{2,1,0:T(8,128)(2,1)}, u32[]{:S(2)}, u32[]{:S(2)}) async-start(bf16[16,16,2048]{2,1,0:T(8,128)(2,1)} %bitcast.41), calls=%async_computation.2 | async-start | bytes 2097152 | tf_op jit(solution)/shard_map/all_to_all | solution.py:350
  117.5 12.3 %collective-permute-start.20 = (bf16[64,2048]{1,0:T(8,128)(2,1)S(1)}, bf16[64,2048]{1,0:T(8,128)(2,1)S(1)}, u32[]{:S(2)}, u32[]{:S(2)}) collective-permute-start(bf16[64,2048]{1,0:T(8,128)(2,1)S(1)} %get-tuple-element.14), channel_id=1, source_target_pairs={{0,6},{1,7},{2,0},{3,1},{4,2},{5,3},{6,4},{7,5},{8,14},{9,15},{10,... | collective-permute-start | bytes 786440 | tf_op jit(solution)/shard_map/ppermute | solution.py:280
  117.6 12.2 %collective-permute-start.19 = (bf16[64,2048]{1,0:T(8,128)(2,1)S(1)}, bf16[64,2048]{1,0:T(8,128)(2,1)S(1)}, u32[]{:S(2)}, u32[]{:S(2)}) collective-permute-start(bf16[64,2048]{1,0:T(8,128)(2,1)S(1)} %get-tuple-element.16), channel_id=1, source_target_pairs={{0,2},{1,3},{2,4},{3,5},{4,6},{5,7},{6,0},{7,1},{8,10},{9,11},{10,... | collective-permute-start | bytes 786440 | tf_op jit(solution)/shard_map/ppermute | solution.py:280
  141.4 69.5 %all-to-all-start.3 = ((bf16[128,8,2048]{2,1,0:T(8,128)(2,1)}), bf16[128,8,2048]{2,1,0:T(8,128)(2,1)}, u32[]{:S(2)}, u32[]{:S(2)}) async-start(bf16[128,8,2048]{2,1,0:T(8,128)(2,1)} %bitcast.45), calls=%async_computation.3 | async-start | bytes 8388608 | tf_op jit(solution)/shard_map/all_to_all | solution.py:417
  149.6 59.3 %collective-permute-start.21 = (bf16[128,2048]{1,0:T(8,128)(2,1)S(1)}, bf16[128,2048]{1,0:T(8,128)(2,1)S(1)}, u32[]{:S(2)}, u32[]{:S(2)}) collective-permute-start(bf16[128,2048]{1,0:T(8,128)(2,1)S(1)} %copy-done.16), channel_id=1, source_target_pairs={{0,2},{1,3},{2,4},{3,5},{4,6},{5,7},{6,0},{7,1},{8,10},{9,11},{10,... | collective-permute-start | bytes 1572872 | tf_op jit(solution)/shard_map/ppermute | solution.py:280
  151.2 57.8 %collective-permute-start.22 = (bf16[128,2048]{1,0:T(8,128)(2,1)S(1)}, bf16[128,2048]{1,0:T(8,128)(2,1)S(1)}, u32[]{:S(2)}, u32[]{:S(2)}) collective-permute-start(bf16[128,2048]{1,0:T(8,128)(2,1)S(1)} %copy-done.15), channel_id=1, source_target_pairs={{0,6},{1,7},{2,0},{3,1},{4,2},{5,3},{6,4},{7,5},{8,14},{9,15},{10,... | collective-permute-start | bytes 1572872 | tf_op jit(solution)/shard_map/ppermute | solution.py:280
  210.9 17.0 %all-to-all-start.4 = ((bf16[16,8,2048]{2,1,0:T(8,128)(2,1)}), bf16[16,8,2048]{2,1,0:T(8,128)(2,1)S(1)}, u32[]{:S(2)}, u32[]{:S(2)}) async-start(bf16[16,8,2048]{2,1,0:T(8,128)(2,1)} %bitcast.46), calls=%async_computation.4 | async-start | bytes 1048576 | tf_op jit(solution)/shard_map/all_to_all | solution.py:420
  (23 other events, 105.0 us)

commit v4 on v2

v4 whole, which is shorter than its diff:
```python
import functools

import jax
import jax.numpy as jnp
from jax import lax
from jax.experimental import pallas as pl
from jax.experimental.pallas import tpu as pltpu
from jax.sharding import PartitionSpec as P

SLOTS = 8
SHIFT = 3
BF16 = jnp.bfloat16
F32 = jnp.float32


def iota(shape, dim):
    return lax.broadcasted_iota(jnp.int32, shape, dim)


def indicator(mask):
    return jnp.where(mask, 1.0, 0.0).astype(F32)


def dot(left, right):
    return jnp.dot(left, right, preferred_element_type=F32)


def ranks_of(named):
    tokens = named.shape[1]
    earlier = indicator(iota((tokens, tokens), 0) < iota((tokens, tokens), 1))
    return dot(named.astype(BF16), earlier.astype(BF16))


def spread(values, slots):
    labels = values.shape[0]
    picks = indicator((iota((labels * slots, labels), 0) >> SHIFT) == iota((labels * slots, labels), 1))
    return dot(picks.astype(BF16), values.astype(BF16))


def group_sums(values, groups):
    experts = values.shape[0]
    per_group = experts // groups
    shape = (groups * SLOTS, experts)
    same = indicator((iota(shape, 0) >> SHIFT) == (iota(shape, 1) // per_group))
    return dot(same.astype(BF16), values.astype(BF16))


def marks_of(ids_ref, labels):
    total = indicator(labels == ids_ref[0:1, :])
    for entry in range(1, ids_ref.shape[0]):
        total = total + indicator(labels == ids_ref[entry : entry + 1, :])
    return total


def spill_codes(named, ranks):
    return named * jnp.maximum(ranks - (SLOTS - 1), 0.0)


def pack_kernel(groups, experts, ids_ref, acts_ref, packed_ref, spill_ref):
    tokens, width = acts_ref.shape
    entries = ids_ref.shape[0]
    packed_ref[:, :width] = acts_ref[...]
    ids = ids_ref[...].astype(F32)
    filler = jnp.zeros((tokens - entries, tokens), F32)
    packed_ref[:, width:] = jnp.concatenate([ids, filler], axis=0).astype(BF16)
    named = marks_of(ids_ref, iota((experts, tokens), 0))
    codes = group_sums(spill_codes(named, ranks_of(named)), groups)
    slot = (iota(codes.shape, 0) & (SLOTS - 1)).astype(F32)
    spill_ref[...] = dot(indicator(codes == slot + 1.0).astype(BF16), acts_ref[...]).astype(BF16)


def weight_kernel(groups, experts, ids_ref, gates_ref, main_ref, spill_ref):
    tokens = ids_ref.shape[1]
    labels = iota((experts, tokens), 0)
    named = marks_of(ids_ref, labels)
    gates = jnp.zeros((experts, tokens), F32)
    for entry in range(ids_ref.shape[0]):
        value = gates_ref[entry : entry + 1, :].astype(F32)
        gates = gates + jnp.where(labels == ids_ref[entry : entry + 1, :], value, 0.0)
    ranks = ranks_of(named)
    rank_rows = spread(jnp.where(named > 0.0, ranks, 99.0), SLOTS)
    gate_rows = spread(gates, SLOTS)
    slot = (iota(rank_rows.shape, 0) & (SLOTS - 1)).astype(F32)
    main_ref[...] = jnp.where(rank_rows == slot, gate_rows, 0.0).astype(BF16)
    codes = spill_codes(named, ranks)
    code_rows = group_sums(codes, groups)
    spill_rows = group_sums(jnp.where(codes > 0.0, gates, 0.0), groups)
    spill_slot = (iota(code_rows.shape, 0) & (SLOTS - 1)).astype(F32)
    spill_ref[...] = jnp.where(code_rows == spill_slot + 1.0, spill_rows, 0.0).astype(BF16)


def picks_for(ids, groups, per_group, mine):
    named = marks_of(ids, iota((groups, ids.shape[1]), 0) * per_group + mine)
    rank_rows = spread(jnp.where(named > 0.0, ranks_of(named), 99.0), SLOTS)
    slot = (iota(rank_rows.shape, 0) & (SLOTS - 1)).astype(F32)
    return indicator(rank_rows == slot).astype(BF16)


def gather_kernel(groups, per_group, my_ref, ids_ref, acts_ref, out_ref, picks):
    sources, _, tokens = picks.shape

    @pl.when(pl.program_id(0) == 0)
    def _():
        for source in range(sources):
            ids = ids_ref[source * tokens : source * tokens + 16].astype(F32)[0:8].astype(jnp.int32)
            picks[source] = picks_for(ids, groups, per_group, my_ref[0])

    for source in range(sources):
        rows = dot(picks[source], acts_ref[source * tokens : (source + 1) * tokens])
        out_ref[:, source] = rows.reshape(groups, SLOTS, rows.shape[1]).astype(BF16)


CHUNKS = 4


def expert_loads(sources, weights, sems):
    loads = []
    for place, (source, weight) in enumerate(zip(sources, weights)):
        rows = weight.shape[0] // CHUNKS
        loads.append(
            [
                pltpu.make_async_copy(
                    source.at[0, pl.ds(part * rows, rows)], weight.at[pl.ds(part * rows, rows)], sems.at[place, part]
                )
                for part in range(CHUNKS)
            ]
        )
    return loads


def wait_all(copies):
    for copy in copies:
        copy.wait()


def expert_rows(blocks, weights, loads):
    gate_w, up_w, down_w = weights
    if loads:
        wait_all(loads[0])
    gates = [dot(rows(), gate_w[...]) for rows in blocks]
    if loads:
        wait_all(loads[1])
    ups = [dot(rows(), up_w[...]) for rows in blocks]
    hidden = [(g / (1.0 + jnp.exp(-g)) * u).astype(BF16) for g, u in zip(gates, ups)]
    if loads:
        wait_all(loads[2])
    return [dot(rows, down_w[...]).astype(BF16) for rows in hidden]


def main_kernel(first, rows_hbm, gate_hbm, up_hbm, down_hbm, *refs):
    out_hbm, held, done, gate_w, up_w, down_w, row_sems, sems, out_sems = refs[-9:]
    chips, groups, slots, width = held.shape
    weights = (gate_w, up_w, down_w)
    loads = expert_loads((gate_hbm, up_hbm, down_hbm), weights, sems)
    rows = [
        pltpu.make_async_copy(rows_hbm.at[:, pl.ds(chip * slots, slots)], held.at[chip], row_sems.at[chip])
        for chip in range(chips)
    ]
    for copy in rows + loads[0] + loads[1] + loads[2]:
        copy.start()
    wait_all(rows)
    blocks = [lambda chip=chip: held[chip].reshape(groups * slots, width) for chip in range(chips)]
    results = expert_rows(blocks, weights, loads)
    stores = [
        pltpu.make_async_copy(done.at[chip], out_hbm.at[:, first + chip], out_sems.at[chip]) for chip in range(chips)
    ]
    for chip in range(chips):
        done[chip] = results[chip].reshape(groups, slots, width)
        stores[chip].start()
    wait_all(stores)


def spill_kernel(on_ref, rows_hbm, gate_hbm, up_hbm, down_hbm, *refs):
    out_hbm, held, done, gate_w, up_w, down_w, row_sems, sems, out_sems = refs[-9:]
    blocks, count, _ = held.shape
    weights = (gate_w, up_w, down_w)
    loads = expert_loads((gate_hbm, up_hbm, down_hbm), weights, sems)
    rows = [
        pltpu.make_async_copy(rows_hbm.at[pl.ds(block * count, count)], held.at[block], row_sems.at[block])
        for block in range(blocks)
    ]
    stores = [
        pltpu.make_async_copy(done.at[block], out_hbm.at[pl.ds(block * count, count)], out_sems.at[block])
        for block in range(blocks)
    ]

    @pl.when(on_ref[0] != 0)
    def _():
        for copy in rows + loads[0] + loads[1] + loads[2]:
            copy.start()
        wait_all(rows)
        for pair in range(0, blocks, 2):
            both = [lambda block=block: held[block] for block in (pair, pair + 1)]
            results = expert_rows(both, weights, loads if pair == 0 else None)
            for block, result in zip((pair, pair + 1), results):
                done[block] = result
                stores[block].start()

    @pl.when(on_ref[0] == 0)
    def _():
        done[...] = jnp.zeros(done.shape, BF16)
        for store in stores:
            store.start()

    wait_all(stores)


def combine_kernel(main_w_ref, spill_w_ref, main_ref, spill_ref, out_ref):
    over_rows = (((0,), (0,)), ((), ()))
    total = lax.dot_general(main_w_ref[...], main_ref[...], over_rows, preferred_element_type=F32)
    total += lax.dot_general(spill_w_ref[...], spill_ref[...], over_rows, preferred_element_type=F32)
    out_ref[...] = total.astype(BF16)


def params(megabytes=48):
    return pltpu.CompilerParams(vmem_limit_bytes=megabytes * 1024 * 1024)


def whole():
    return pl.BlockSpec(memory_space=pltpu.VMEM)


def scalar():
    return pl.BlockSpec(memory_space=pltpu.SMEM)


def hbm():
    return pl.BlockSpec(memory_space=pltpu.HBM)


def anywhere():
    return pl.BlockSpec(memory_space=pl.ANY)


def expert_cost(count, width, hidden):
    return pl.CostEstimate(
        flops=6 * count * width * hidden,
        bytes_accessed=4 * count * width + 6 * width * hidden,
        transcendentals=count * hidden,
    )


def order_kernel(value_ref, *refs):
    pass


def after(value, *earlier):
    return pl.pallas_call(
        order_kernel,
        in_specs=[hbm()] + [anywhere()] * len(earlier),
        out_specs=hbm(),
        out_shape=jax.ShapeDtypeStruct(value.shape, value.dtype),
        input_output_aliases={0: 0},
        compiler_params=params(60),
        name="order",
    )(value, *earlier)


def shards(activations, expert_ids, route_gates, gate_proj, up_proj, down_proj):
    tokens, width = activations.shape
    hidden = gate_proj.shape[2]
    groups = lax.axis_size("node")
    per_group = lax.axis_size("local")
    experts = groups * per_group
    chips = per_group // 2
    my_node = lax.axis_index("node").astype(jnp.int32)
    my_local = lax.axis_index("local").astype(jnp.int32)
    my_expert = my_node * per_group + my_local
    id_rows = expert_ids.T
    gate_rows = route_gates.T

    packed, spill = pl.pallas_call(
        functools.partial(pack_kernel, groups, experts),
        in_specs=[whole(), whole()],
        out_specs=[whole(), whole()],
        out_shape=[
            jax.ShapeDtypeStruct((tokens, width + tokens), BF16),
            jax.ShapeDtypeStruct((groups * SLOTS, width), BF16),
        ],
        compiler_params=params(60),
        name="pack_rows",
    )(id_rows, activations)
    packed_all = lax.all_gather(packed, "local", tiled=True)
    spill_in = lax.all_to_all(spill.reshape(groups, SLOTS, width), "node", split_axis=0, concat_axis=0, tiled=True)
    spill_in = after(spill_in.reshape(groups * SLOTS, width), packed_all)
    spill_all = lax.all_gather(spill_in, "local", tiled=True)

    columns = min(1024, width)

    def pick(part, sources):
        return pl.pallas_call(
            functools.partial(gather_kernel, groups, per_group),
            grid=(width // columns,),
            in_specs=[
                scalar(),
                pl.BlockSpec((sources * tokens, tokens), lambda i: (part, width // tokens)),
                pl.BlockSpec((sources * tokens, columns), lambda i: (part, i)),
            ],
            out_specs=pl.BlockSpec((groups, sources, SLOTS, columns), lambda i: (0, 0, 0, i)),
            out_shape=jax.ShapeDtypeStruct((groups, sources, SLOTS, width), BF16),
            scratch_shapes=[pltpu.VMEM((sources, groups * SLOTS, tokens), BF16)],
            compiler_params=params(60),
            name="main_rows",
        )(my_local.reshape(1), packed_all, packed_all)

    def send(rows):
        sent = rows.reshape(groups, rows.shape[1] * SLOTS, width)
        return lax.all_to_all(sent, "node", split_axis=0, concat_axis=0, tiled=True)

    late_chips = 1
    early_chips = chips - late_chips
    early_in = send(pick(0, 2 * early_chips))
    late_rows = pick(early_chips // late_chips, 2 * late_chips)

    weight_space = [
        pltpu.VMEM((width, hidden), BF16),
        pltpu.VMEM((width, hidden), BF16),
        pltpu.VMEM((hidden, width), BF16),
    ]
    busiest = (jnp.sum((expert_ids == my_expert).astype(jnp.int32)) > SLOTS).astype(jnp.int32).reshape(1)
    spill_rows = groups * SLOTS * per_group
    spill_out = pl.pallas_call(
        spill_kernel,
        in_specs=[scalar()] + [anywhere()] * 4,
        out_specs=hbm(),
        out_shape=jax.ShapeDtypeStruct((spill_rows, width), BF16),
        scratch_shapes=[pltpu.VMEM((4, spill_rows // 4, width), BF16)] * 2
        + weight_space
        + [pltpu.SemaphoreType.DMA((4,)), pltpu.SemaphoreType.DMA((3, CHUNKS)), pltpu.SemaphoreType.DMA((4,))],
        compiler_params=params(60),
        cost_estimate=expert_cost(spill_rows, width, hidden),
        name="spill_expert",
    )(busiest, spill_all, gate_proj, up_proj, down_proj)
    spill_out = after(spill_out, early_in)
    late_in = send(after(late_rows, early_in, spill_out))
    spill_back = lax.psum_scatter(spill_out, "local", tiled=True)

    def main_expert(arrival, first, count, *main_out):
        return pl.pallas_call(
            functools.partial(main_kernel, first),
            in_specs=[anywhere()] * (4 + len(main_out)),
            out_specs=hbm(),
            out_shape=jax.ShapeDtypeStruct((groups, chips, 2 * SLOTS, width), BF16),
            scratch_shapes=[pltpu.VMEM((count, groups, 2 * SLOTS, width), BF16)] * 2
            + weight_space
            + [pltpu.SemaphoreType.DMA((count,)), pltpu.SemaphoreType.DMA((3, CHUNKS)), pltpu.SemaphoreType.DMA((count,))],
            input_output_aliases={4: 0} if main_out else {},
            compiler_params=params(60),
            cost_estimate=expert_cost(count * 2 * groups * SLOTS, width, hidden),
            name="main_expert",
        )(arrival, gate_proj, up_proj, down_proj, *main_out)

    main_out = main_expert(late_in, early_chips, late_chips, main_expert(early_in, 0, early_chips))
    main_back = lax.all_to_all(
        main_out.reshape(experts, SLOTS, width), ("node", "local"), split_axis=0, concat_axis=0, tiled=True
    )

    blocks = spill_back.reshape(groups, SLOTS, width)
    rolled = lax.dynamic_slice_in_dim(jnp.concatenate([blocks, blocks], axis=0), my_node, groups, axis=0)
    home = [rolled[0]]
    for hop in range(1, groups):
        home.append(lax.ppermute(rolled[hop], "node", [(i, (i + hop) % groups) for i in range(groups)]))
    spill_home = jnp.concatenate(home, axis=0)

    main_w, spill_w = pl.pallas_call(
        functools.partial(weight_kernel, groups, experts),
        in_specs=[whole(), whole()],
        out_specs=[whole(), whole()],
        out_shape=[
            jax.ShapeDtypeStruct((experts * SLOTS, tokens), BF16),
            jax.ShapeDtypeStruct((groups * SLOTS, tokens), BF16),
        ],
        compiler_params=params(16),
        name="combine_weights",
    )(id_rows, gate_rows)
    senders = (my_node - jnp.arange(groups, dtype=jnp.int32)) % groups
    spill_w = jnp.take(spill_w.reshape(groups, SLOTS, tokens), senders, axis=0).reshape(groups * SLOTS, tokens)

    return pl.pallas_call(
        combine_kernel,
        grid=(width // columns,),
        in_specs=[
            pl.BlockSpec((experts * SLOTS, tokens), lambda i: (0, 0)),
            pl.BlockSpec((groups * SLOTS, tokens), lambda i: (0, 0)),
            pl.BlockSpec((experts * SLOTS, columns), lambda i: (0, i)),
            pl.BlockSpec((groups * SLOTS, columns), lambda i: (0, i)),
        ],
        out_specs=pl.BlockSpec((tokens, columns), lambda i: (0, i)),
        out_shape=jax.ShapeDtypeStruct((tokens, width), BF16),
        compiler_params=params(60),
        name="combine",
    )(main_w, spill_w, main_back.reshape(experts * SLOTS, width), spill_home)


def solution(mesh):
    rows = P(("node", "local"), None)
    stacks = P(("node", "local"), None, None)
    return jax.shard_map(
        shards, mesh=mesh, in_specs=(rows, rows, rows, stacks, stacks, stacks), out_specs=rows, check_vma=False
    )
```

time: 227 us -> 277 us (1.22)
  waiting for transfers between devices: 93.5 us -> 154 us
  starting transfers between devices: 69.6 us -> 40.5 us
  blocking collectives: 0 us -> 17.8 us
  between operations: 0.96 us -> 14 us
  local copies, waits for them, and re-layouts: 14.7 us -> 5.49 us
    all_gather x0 -> x2, waiting for transfers between devices: none -> 38.1 us  [the longest x1 20.2 us: shards(): spill_all = lax.all_gather(spill_in, 'local', tiled=True)]
    ppermute x23 -> x15, waiting for transfers between devices: 77.7 us -> 97.9 us  [shards(): lax.ppermute(rolled[hop], 'node', [(i, (i + hop) % groups) for i in range...]
    all_to_all x5 -> x2, starting transfers between devices: 36.8 us -> 18.5 us  [send(): return lax.all_to_all(sent, 'node', split_axis=0, concat_axis=0, tiled=True)]
    all_to_all x0 -> x1, blocking collectives: none -> 17.8 us  [shards(): lax.all_to_all(spill.reshape(groups, SLOTS, width), 'node', split_axis=0,...]
    ppermute x23 -> x15, starting transfers between devices: 25.5 us -> 13.9 us  [shards(): lax.ppermute(rolled[hop], 'node', [(i, (i + hop) % groups) for i in range...]
    unnamed x36 -> x27, local copies, waits for them, and re-layouts: 12 us -> 4.7 us
    add x3 -> x0, other arithmetic: 3.32 us -> none  [the longest x1 2.39 us: back_home(): total = same + swap_cores(other)]
    pallas_call x12 -> x8, Pallas kernels: 35.2 us -> 32.8 us  [the longest x2 22.8 us: main_expert(): pl.pallas_call(functools.partial(main_kernel, first), in_specs=[anywhere(...]
  transfers between devices with their start and end apart: 29 -> 21, of which waited for: 11 -> 14; matrix products, arithmetic and copies ran while one was open for 3% -> 1% of each run, Pallas kernels for 16% -> 12%
where the time goes in v4:
time: 277 us; the launch traced here: 274 us
  waiting for transfers between devices  154 us (56%)
  starting transfers between devices  40.5 us (15%)
  Pallas kernels  39.5 us (14%)
  blocking collectives  17.8 us (6%)
  between operations  14 us (5%)
  local copies, waits for them, and re-layouts  5.49 us (2%)
    ppermute x15, waiting for transfers between devices, shards(): lax.ppermute(rolled[hop], 'node', [(i, (i + hop) % groups) for i in range...  97.9 us
    pallas_call x2, Pallas kernels, main_expert(): pl.pallas_call(functools.partial(main_kernel, first), in_specs=[anywhere(...  22.8 us
    all_gather x1, waiting for transfers between devices, shards(): spill_all = lax.all_gather(spill_in, 'local', tiled=True)  20.2 us
    all_to_all x2, starting transfers between devices, send(): return lax.all_to_all(sent, 'node', split_axis=0, concat_axis=0, tiled=True)  18.5 us
    all_to_all x2, waiting for transfers between devices, send(): return lax.all_to_all(sent, 'node', split_axis=0, concat_axis=0, tiled=True)  18.1 us
    all_gather x1, waiting for transfers between devices, shards(): packed_all = lax.all_gather(packed, 'local', tiled=True)  17.9 us
    all_to_all x1, blocking collectives, shards(): lax.all_to_all(spill.reshape(groups, SLOTS, width), 'node', split_axis=0,...  17.8 us
    ppermute x15, starting transfers between devices, shards(): lax.ppermute(rolled[hop], 'node', [(i, (i + hop) % groups) for i in range...  13.9 us
  transfers between devices with their start and end apart: 21, of which 14 were waited for; matrix products, arithmetic and copies ran while one was open for 1% of the time, Pallas kernels for 12%

profile of v4, /device:TPU:2, one launch (start us, length us, event | category | flops | bytes accessed | tf_op | source)
XLA Modules:
  0.0 274.0 jit_solution(17525656538710033)
XLA Ops:
  9.2 17.8 %all_to_all.20 = bf16[16,8,2048]{2,1,0:T(8,128)(2,1)} all-to-all(bf16[16,8,2048]{2,1,0:T(8,128)(2,1)} %bitcast.58), channel_id=1, replica_groups=mesh['node'=16,'local'=8] {'node'}, dimensions={0} | all-to-all | bytes 1048576 | tf_op jit(solution)/shard_map/all_to_all | solution.py:284
  26.9 17.9 %all-gather.3.cloned.1.call-done.ids_ref.acts_ref.refs_0_ = bf16[1024,2176]{1,0:T(8,128)(2,1)} async-done(((bf16[128,2176]{1,0:T(8,128)(2,1)}), bf16[1024,2176]{1,0:T(8,128)(2,1)}) %all-gather.3.cloned.1.call-update) | async-done | bytes 4456464 | tf_op jit(solution)/shard_map/all_gather | solution.py:283
  44.9 4.7 %main_rows.3 = bf16[16,6,8,2048]{3,2,1,0:T(8,128)(2,1)} custom-call(s32[1]{0:T(128)} %bitcast.5.my_ref, bf16[1024,2176]{1,0:T(8,128)(2,1)} %all-gather.3.cloned.1.call-done.ids_ref.acts_ref.refs_0_, bf16[1024,2176]{1,0:T(8,128)(2,1)} %all-gather.3.cloned.1.call-done.ids_ref.acts_ref.refs_0_), custom_call_target="tpu_custom_call" | custom-call | tf_op jit(solution)/shard_map/main_rows/pallas_call | solution.py:291
  49.6 7.5 %all-to-all-start = ((bf16[16,48,2048]{2,1,0:T(8,128)(2,1)}), bf16[16,48,2048]{2,1,0:T(8,128)(2,1)S(1)}, u32[]{:S(2)}, u32[]{:S(2)}) async-start(bf16[16,48,2048]{2,1,0:T(8,128)(2,1)} %bitcast.55), calls=%async_computation | async-start | bytes 6291456 | tf_op jit(solution)/shard_map/all_to_all | solution.py:308
  58.5 20.2 %all-gather.5.cloned.1.call-done.rows_hbm = bf16[1024,2048]{1,0:T(8,128)(2,1)} async-done(((bf16[128,2048]{1,0:T(8,128)(2,1)}), bf16[1024,2048]{1,0:T(8,128)(2,1)}) %all-gather.5.cloned.1.call-update) | async-done | bytes 4194320 | tf_op jit(solution)/shard_map/all_gather | solution.py:286
  81.1 18.1 %all-to-all-done.refs_0_.rows_hbm = bf16[16,48,2048]{2,1,0:T(8,128)(2,1)S(1)} async-done(((bf16[16,48,2048]{2,1,0:T(8,128)(2,1)}), bf16[16,48,2048]{2,1,0:T(8,128)(2,1)S(1)}, u32[]{:S(2)}, u32[]{:S(2)}) %all-to-all-start) | async-done | bytes 3145760 | tf_op jit(solution)/shard_map/all_to_all | solution.py:308
  102.8 2.9 %main_rows.2.value_ref = bf16[16,2,8,2048]{3,2,1,0:T(8,128)(2,1)} custom-call(s32[1]{0:T(128)} %bitcast.5.my_ref, bf16[1024,2176]{1,0:T(8,128)(2,1)} %all-gather.3.cloned.1.call-done.ids_ref.acts_ref.refs_0_, bf16[1024,2176]{1,0:T(8,128)(2,1)} %all-gather.3.cloned.1.call-done.ids_ref.acts_ref.refs_0_), custom_call_target="tpu_custom_call" | custom-call | tf_op jit(solution)/shard_map/main_rows/pallas_call | solution.py:291
  105.7 11.0 %all-to-all-start.2 = ((bf16[16,16,2048]{2,1,0:T(8,128)(2,1)}), bf16[16,16,2048]{2,1,0:T(8,128)(2,1)S(1)}, u32[]{:S(2)}, u32[]{:S(2)}) async-start(bf16[16,16,2048]{2,1,0:T(8,128)(2,1)} %bitcast.56), calls=%async_computation.2 | async-start | bytes 2097152 | tf_op jit(solution)/shard_map/all_to_all | solution.py:308
  118.0 14.2 %main_expert.2.refs_0_ = bf16[16,4,16,2048]{3,2,1,0:T(8,128)(2,1)} custom-call(bf16[16,48,2048]{2,1,0:T(8,128)(2,1)} %copy-done.3, bf16[1,2048,768]{2,1,0:T(8,128)(2,1)} %gate_hbm.5, bf16[1,2048,768]{2,1,0:T(8,128)(2,1)} %up_hbm.5, bf16[1,768,2048]{2,1,0:T(8,128)(2,1)} %down_hbm.5), custom_call_target="tpu_custom_call" | custom-call | flops 7247757312 | bytes 15728640 | tf_op jit(solution)/shard_map/main_expert/pallas_call | solution.py:339
  133.2 8.6 %main_expert.3 = bf16[16,4,16,2048]{3,2,1,0:T(8,128)(2,1)} custom-call(bf16[16,16,2048]{2,1,0:T(8,128)(2,1)} %copy-done.4, bf16[1,2048,768]{2,1,0:T(8,128)(2,1)} %gate_hbm.5, bf16[1,2048,768]{2,1,0:T(8,128)(2,1)} %up_hbm.5, bf16[1,768,2048]{2,1,0:T(8,128)(2,1)} %down_hbm.5, bf16[16,4,16,2048]{3,2,1,0:T(8,128)(2,1)} %main_expert.2.refs_0_), custom_call_target="tpu_custom_call", output_to_operand_aliasing={{}: (4, {})} | custom-call | flops 2415919104 | bytes 11534336 | tf_op jit(solution)/shard_map/main_expert/pallas_call | solution.py:339
  141.8 8.0 %all-to-all-start.3 = ((bf16[128,8,2048]{2,1,0:T(8,128)(2,1)}), bf16[128,8,2048]{2,1,0:T(8,128)(2,1)}, u32[]{:S(2)}, u32[]{:S(2)}) async-start(bf16[128,8,2048]{2,1,0:T(8,128)(2,1)} %bitcast.54), calls=%async_computation.3 | async-start | bytes 8388608 | tf_op jit(solution)/shard_map/all_to_all | solution.py:354
  156.6 3.0 %collective-permute-start.12 = (bf16[8,2048]{1,0:T(8,128)(2,1)S(1)}, bf16[8,2048]{1,0:T(8,128)(2,1)S(1)}, u32[]{:S(2)}, u32[]{:S(2)}) collective-permute-start(bf16[8,2048]{1,0:T(8,128)(2,1)S(1)} %get-tuple-element.15), channel_id=1, source_target_pairs={{0,104},{8,112},{16,120},{24,0},{32,8},{40,16},{48,24},{56,32},{64... | collective-permute-start | bytes 98312 | tf_op jit(solution)/shard_map/ppermute | solution.py:362
  160.4 39.5 %collective-permute-done = bf16[8,2048]{1,0:T(8,128)(2,1)S(1)} collective-permute-done((bf16[8,2048]{1,0:T(8,128)(2,1)S(1)}, bf16[8,2048]{1,0:T(8,128)(2,1)S(1)}, u32[]{:S(2)}, u32[]{:S(2)}) %collective-permute-start) | collective-permute-done | bytes 32800 | tf_op jit(solution)/shard_map/ppermute | solution.py:362
  199.9 6.3 %collective-permute-done.1 = bf16[8,2048]{1,0:T(8,128)(2,1)S(1)} collective-permute-done((bf16[8,2048]{1,0:T(8,128)(2,1)S(1)}, bf16[8,2048]{1,0:T(8,128)(2,1)S(1)}, u32[]{:S(2)}, u32[]{:S(2)}) %collective-permute-start.1) | collective-permute-done | bytes 32800 | tf_op jit(solution)/shard_map/ppermute | solution.py:362
  206.2 4.8 %collective-permute-done.2 = bf16[8,2048]{1,0:T(8,128)(2,1)S(1)} collective-permute-done((bf16[8,2048]{1,0:T(8,128)(2,1)S(1)}, bf16[8,2048]{1,0:T(8,128)(2,1)S(1)}, u32[]{:S(2)}, u32[]{:S(2)}) %collective-permute-start.2) | collective-permute-done | bytes 32800 | tf_op jit(solution)/shard_map/ppermute | solution.py:362
  211.9 6.2 %collective-permute-done.3 = bf16[8,2048]{1,0:T(8,128)(2,1)S(1)} collective-permute-done((bf16[8,2048]{1,0:T(8,128)(2,1)S(1)}, bf16[8,2048]{1,0:T(8,128)(2,1)S(1)}, u32[]{:S(2)}, u32[]{:S(2)}) %collective-permute-start.3) | collective-permute-done | bytes 32800 | tf_op jit(solution)/shard_map/ppermute | solution.py:362
  218.1 7.8 %collective-permute-done.4 = bf16[8,2048]{1,0:T(8,128)(2,1)S(1)} collective-permute-done((bf16[8,2048]{1,0:T(8,128)(2,1)S(1)}, bf16[8,2048]{1,0:T(8,128)(2,1)S(1)}, u32[]{:S(2)}, u32[]{:S(2)}) %collective-permute-start.4) | collective-permute-done | bytes 32800 | tf_op jit(solution)/shard_map/ppermute | solution.py:362
  225.8 7.8 %collective-permute-done.5 = bf16[8,2048]{1,0:T(8,128)(2,1)S(1)} collective-permute-done((bf16[8,2048]{1,0:T(8,128)(2,1)S(1)}, bf16[8,2048]{1,0:T(8,128)(2,1)S(1)}, u32[]{:S(2)}, u32[]{:S(2)}) %collective-permute-start.5) | collective-permute-done | bytes 32800 | tf_op jit(solution)/shard_map/ppermute | solution.py:362
  233.7 6.6 %collective-permute-done.6 = bf16[8,2048]{1,0:T(8,128)(2,1)S(1)} collective-permute-done((bf16[8,2048]{1,0:T(8,128)(2,1)S(1)}, bf16[8,2048]{1,0:T(8,128)(2,1)S(1)}, u32[]{:S(2)}, u32[]{:S(2)}) %collective-permute-start.6) | collective-permute-done | bytes 32800 | tf_op jit(solution)/shard_map/ppermute | solution.py:362
  241.3 4.4 %collective-permute-done.7 = bf16[8,2048]{1,0:T(8,128)(2,1)S(1)} collective-permute-done((bf16[8,2048]{1,0:T(8,128)(2,1)S(1)}, bf16[8,2048]{1,0:T(8,128)(2,1)S(1)}, u32[]{:S(2)}, u32[]{:S(2)}) %collective-permute-start.7) | collective-permute-done | bytes 32800 | tf_op jit(solution)/shard_map/ppermute | solution.py:362
  245.8 6.0 %collective-permute-done.8 = bf16[8,2048]{1,0:T(8,128)(2,1)S(1)} collective-permute-done((bf16[8,2048]{1,0:T(8,128)(2,1)S(1)}, bf16[8,2048]{1,0:T(8,128)(2,1)S(1)}, u32[]{:S(2)}, u32[]{:S(2)}) %collective-permute-start.8) | collective-permute-done | bytes 32800 | tf_op jit(solution)/shard_map/ppermute | solution.py:362
  252.2 5.9 %collective-permute-done.9 = bf16[8,2048]{1,0:T(8,128)(2,1)S(1)} collective-permute-done((bf16[8,2048]{1,0:T(8,128)(2,1)S(1)}, bf16[8,2048]{1,0:T(8,128)(2,1)S(1)}, u32[]{:S(2)}, u32[]{:S(2)}) %collective-permute-start.9) | collective-permute-done | bytes 32800 | tf_op jit(solution)/shard_map/ppermute | solution.py:362
  260.3 2.6 collective-permute-done.10
  263.8 3.6 %combine.1 = bf16[128,2048]{1,0:T(8,128)(2,1)} custom-call(bf16[1024,128]{1,0:T(8,128)(2,1)} %copy-done, bf16[128,128]{1,0:T(8,128)(2,1)} %bitcast_select_fusion.spill_w_ref, bf16[1024,2048]{1,0:T(8,128)(2,1)} %bitcast.12.main_ref, bf16[128,2048]{1,0:T(8,128)(2,1)} %copy-done.5), custom_call_target="tpu_custom_call" | custom-call | tf_op jit(solution)/shard_map/combine/pallas_call | solution.py:379
  (71 shorter events, 24.6 us)
Async XLA Ops:
  6.5 38.3 %all-gather.3.cloned.1.call-start = ((), (), s32[]{:S(2)}) async-start(), calls=%async_computation.5 | async-start | bytes 5013504 | tf_op jit(solution)/shard_map/all_gather | solution.py:283
  9.1 69.6 %all-gather.5.cloned.1.call-start = ((), (), s32[]{:S(2)}) async-start(), calls=%async_computation.6 | async-start | bytes 4718592 | tf_op jit(solution)/shard_map/all_gather | solution.py:286
  49.6 7.6 %copy-start.1 = (s32[128,8]{0,1:T(8,128)S(1)}, s32[128,8]{0,1:T(8,128)}, u32[]{:S(2)}) copy-start(s32[128,8]{0,1:T(8,128)} %param.7) | copy-start | bytes 12292
  49.6 49.6 %all-to-all-start = ((bf16[16,48,2048]{2,1,0:T(8,128)(2,1)}), bf16[16,48,2048]{2,1,0:T(8,128)(2,1)S(1)}, u32[]{:S(2)}, u32[]{:S(2)}) async-start(bf16[16,48,2048]{2,1,0:T(8,128)(2,1)} %bitcast.55), calls=%async_computation | async-start | bytes 6291456 | tf_op jit(solution)/shard_map/all_to_all | solution.py:308
  57.1 92.7 %reduce-scatter.2.cloned.1.call-start = ((), (), s32[]{:S(2)}) async-start(), calls=%async_computation.7 | async-start | bytes 4718592 | tf_op jit(solution)/shard_map/reduce_scatter | solution.py:336
  99.2 1.7 copy-start.3
  105.7 26.5 %all-to-all-start.2 = ((bf16[16,16,2048]{2,1,0:T(8,128)(2,1)}), bf16[16,16,2048]{2,1,0:T(8,128)(2,1)S(1)}, u32[]{:S(2)}, u32[]{:S(2)}) async-start(bf16[16,16,2048]{2,1,0:T(8,128)(2,1)} %bitcast.56), calls=%async_computation.2 | async-start | bytes 2097152 | tf_op jit(solution)/shard_map/all_to_all | solution.py:308
  132.2 1.0 copy-start.4
  141.8 121.2 %all-to-all-start.3 = ((bf16[128,8,2048]{2,1,0:T(8,128)(2,1)}), bf16[128,8,2048]{2,1,0:T(8,128)(2,1)}, u32[]{:S(2)}, u32[]{:S(2)}) async-start(bf16[128,8,2048]{2,1,0:T(8,128)(2,1)} %bitcast.54), calls=%async_computation.3 | async-start | bytes 8388608 | tf_op jit(solution)/shard_map/all_to_all | solution.py:354
  151.1 48.8 %collective-permute-start = (bf16[8,2048]{1,0:T(8,128)(2,1)S(1)}, bf16[8,2048]{1,0:T(8,128)(2,1)S(1)}, u32[]{:S(2)}, u32[]{:S(2)}) collective-permute-start(bf16[8,2048]{1,0:T(8,128)(2,1)S(1)} %get-tuple-element.27), channel_id=1, source_target_pairs={{0,8},{8,16},{16,24},{24,32},{32,40},{40,48},{48,56},{56,64},{64,7... | collective-permute-start | bytes 98312 | tf_op jit(solution)/shard_map/ppermute | solution.py:362
  152.8 110.2 %collective-permute-start.14 = (bf16[8,2048]{1,0:T(8,128)(2,1)S(1)}, bf16[8,2048]{1,0:T(8,128)(2,1)S(1)}, u32[]{:S(2)}, u32[]{:S(2)}) collective-permute-start(bf16[8,2048]{1,0:T(8,128)(2,1)S(1)} %get-tuple-element.13), channel_id=1, source_target_pairs={{0,120},{8,0},{16,8},{24,16},{32,24},{40,32},{48,40},{56,48},{64,5... | collective-permute-start | bytes 98312 | tf_op jit(solution)/shard_map/ppermute | solution.py:362
  155.3 107.6 %collective-permute-start.13 = (bf16[8,2048]{1,0:T(8,128)(2,1)S(1)}, bf16[8,2048]{1,0:T(8,128)(2,1)S(1)}, u32[]{:S(2)}, u32[]{:S(2)}) collective-permute-start(bf16[8,2048]{1,0:T(8,128)(2,1)S(1)} %get-tuple-element.14), channel_id=1, source_target_pairs={{0,112},{8,120},{16,0},{24,8},{32,16},{40,24},{48,32},{56,40},{64,... | collective-permute-start | bytes 98312 | tf_op jit(solution)/shard_map/ppermute | solution.py:362
  156.6 106.4 %collective-permute-start.12 = (bf16[8,2048]{1,0:T(8,128)(2,1)S(1)}, bf16[8,2048]{1,0:T(8,128)(2,1)S(1)}, u32[]{:S(2)}, u32[]{:S(2)}) collective-permute-start(bf16[8,2048]{1,0:T(8,128)(2,1)S(1)} %get-tuple-element.15), channel_id=1, source_target_pairs={{0,104},{8,112},{16,120},{24,0},{32,8},{40,16},{48,24},{56,32},{64... | collective-permute-start | bytes 98312 | tf_op jit(solution)/shard_map/ppermute | solution.py:362
  159.6 103.3 %collective-permute-start.11 = (bf16[8,2048]{1,0:T(8,128)(2,1)S(1)}, bf16[8,2048]{1,0:T(8,128)(2,1)S(1)}, u32[]{:S(2)}, u32[]{:S(2)}) collective-permute-start(bf16[8,2048]{1,0:T(8,128)(2,1)S(1)} %get-tuple-element.16), channel_id=1, source_target_pairs={{0,96},{8,104},{16,112},{24,120},{32,0},{40,8},{48,16},{56,24},{64... | collective-permute-start | bytes 98312 | tf_op jit(solution)/shard_map/ppermute | solution.py:362
  199.9 6.3 %collective-permute-start.1 = (bf16[8,2048]{1,0:T(8,128)(2,1)S(1)}, bf16[8,2048]{1,0:T(8,128)(2,1)S(1)}, u32[]{:S(2)}, u32[]{:S(2)}) collective-permute-start(bf16[8,2048]{1,0:T(8,128)(2,1)S(1)} %get-tuple-element.26), channel_id=1, source_target_pairs={{0,16},{8,24},{16,32},{24,40},{32,48},{40,56},{48,64},{56,72},{64,... | collective-permute-start | bytes 98312 | tf_op jit(solution)/shard_map/ppermute | solution.py:362
  206.2 4.8 %collective-permute-start.2 = (bf16[8,2048]{1,0:T(8,128)(2,1)S(1)}, bf16[8,2048]{1,0:T(8,128)(2,1)S(1)}, u32[]{:S(2)}, u32[]{:S(2)}) collective-permute-start(bf16[8,2048]{1,0:T(8,128)(2,1)S(1)} %get-tuple-element.25), channel_id=1, source_target_pairs={{0,24},{8,32},{16,40},{24,48},{32,56},{40,64},{48,72},{56,80},{64,... | collective-permute-start | bytes 98312 | tf_op jit(solution)/shard_map/ppermute | solution.py:362
  211.0 7.0 %collective-permute-start.3 = (bf16[8,2048]{1,0:T(8,128)(2,1)S(1)}, bf16[8,2048]{1,0:T(8,128)(2,1)S(1)}, u32[]{:S(2)}, u32[]{:S(2)}) collective-permute-start(bf16[8,2048]{1,0:T(8,128)(2,1)S(1)} %get-tuple-element.24), channel_id=1, source_target_pairs={{0,32},{8,40},{16,48},{24,56},{32,64},{40,72},{48,80},{56,88},{64,... | collective-permute-start | bytes 98312 | tf_op jit(solution)/shard_map/ppermute | solution.py:362
  218.1 7.8 %collective-permute-start.4 = (bf16[8,2048]{1,0:T(8,128)(2,1)S(1)}, bf16[8,2048]{1,0:T(8,128)(2,1)S(1)}, u32[]{:S(2)}, u32[]{:S(2)}) collective-permute-start(bf16[8,2048]{1,0:T(8,128)(2,1)S(1)} %get-tuple-element.23), channel_id=1, source_target_pairs={{0,40},{8,48},{16,56},{24,64},{32,72},{40,80},{48,88},{56,96},{64,... | collective-permute-start | bytes 98312 | tf_op jit(solution)/shard_map/ppermute | solution.py:362
  225.8 7.8 %collective-permute-start.5 = (bf16[8,2048]{1,0:T(8,128)(2,1)S(1)}, bf16[8,2048]{1,0:T(8,128)(2,1)S(1)}, u32[]{:S(2)}, u32[]{:S(2)}) collective-permute-start(bf16[8,2048]{1,0:T(8,128)(2,1)S(1)} %get-tuple-element.22), channel_id=1, source_target_pairs={{0,48},{8,56},{16,64},{24,72},{32,80},{40,88},{48,96},{56,104},{64... | collective-permute-start | bytes 98312 | tf_op jit(solution)/shard_map/ppermute | solution.py:362
  233.7 6.6 %collective-permute-start.6 = (bf16[8,2048]{1,0:T(8,128)(2,1)S(1)}, bf16[8,2048]{1,0:T(8,128)(2,1)S(1)}, u32[]{:S(2)}, u32[]{:S(2)}) collective-permute-start(bf16[8,2048]{1,0:T(8,128)(2,1)S(1)} %get-tuple-element.21), channel_id=1, source_target_pairs={{0,56},{8,64},{16,72},{24,80},{32,88},{40,96},{48,104},{56,112},{6... | collective-permute-start | bytes 98312 | tf_op jit(solution)/shard_map/ppermute | solution.py:362
  240.2 5.5 %collective-permute-start.7 = (bf16[8,2048]{1,0:T(8,128)(2,1)S(1)}, bf16[8,2048]{1,0:T(8,128)(2,1)S(1)}, u32[]{:S(2)}, u32[]{:S(2)}) collective-permute-start(bf16[8,2048]{1,0:T(8,128)(2,1)S(1)} %get-tuple-element.20), channel_id=1, source_target_pairs={{0,64},{8,72},{16,80},{24,88},{32,96},{40,104},{48,112},{56,120},{... | collective-permute-start | bytes 98312 | tf_op jit(solution)/shard_map/ppermute | solution.py:362
  245.8 6.0 %collective-permute-start.8 = (bf16[8,2048]{1,0:T(8,128)(2,1)S(1)}, bf16[8,2048]{1,0:T(8,128)(2,1)S(1)}, u32[]{:S(2)}, u32[]{:S(2)}) collective-permute-start(bf16[8,2048]{1,0:T(8,128)(2,1)S(1)} %get-tuple-element.19), channel_id=1, source_target_pairs={{0,72},{8,80},{16,88},{24,96},{32,104},{40,112},{48,120},{56,0},{6... | collective-permute-start | bytes 98312 | tf_op jit(solution)/shard_map/ppermute | solution.py:362
  251.8 6.3 %collective-permute-start.9 = (bf16[8,2048]{1,0:T(8,128)(2,1)S(1)}, bf16[8,2048]{1,0:T(8,128)(2,1)S(1)}, u32[]{:S(2)}, u32[]{:S(2)}) collective-permute-start(bf16[8,2048]{1,0:T(8,128)(2,1)S(1)} %get-tuple-element.18), channel_id=1, source_target_pairs={{0,80},{8,88},{16,96},{24,104},{32,112},{40,120},{48,0},{56,8},{64... | collective-permute-start | bytes 98312 | tf_op jit(solution)/shard_map/ppermute | solution.py:362
  258.1 4.8 %collective-permute-start.10 = (bf16[8,2048]{1,0:T(8,128)(2,1)S(1)}, bf16[8,2048]{1,0:T(8,128)(2,1)S(1)}, u32[]{:S(2)}, u32[]{:S(2)}) collective-permute-start(bf16[8,2048]{1,0:T(8,128)(2,1)S(1)} %get-tuple-element.17), channel_id=1, source_target_pairs={{0,88},{8,96},{16,104},{24,112},{32,120},{40,0},{48,8},{56,16},{64... | collective-permute-start | bytes 98312 | tf_op jit(solution)/shard_map/ppermute | solution.py:362
  (3 other events, 2.2 us)
Sparse Core Ops, SparseCore 0:
  9.2 35.5 all-gather.2
  46.6 32.0 all-gather.4
  101.0 41.5 reduce-scatter.1

commit v5 on v0

v5 whole, which is shorter than its diff:
```python
import functools

import jax
import jax.numpy as jnp
from jax import lax
from jax.experimental import pallas as pl
from jax.experimental.pallas import tpu as pltpu
from jax.sharding import PartitionSpec as P

SLOTS = 8
EXTRA = 4
SHIFT = 3
BF16 = jnp.bfloat16
F32 = jnp.float32


def iota(shape, dim):
    return lax.broadcasted_iota(jnp.int32, shape, dim)


def indicator(mask):
    return jnp.where(mask, 1.0, 0.0).astype(F32)


def dot(left, right):
    return jnp.dot(left, right, preferred_element_type=F32)


def ranks_of(named):
    tokens = named.shape[1]
    earlier = indicator(iota((tokens, tokens), 0) < iota((tokens, tokens), 1))
    return dot(named.astype(BF16), earlier.astype(BF16))


def spread(values, flip):
    labels = values.shape[0]
    owner = (iota((labels * SLOTS, labels), 0) >> SHIFT) ^ flip
    picks = indicator(owner == iota((labels * SLOTS, labels), 1))
    return dot(picks.astype(BF16), values.astype(BF16))


def marks_of(ids_ref, labels):
    total = indicator(labels == ids_ref[0:1, :])
    for entry in range(1, ids_ref.shape[0]):
        total = total + indicator(labels == ids_ref[entry : entry + 1, :])
    return total


def slot_of(shape):
    return (iota(shape, 0) & (SLOTS - 1)).astype(F32)


def extra_of(shape):
    return (iota(shape, 0) & (EXTRA - 1)).astype(F32)


def first_half(shape):
    return (iota(shape, 0) & EXTRA) == 0


def send_kernel(ids_ref, acts_ref, out_ref, ranks):
    tokens, width = acts_ref.shape
    experts = ranks.shape[0]
    block = out_ref.shape[0]
    half = width // 2

    @pl.when(pl.program_id(0) == 0)
    def _():
        named = marks_of(ids_ref, iota((experts, tokens), 0))
        ranks[...] = jnp.where(named > 0.0, ranks_of(named), 99.0)

    mine = ranks[pl.ds(pl.multiple_of(pl.program_id(0) * block, block), block)]
    own = spread(mine, 0)
    other = spread(mine, 1)
    main = indicator(own == slot_of(own.shape)).astype(BF16)
    place = extra_of(own.shape)
    extra = jnp.maximum(indicator(own == place + SLOTS), indicator(other == place + (SLOTS + EXTRA)))
    low = jnp.where(first_half(own.shape), extra, 0.0).astype(BF16)
    high = jnp.where(first_half(own.shape), 0.0, extra).astype(BF16)
    rows = dot(main, acts_ref[...])
    out_ref[:, :, :width] = rows.reshape(block, SLOTS, width).astype(BF16)
    folded = dot(low, acts_ref[:, :half]) + dot(high, acts_ref[:, half:])
    out_ref[:, :, width:] = folded.reshape(block, SLOTS, half).astype(BF16)


def weight_kernel(ids_ref, gates_ref, main_ref, extra_ref):
    tokens = ids_ref.shape[1]
    experts = main_ref.shape[0] // SLOTS
    labels = iota((experts, tokens), 0)
    named = marks_of(ids_ref, labels)
    gates = jnp.zeros((experts, tokens), F32)
    for entry in range(ids_ref.shape[0]):
        value = gates_ref[entry : entry + 1, :].astype(F32)
        gates = gates + jnp.where(labels == ids_ref[entry : entry + 1, :], value, 0.0)
    ranks = jnp.where(named > 0.0, ranks_of(named), 99.0)
    own = spread(ranks, 0)
    own_gates = spread(gates, 0)
    main_ref[...] = jnp.where(own == slot_of(own.shape), own_gates, 0.0).astype(BF16)
    place = extra_of(own.shape)
    extra = jnp.where(own == place + SLOTS, own_gates, 0.0)
    extra += jnp.where(spread(ranks, 1) == place + (SLOTS + EXTRA), spread(gates, 1), 0.0)
    extra_ref[0] = jnp.where(first_half(own.shape), extra, 0.0).astype(BF16)
    extra_ref[1] = jnp.where(first_half(own.shape), 0.0, extra).astype(BF16)


CHUNKS = 4


def expert_loads(sources, weights, sems):
    loads = []
    for place, (source, weight) in enumerate(zip(sources, weights)):
        rows = weight.shape[0] // CHUNKS
        loads.append(
            [
                pltpu.make_async_copy(
                    source.at[0, pl.ds(part * rows, rows)], weight.at[pl.ds(part * rows, rows)], sems.at[place, part]
                )
                for part in range(CHUNKS)
            ]
        )
    return loads


def wait_all(copies):
    for copy in copies:
        copy.wait()


def expert_rows(blocks, weights, loads):
    gate_w, up_w, down_w = weights
    if loads:
        wait_all(loads[0])
    gates = [dot(rows(), gate_w[...]) for rows in blocks]
    if loads:
        wait_all(loads[1])
    ups = [dot(rows(), up_w[...]) for rows in blocks]
    hidden = [(g / (1.0 + jnp.exp(-g)) * u).astype(BF16) for g, u in zip(gates, ups)]
    if loads:
        wait_all(loads[2])
    return [dot(rows, down_w[...]).astype(BF16) for rows in hidden]


def unfold(folded):
    shape = (folded.shape[0] // 2, folded.shape[0])
    row = iota(shape, 0)
    start = (row >> 2) * SLOTS + (row & (EXTRA - 1))
    low = indicator(iota(shape, 1) == start).astype(BF16)
    high = indicator(iota(shape, 1) == start + EXTRA).astype(BF16)
    return jnp.concatenate([dot(low, folded).astype(BF16), dot(high, folded).astype(BF16)], axis=1)


def fold(rows):
    half = rows.shape[1] // 2
    shape = (rows.shape[0] * 2, rows.shape[0])
    source = (iota(shape, 0) >> SHIFT) * EXTRA + (iota(shape, 0) & (EXTRA - 1))
    match = iota(shape, 1) == source
    low = indicator(match & first_half(shape)).astype(BF16)
    high = indicator(match & jnp.logical_not(first_half(shape))).astype(BF16)
    return (dot(low, rows[:, :half]) + dot(high, rows[:, half:])).astype(BF16)


def expert_kernel(mode_ref, rows_hbm, *refs):
    sources = refs[:3], refs[3:6]
    out_hbm, held, done = refs[6:9]
    weights = refs[9:12], refs[12:15]
    row_sems, sems, out_sems = refs[15:]
    blocks, count, slots, full = held.shape
    width = weights[0][0].shape[0]
    half = width // 2
    mode = mode_ref[0]
    loads = [expert_loads(sources[side], weights[side], sems.at[side]) for side in range(2)]
    rows = [
        pltpu.make_async_copy(rows_hbm.at[pl.ds(block * count, count)], held.at[block], row_sems.at[block])
        for block in range(blocks)
    ]
    stores = [
        pltpu.make_async_copy(done.at[block], out_hbm.at[pl.ds(block * count, count)], out_sems.at[block])
        for block in range(blocks)
    ]
    for copy in rows[:2] + loads[0][0] + loads[0][1] + rows[2:] + loads[0][2]:
        copy.start()

    @pl.when(mode == 2)
    def _():
        for copy in loads[1][0] + loads[1][1] + loads[1][2]:
            copy.start()

    for pair in range(0, blocks, 2):
        wait_all(rows[pair : pair + 2])
        both = [lambda b=b: held[b, :, :, :width].reshape(count * slots, width) for b in (pair, pair + 1)]
        results = expert_rows(both, weights[0], loads[0] if pair == 0 else None)
        for block, result in zip((pair, pair + 1), results):
            done[block, :, :, :width] = result.reshape(count, slots, width)

    def extras(side):
        if side:
            wait_all(loads[1][0] + loads[1][1] + loads[1][2])
        parts = [unfold(held[block, :, :, width:].reshape(count * slots, half)) for block in range(blocks)]
        both = [lambda a=a: jnp.concatenate(parts[a : a + 2], axis=0) for a in range(0, blocks, 2)]
        results = expert_rows(both, weights[side], None)
        for block in range(blocks):
            start = (block % 2) * count * EXTRA
            result = results[block // 2][start : start + count * EXTRA]
            done[block, :, :, width:] = fold(result).reshape(count, slots, half)

    for side in range(2):

        @pl.when(mode == side + 1)
        def _():
            extras(side)

    @pl.when(mode == 0)
    def _():
        done[:, :, :, width:] = jnp.zeros((blocks, count, slots, half), BF16)

    for store in stores:
        store.start()
    wait_all(stores)


def combine_kernel(main_w_ref, extra_w_ref, main_ref, extra_ref, out_ref):
    over_rows = (((0,), (0,)), ((), ()))
    total = lax.dot_general(main_w_ref[...], main_ref[...], over_rows, preferred_element_type=F32)
    total += lax.dot_general(extra_w_ref[0], extra_ref[...], over_rows, preferred_element_type=F32)
    out_ref[...] = total.astype(BF16)


def params(megabytes):
    return pltpu.CompilerParams(vmem_limit_bytes=megabytes * 1024 * 1024)


def whole():
    return pl.BlockSpec(memory_space=pltpu.VMEM)


def hbm():
    return pl.BlockSpec(memory_space=pltpu.HBM)


def shards(activations, expert_ids, route_gates, gate_proj, up_proj, down_proj):
    tokens, width = activations.shape
    top = expert_ids.shape[1]
    hidden = gate_proj.shape[2]
    groups = lax.axis_size("node")
    per_group = lax.axis_size("local")
    experts = groups * per_group
    half = width // 2
    full = width + half
    my_expert = (lax.axis_index("node") * per_group + lax.axis_index("local")).astype(jnp.int32)
    id_rows = expert_ids.T
    gate_rows = route_gates.T

    block = experts // 4
    sent = pl.pallas_call(
        send_kernel,
        grid=(experts // block,),
        in_specs=[
            pl.BlockSpec((top, tokens), lambda i: (0, 0)),
            pl.BlockSpec((tokens, width), lambda i: (0, 0)),
        ],
        out_specs=pl.BlockSpec((block, SLOTS, full), lambda i: (i, 0, 0)),
        out_shape=jax.ShapeDtypeStruct((experts, SLOTS, full), BF16),
        scratch_shapes=[pltpu.VMEM((experts, tokens), F32)],
        compiler_params=params(60),
        name="send_rows",
    )(id_rows, activations)

    def exchange(rows):
        return lax.all_to_all(rows, ("node", "local"), split_axis=0, concat_axis=0, tiled=True)

    arrived = exchange(sent)
    cores = [(i, i ^ 1) for i in range(per_group)]
    other = [lax.ppermute(weight, "local", cores) for weight in (gate_proj, up_proj, down_proj)]

    mine = jnp.sum((expert_ids == my_expert).astype(jnp.int32)) > SLOTS
    theirs = jnp.sum((expert_ids == (my_expert ^ 1)).astype(jnp.int32)) > SLOTS
    mode = jnp.where(mine, 1, jnp.where(theirs, 2, 0)).astype(jnp.int32).reshape(1)
    weight_space = [
        pltpu.VMEM((width, hidden), BF16),
        pltpu.VMEM((width, hidden), BF16),
        pltpu.VMEM((hidden, width), BF16),
    ]
    count = experts * SLOTS
    results = pl.pallas_call(
        expert_kernel,
        in_specs=[pl.BlockSpec(memory_space=pltpu.SMEM)] + [hbm()] * 7,
        out_specs=hbm(),
        out_shape=jax.ShapeDtypeStruct((experts, SLOTS, full), BF16),
        scratch_shapes=[pltpu.VMEM((4, experts // 4, SLOTS, full), BF16)] * 2
        + weight_space * 2
        + [pltpu.SemaphoreType.DMA((4,)), pltpu.SemaphoreType.DMA((2, 3, CHUNKS)), pltpu.SemaphoreType.DMA((4,))],
        compiler_params=params(60),
        cost_estimate=pl.CostEstimate(
            flops=9 * count * width * hidden,
            bytes_accessed=6 * count * width + 12 * width * hidden,
            transcendentals=2 * count * hidden,
        ),
        name="expert",
    )(mode, arrived, gate_proj, up_proj, down_proj, *other)

    main_w, extra_w = pl.pallas_call(
        weight_kernel,
        in_specs=[whole(), whole()],
        out_specs=[whole(), whole()],
        out_shape=[
            jax.ShapeDtypeStruct((count, tokens), BF16),
            jax.ShapeDtypeStruct((2, count, tokens), BF16),
        ],
        compiler_params=params(24),
        name="combine_weights",
    )(id_rows, gate_rows)

    returned = exchange(results).reshape(count, full)
    return pl.pallas_call(
        combine_kernel,
        grid=(2,),
        in_specs=[
            pl.BlockSpec((count, tokens), lambda i: (0, 0)),
            pl.BlockSpec((1, count, tokens), lambda i: (i, 0, 0)),
            pl.BlockSpec((count, half), lambda i: (0, i)),
            pl.BlockSpec((count, half), lambda i: (0, 2)),
        ],
        out_specs=pl.BlockSpec((tokens, half), lambda i: (0, i)),
        out_shape=jax.ShapeDtypeStruct((tokens, width), BF16),
        compiler_params=params(60),
        name="combine",
    )(main_w, extra_w, returned, returned)


def solution(mesh):
    rows = P(("node", "local"), None)
    stacks = P(("node", "local"), None, None)
    return jax.shard_map(
        shards, mesh=mesh, in_specs=(rows, rows, rows, stacks, stacks, stacks), out_specs=rows, check_vma=False
    )
```

time: 349 us -> 209 us (0.60); the launches traced: 343 us -> 209 us
  blocking collectives: 108 us -> 0 us
  local copies, waits for them, and re-layouts: 70.4 us -> 1.54 us
  waiting for transfers between devices: 103 us -> 149 us
  matrix products: 29.8 us -> 0 us
  Pallas kernels: 0 us -> 29.7 us
  other arithmetic: 23.3 us -> 0.63 us
  starting transfers between devices: 8.96 us -> 26.4 us
    all_to_all x1 -> x0, blocking collectives: 108 us -> none  [shards(): lax.all_to_all(send_buf, ('node', 'local'), split_axis=0, concat_axis=0,...]
    all_to_all x1 -> x2, waiting for transfers between devices: 103 us -> 136 us  [exchange(): lax.all_to_all(rows, ('node', 'local'), split_axis=0, concat_axis=0, tile...]
    dot_general x2 -> x0, matrix products: 29.8 us -> none  [the longest x1 21.3 us: expert_apply(): jnp.dot(hidden_act, down_w, preferred_element_type=jnp.float32)]
    pallas_call x0 -> x4, Pallas kernels: none -> 29.7 us  [the longest x1 18.4 us: shards(): pl.pallas_call(expert_kernel, in_specs=[pl.BlockSpec(memory_space=pltpu.S...]
    unnamed x14 -> x10, local copies, waits for them, and re-layouts: 30.3 us -> 1.54 us
    gather x1 -> x0, local copies, waits for them, and re-layouts: 25.5 us -> none  [shards(): returned[flat_ids, slot_ranks]]
    reduce_sum x3 -> x1, other arithmetic: 20.4 us -> 0.63 us  [shards(): theirs = jnp.sum((expert_ids == my_expert ^ 1).astype(jnp.int32)) > SLOTS]
    all_to_all x1 -> x2, starting transfers between devices: 8.96 us -> 25.6 us  [exchange(): lax.all_to_all(rows, ('node', 'local'), split_axis=0, concat_axis=0, tile...]
  transfers between devices with their start and end apart: 1 -> 5, of which waited for: 1 -> 5; matrix products, arithmetic and copies ran while one was open for 0% -> 0% of each run, Pallas kernels for 0% -> 0%
where the time goes in v5:
time: 209 us
  waiting for transfers between devices  149 us (71%)
  Pallas kernels  29.7 us (14%)
  starting transfers between devices  26.4 us (13%)
    all_to_all x2, waiting for transfers between devices, exchange(): lax.all_to_all(rows, ('node', 'local'), split_axis=0, concat_axis=0, tile...  136 us
    all_to_all x2, starting transfers between devices, exchange(): lax.all_to_all(rows, ('node', 'local'), split_axis=0, concat_axis=0, tile...  25.6 us
    pallas_call x1, Pallas kernels, shards(): pl.pallas_call(expert_kernel, in_specs=[pl.BlockSpec(memory_space=pltpu.S...  18.4 us
    ppermute x3, waiting for transfers between devices, shards(): lax.ppermute(weight, 'local', cores)  12.5 us
    pallas_call x1, Pallas kernels, shards(): pl.pallas_call(send_kernel, grid=(experts // block,), in_specs=[pl.BlockS...  6.06 us
    pallas_call x1, Pallas kernels, shards(): pl.pallas_call(combine_kernel, grid=(2,), in_specs=[pl.BlockSpec((count,...  4.57 us
  transfers between devices with their start and end apart: 5, of which 5 were waited for; matrix products, arithmetic and copies ran while one was open for 0% of the time, Pallas kernels for 0%

profile of v5, /device:TPU:2, one launch (start us, length us, event | category | flops | bytes accessed | tf_op | source)
XLA Modules:
  0.0 208.5 jit_solution(11389424404889868096)
XLA Ops:
  0.0 6.1 %send_rows.1 = bf16[128,8,3072]{2,1,0:T(8,128)(2,1)} custom-call(s32[8,128]{1,0:T(8,128)} %bitcast.4, bf16[128,2048]{1,0:T(8,128)(2,1)} %acts_ref.1), custom_call_target="tpu_custom_call" | custom-call | tf_op jit(solution)/shard_map/send_rows/pallas_call | solution.py:254
  6.1 0.0 copy-start.4
  6.1 0.0 copy-start.2
  6.1 10.9 %all-to-all-start = ((bf16[128,8,3072]{2,1,0:T(8,128)(2,1)}), bf16[128,8,3072]{2,1,0:T(8,128)(2,1)}, u32[]{:S(2)}, u32[]{:S(2)}) async-start(bf16[128,8,3072]{2,1,0:T(8,128)(2,1)} %send_rows.1), calls=%async_computation | async-start | bytes 12582912 | tf_op jit(solution)/shard_map/all_to_all | solution.py:269
  17.0 0.0 copy-done.4
  17.0 0.2 collective-permute-start
  17.2 0.4 collective-permute-start.1
  17.6 0.1 collective-permute-start.2
  17.7 0.0 copy-done.2
  17.8 0.6 convert_reduce_fusion
  19.6 6.3 %collective-permute-done.refs_3_ = bf16[1,2048,768]{2,1,0:T(8,128)(2,1)} collective-permute-done((bf16[1,2048,768]{2,1,0:T(8,128)(2,1)S(1)}, bf16[1,2048,768]{2,1,0:T(8,128)(2,1)}, u32[]{:S(2)}, u32[]{:S(2)}) %collective-permute-start) | collective-permute-done | bytes 3145760 | tf_op jit(solution)/shard_map/ppermute | solution.py:273
  25.9 1.7 collective-permute-done.1.refs_4_
  27.6 4.5 %collective-permute-done.2.refs_5_ = bf16[1,768,2048]{2,1,0:T(8,128)(2,1)} collective-permute-done((bf16[1,768,2048]{2,1,0:T(8,128)(2,1)}, bf16[1,768,2048]{2,1,0:T(8,128)(2,1)}, u32[]{:S(2)}, u32[]{:S(2)}) %collective-permute-start.2) | collective-permute-done | bytes 3145760 | tf_op jit(solution)/shard_map/ppermute | solution.py:273
  32.1 61.8 %all-to-all-done.rows_hbm = bf16[128,8,3072]{2,1,0:T(8,128)(2,1)} async-done(((bf16[128,8,3072]{2,1,0:T(8,128)(2,1)}), bf16[128,8,3072]{2,1,0:T(8,128)(2,1)}, u32[]{:S(2)}, u32[]{:S(2)}) %all-to-all-start) | async-done | bytes 6291488 | tf_op jit(solution)/shard_map/all_to_all | solution.py:269
  93.9 18.4 %expert.1 = bf16[128,8,3072]{2,1,0:T(8,128)(2,1)} custom-call(s32[1]{0:T(128)} %bitcast.2.mode_ref, bf16[128,8,3072]{2,1,0:T(8,128)(2,1)} %all-to-all-done.rows_hbm, bf16[1,2048,768]{2,1,0:T(8,128)(2,1)} %refs_0_.1, bf16[1,2048,768]{2,1,0:T(8,128)(2,1)} %refs_1_.1, bf16[1,768,2048]{2,1,0:T(8,128)(2,1)} %refs_2_.1, ...), custom_call_target="tpu_custom_call" | custom-call | flops 14495514624 | bytes 31457280 | tf_op jit(solution)/shard_map/expert/pallas_call | solution.py:284
  112.3 0.0 copy-start.3
  112.3 14.7 %all-to-all-start.1 = ((bf16[128,8,3072]{2,1,0:T(8,128)(2,1)}), bf16[128,8,3072]{2,1,0:T(8,128)(2,1)}, u32[]{:S(2)}, u32[]{:S(2)}) async-start(bf16[128,8,3072]{2,1,0:T(8,128)(2,1)} %expert.1), calls=%async_computation.1 | async-start | bytes 12582912 | tf_op jit(solution)/shard_map/all_to_all | solution.py:269
  127.0 0.0 copy-done.3
  127.0 0.7 combine_weights.1
  127.8 0.0 copy-start
  127.8 0.8 copy-done
  128.6 0.7 copy-done.1
  129.3 74.6 %all-to-all-done.1 = bf16[128,8,3072]{2,1,0:T(8,128)(2,1)} async-done(((bf16[128,8,3072]{2,1,0:T(8,128)(2,1)}), bf16[128,8,3072]{2,1,0:T(8,128)(2,1)}, u32[]{:S(2)}, u32[]{:S(2)}) %all-to-all-start.1) | async-done | bytes 6291488 | tf_op jit(solution)/shard_map/all_to_all | solution.py:269
  203.9 4.6 %combine.1 = bf16[128,2048]{1,0:T(8,128)(2,1)} custom-call(bf16[1024,128]{1,0:T(8,128)(2,1)} %copy-done.1, bf16[2,1024,128]{2,1,0:T(8,128)(2,1)} %copy-done, bf16[1024,3072]{1,0:T(8,128)(2,1)} %bitcast.3.main_ref.extra_ref, bf16[1024,3072]{1,0:T(8,128)(2,1)} %bitcast.3.main_ref.extra_ref), custom_call_target="tpu_custom_call" | custom-call | tf_op jit(solution)/shard_map/combine/pallas_call | solution.py:314
  (1 shorter events, 0.0 us)
Async XLA Ops:
  6.1 10.9 %copy-start.4 = (bf16[1,2048,768]{2,1,0:T(8,128)(2,1)S(1)}, bf16[1,2048,768]{2,1,0:T(8,128)(2,1)}, u32[]{:S(2)}) copy-start(bf16[1,2048,768]{2,1,0:T(8,128)(2,1)} %refs_0_.1) | copy-start | bytes 9437188
  6.1 11.7 %copy-start.2 = (s32[128,8]{0,1:T(8,128)S(1)}, s32[128,8]{0,1:T(8,128)}, u32[]{:S(2)}) copy-start(s32[128,8]{0,1:T(8,128)} %param.7) | copy-start | bytes 12292
  6.1 87.9 %all-to-all-start = ((bf16[128,8,3072]{2,1,0:T(8,128)(2,1)}), bf16[128,8,3072]{2,1,0:T(8,128)(2,1)}, u32[]{:S(2)}, u32[]{:S(2)}) async-start(bf16[128,8,3072]{2,1,0:T(8,128)(2,1)} %send_rows.1), calls=%async_computation | async-start | bytes 12582912 | tf_op jit(solution)/shard_map/all_to_all | solution.py:269
  17.0 8.9 %collective-permute-start = (bf16[1,2048,768]{2,1,0:T(8,128)(2,1)S(1)}, bf16[1,2048,768]{2,1,0:T(8,128)(2,1)}, u32[]{:S(2)}, u32[]{:S(2)}) collective-permute-start(bf16[1,2048,768]{2,1,0:T(8,128)(2,1)S(1)} %copy-done.4), channel_id=1, source_target_pairs={{0,1},{1,0},{2,3},{3,2},{4,5},{5,4},{6,7},{7,6},{8,9},{9,8},{10,11... | collective-permute-start | bytes 9437192 | tf_op jit(solution)/shard_map/ppermute | solution.py:273
  17.2 10.4 %collective-permute-start.1 = (bf16[1,2048,768]{2,1,0:T(8,128)(2,1)}, bf16[1,2048,768]{2,1,0:T(8,128)(2,1)}, u32[]{:S(2)}, u32[]{:S(2)}) collective-permute-start(bf16[1,2048,768]{2,1,0:T(8,128)(2,1)} %refs_1_.1), channel_id=1, source_target_pairs={{0,1},{1,0},{2,3},{3,2},{4,5},{5,4},{6,7},{7,6},{8,9},{9,8},{10,11... | collective-permute-start | bytes 9437192 | tf_op jit(solution)/shard_map/ppermute | solution.py:273
  17.6 14.5 %collective-permute-start.2 = (bf16[1,768,2048]{2,1,0:T(8,128)(2,1)}, bf16[1,768,2048]{2,1,0:T(8,128)(2,1)}, u32[]{:S(2)}, u32[]{:S(2)}) collective-permute-start(bf16[1,768,2048]{2,1,0:T(8,128)(2,1)} %refs_2_.1), channel_id=1, source_target_pairs={{0,1},{1,0},{2,3},{3,2},{4,5},{5,4},{6,7},{7,6},{8,9},{9,8},{10,11... | collective-permute-start | bytes 9437192 | tf_op jit(solution)/shard_map/ppermute | solution.py:273
  112.3 14.7 %copy-start.3 = (bf16[128,8]{0,1:T(8,128)(2,1)S(1)}, bf16[128,8]{0,1:T(8,128)(2,1)}, u32[]{:S(2)}) copy-start(bf16[128,8]{0,1:T(8,128)(2,1)} %param.8) | copy-start | bytes 6148
  112.3 91.6 %all-to-all-start.1 = ((bf16[128,8,3072]{2,1,0:T(8,128)(2,1)}), bf16[128,8,3072]{2,1,0:T(8,128)(2,1)}, u32[]{:S(2)}, u32[]{:S(2)}) async-start(bf16[128,8,3072]{2,1,0:T(8,128)(2,1)} %expert.1), calls=%async_computation.1 | async-start | bytes 12582912 | tf_op jit(solution)/shard_map/all_to_all | solution.py:269
  127.8 0.8 copy-start
  128.6 0.7 copy-start.1

commit v6 on v5

--- a/solution.py
+++ b/solution.py
@@ -103,6 +103,11 @@
     extra_ref[1] = jnp.where(first_half(own.shape), 0.0, extra).astype(BF16)
 
 
+def wait_all(copies):
+    for copy in copies:
+        copy.wait()
+
+
 CHUNKS = 4
 
 
@@ -110,33 +115,23 @@
     loads = []
     for place, (source, weight) in enumerate(zip(sources, weights)):
         rows = weight.shape[0] // CHUNKS
-        loads.append(
-            [
-                pltpu.make_async_copy(
-                    source.at[0, pl.ds(part * rows, rows)], weight.at[pl.ds(part * rows, rows)], sems.at[place, part]
-                )
-                for part in range(CHUNKS)
-            ]
-        )
+        for part in range(CHUNKS):
+            there = pl.ds(part * rows, rows)
+            loads.append(pltpu.make_async_copy(source.at[0, there], weight.at[there], sems.at[place, part]))
     return loads
 
 
-def wait_all(copies):
-    for copy in copies:
-        copy.wait()
-
-
-def expert_rows(blocks, weights, loads):
+def expert_rows(blocks, weights, loads=None):
     gate_w, up_w, down_w = weights
     if loads:
-        wait_all(loads[0])
-    gates = [dot(rows(), gate_w[...]) for rows in blocks]
+        wait_all(loads[:CHUNKS])
+    gates = [dot(rows, gate_w[...]) for rows in blocks]
     if loads:
-        wait_all(loads[1])
-    ups = [dot(rows(), up_w[...]) for rows in blocks]
+        wait_all(loads[CHUNKS : 2 * CHUNKS])
+    ups = [dot(rows, up_w[...]) for rows in blocks]
     hidden = [(g / (1.0 + jnp.exp(-g)) * u).astype(BF16) for g, u in zip(gates, ups)]
     if loads:
-        wait_all(loads[2])
+        wait_all(loads[2 * CHUNKS :])
     return [dot(rows, down_w[...]).astype(BF16) for rows in hidden]
 
 
@@ -160,48 +155,61 @@
 
 
 def expert_kernel(mode_ref, rows_hbm, *refs):
-    sources = refs[:3], refs[3:6]
-    out_hbm, held, done = refs[6:9]
-    weights = refs[9:12], refs[12:15]
-    row_sems, sems, out_sems = refs[15:]
-    blocks, count, slots, full = held.shape
-    width = weights[0][0].shape[0]
+    out_hbm, held, held_extra, done, done_extra = refs[6:11]
+    weights = refs[11:14], refs[14:17]
+    row_sems, out_sems, sems = refs[17:]
+    blocks, count, slots, width = held.shape
     half = width // 2
     mode = mode_ref[0]
-    loads = [expert_loads(sources[side], weights[side], sems.at[side]) for side in range(2)]
-    rows = [
-        pltpu.make_async_copy(rows_hbm.at[pl.ds(block * count, count)], held.at[block], row_sems.at[block])
-        for block in range(blocks)
-    ]
-    stores = [
-        pltpu.make_async_copy(done.at[block], out_hbm.at[pl.ds(block * count, count)], out_sems.at[block])
-        for block in range(blocks)
-    ]
-    for copy in rows[:2] + loads[0][0] + loads[0][1] + rows[2:] + loads[0][2]:
+
+    def moves(block):
+        there = pl.ds(block * count, count)
+        main, extra = pl.ds(0, width), pl.ds(width, half)
+        return (
+            pltpu.make_async_copy(rows_hbm.at[there, :, main], held.at[block], row_sems.at[0, block]),
+            pltpu.make_async_copy(rows_hbm.at[there, :, extra], held_extra.at[block], row_sems.at[1, block]),
+            pltpu.make_async_copy(done.at[block], out_hbm.at[there, :, main], out_sems.at[0, block]),
+            pltpu.make_async_copy(done_extra.at[block], out_hbm.at[there, :, extra], out_sems.at[1, block]),
+        )
+
+    rows, extra_rows, stores, extra_stores = zip(*[moves(block) for block in range(blocks)])
+    loads = [expert_loads(refs[3 * side : 3 * side + 3], weights[side], sems.at[side]) for side in range(2)]
+    for copy in [*rows[:2], *loads[0][: 2 * CHUNKS], *rows[2:], *loads[0][2 * CHUNKS :], *extra_rows]:
         copy.start()
 
-    @pl.when(mode == 2)
+    @pl.when(mode == 0)
     def _():
-        for copy in loads[1][0] + loads[1][1] + loads[1][2]:
-            copy.start()
+        done_extra[...] = jnp.zeros(done_extra.shape, BF16)
+        for store in extra_stores:
+            store.start()
 
     for pair in range(0, blocks, 2):
         wait_all(rows[pair : pair + 2])
-        both = [lambda b=b: held[b, :, :, :width].reshape(count * slots, width) for b in (pair, pair + 1)]
+        both = [held[block].reshape(count * slots, width) for block in (pair, pair + 1)]
         results = expert_rows(both, weights[0], loads[0] if pair == 0 else None)
         for block, result in zip((pair, pair + 1), results):
-            done[block, :, :, :width] = result.reshape(count, slots, width)
+            done[block] = result.reshape(count, slots, width)
+            stores[block].start()
+        if pair == 0:
+
+            @pl.when(mode == 2)
+            def _():
+                for copy in loads[1]:
+                    copy.start()
+
+    wait_all(extra_rows)
 
     def extras(side):
         if side:
-            wait_all(loads[1][0] + loads[1][1] + loads[1][2])
-        parts = [unfold(held[block, :, :, width:].reshape(count * slots, half)) for block in range(blocks)]
-        both = [lambda a=a: jnp.concatenate(parts[a : a + 2], axis=0) for a in range(0, blocks, 2)]
-        results = expert_rows(both, weights[side], None)
+            wait_all(loads[1])
+        parts = [unfold(held_extra[block].reshape(count * slots, half)) for block in range(blocks)]
+        both = [jnp.concatenate(parts[a : a + 2], axis=0) for a in range(0, blocks, 2)]
+        results = expert_rows(both, weights[side])
         for block in range(blocks):
             start = (block % 2) * count * EXTRA
             result = results[block // 2][start : start + count * EXTRA]
-            done[block, :, :, width:] = fold(result).reshape(count, slots, half)
+            done_extra[block] = fold(result).reshape(count, slots, half)
+            extra_stores[block].start()
 
     for side in range(2):
 
@@ -209,13 +217,7 @@
         def _():
             extras(side)
 
-    @pl.when(mode == 0)
-    def _():
-        done[:, :, :, width:] = jnp.zeros((blocks, count, slots, half), BF16)
-
-    for store in stores:
-        store.start()
-    wait_all(stores)
+    wait_all(stores + extra_stores)
 
 
 def combine_kernel(main_w_ref, extra_w_ref, main_ref, extra_ref, out_ref):
@@ -275,20 +277,20 @@
     mine = jnp.sum((expert_ids == my_expert).astype(jnp.int32)) > SLOTS
     theirs = jnp.sum((expert_ids == (my_expert ^ 1)).astype(jnp.int32)) > SLOTS
     mode = jnp.where(mine, 1, jnp.where(theirs, 2, 0)).astype(jnp.int32).reshape(1)
-    weight_space = [
-        pltpu.VMEM((width, hidden), BF16),
-        pltpu.VMEM((width, hidden), BF16),
-        pltpu.VMEM((hidden, width), BF16),
-    ]
     count = experts * SLOTS
+    weight_shapes = [(width, hidden), (width, hidden), (hidden, width)]
     results = pl.pallas_call(
         expert_kernel,
-        in_specs=[pl.BlockSpec(memory_space=pltpu.SMEM)] + [hbm()] * 7,
+        in_specs=[pl.BlockSpec(memory_space=pltpu.SMEM), hbm()] + [hbm()] * 6,
         out_specs=hbm(),
         out_shape=jax.ShapeDtypeStruct((experts, SLOTS, full), BF16),
-        scratch_shapes=[pltpu.VMEM((4, experts // 4, SLOTS, full), BF16)] * 2
-        + weight_space * 2
-        + [pltpu.SemaphoreType.DMA((4,)), pltpu.SemaphoreType.DMA((2, 3, CHUNKS)), pltpu.SemaphoreType.DMA((4,))],
+        scratch_shapes=[
+            pltpu.VMEM((4, experts // 4, SLOTS, width), BF16),
+            pltpu.VMEM((4, experts // 4, SLOTS, half), BF16),
+        ]
+        * 2
+        + [pltpu.VMEM(shape, BF16) for shape in weight_shapes] * 2
+        + [pltpu.SemaphoreType.DMA((2, 4)), pltpu.SemaphoreType.DMA((2, 4)), pltpu.SemaphoreType.DMA((2, 3, CHUNKS))],
         compiler_params=params(60),
         cost_estimate=pl.CostEstimate(
             flops=9 * count * width * hidden,
@@ -313,14 +315,14 @@
     returned = exchange(results).reshape(count, full)
     return pl.pallas_call(
         combine_kernel,
-        grid=(2,),
+        grid=(2, 2),
         in_specs=[
-            pl.BlockSpec((count, tokens), lambda i: (0, 0)),
-            pl.BlockSpec((1, count, tokens), lambda i: (i, 0, 0)),
-            pl.BlockSpec((count, half), lambda i: (0, i)),
-            pl.BlockSpec((count, half), lambda i: (0, 2)),
+            pl.BlockSpec((count, tokens), lambda j, side: (0, 0)),
+            pl.BlockSpec((1, count, tokens), lambda j, side: (side, 0, 0)),
+            pl.BlockSpec((count, half // 2), lambda j, side: (0, 2 * side + j)),
+            pl.BlockSpec((count, half // 2), lambda j, side: (0, 4 + j)),
         ],
-        out_specs=pl.BlockSpec((tokens, half), lambda i: (0, i)),
+        out_specs=pl.BlockSpec((tokens, half // 2), lambda j, side: (0, 2 * side + j)),
         out_shape=jax.ShapeDtypeStruct((tokens, width), BF16),
         compiler_params=params(60),
         name="combine",

time: 209 us -> 206 us (0.986)
    pallas_call x1, Pallas kernels: 18.4 us -> 15.5 us  [shards(): pl.pallas_call(expert_kernel, in_specs=[pl.BlockSpec(memory_space=pltpu.S...]
where the time goes in v6:
time: 206 us; the launch traced here: 205 us
  waiting for transfers between devices  149 us (72%)
  Pallas kernels  28.2 us (14%)
  starting transfers between devices  24.9 us (12%)
    all_to_all x2, waiting for transfers between devices, exchange(): lax.all_to_all(rows, ('node', 'local'), split_axis=0, concat_axis=0, tile...  136 us
    all_to_all x2, starting transfers between devices, exchange(): lax.all_to_all(rows, ('node', 'local'), split_axis=0, concat_axis=0, tile...  24.1 us
    pallas_call x1, Pallas kernels, shards(): pl.pallas_call(expert_kernel, in_specs=[pl.BlockSpec(memory_space=pltpu.S...  15.5 us
    ppermute x3, waiting for transfers between devices, shards(): lax.ppermute(weight, 'local', cores)  12.5 us
    pallas_call x1, Pallas kernels, shards(): pl.pallas_call(send_kernel, grid=(experts // block,), in_specs=[pl.BlockS...  6.06 us
    pallas_call x1, Pallas kernels, shards(): pl.pallas_call(combine_kernel, grid=(2, 2), in_specs=[pl.BlockSpec((count...  5.85 us
  transfers between devices with their start and end apart: 5, of which 5 were waited for; matrix products, arithmetic and copies ran while one was open for 0% of the time, Pallas kernels for 0%

profile of v6, /device:TPU:2, one launch (start us, length us, event | category | flops | bytes accessed | tf_op | source)
XLA Modules:
  0.0 205.4 jit_solution(16132305233275331217)
XLA Ops:
  0.0 6.1 %send_rows.1 = bf16[128,8,3072]{2,1,0:T(8,128)(2,1)} custom-call(s32[8,128]{1,0:T(8,128)} %bitcast.4, bf16[128,2048]{1,0:T(8,128)(2,1)} %acts_ref.1), custom_call_target="tpu_custom_call" | custom-call | tf_op jit(solution)/shard_map/send_rows/pallas_call | solution.py:256
  6.1 0.0 copy-start.4
  6.1 0.0 copy-start.2
  6.1 10.9 %all-to-all-start = ((bf16[128,8,3072]{2,1,0:T(8,128)(2,1)}), bf16[128,8,3072]{2,1,0:T(8,128)(2,1)}, u32[]{:S(2)}, u32[]{:S(2)}) async-start(bf16[128,8,3072]{2,1,0:T(8,128)(2,1)} %send_rows.1), calls=%async_computation | async-start | bytes 12582912 | tf_op jit(solution)/shard_map/all_to_all | solution.py:271
  17.0 0.0 copy-done.4
  17.0 0.2 collective-permute-start
  17.2 0.4 collective-permute-start.1
  17.6 0.1 collective-permute-start.2
  17.7 0.0 copy-done.2
  17.8 0.6 convert_reduce_fusion
  19.6 6.3 %collective-permute-done.refs_3_ = bf16[1,2048,768]{2,1,0:T(8,128)(2,1)} collective-permute-done((bf16[1,2048,768]{2,1,0:T(8,128)(2,1)S(1)}, bf16[1,2048,768]{2,1,0:T(8,128)(2,1)}, u32[]{:S(2)}, u32[]{:S(2)}) %collective-permute-start) | collective-permute-done | bytes 3145760 | tf_op jit(solution)/shard_map/ppermute | solution.py:275
  25.9 1.7 collective-permute-done.1.refs_4_
  27.6 4.5 %collective-permute-done.2.refs_5_ = bf16[1,768,2048]{2,1,0:T(8,128)(2,1)} collective-permute-done((bf16[1,768,2048]{2,1,0:T(8,128)(2,1)}, bf16[1,768,2048]{2,1,0:T(8,128)(2,1)}, u32[]{:S(2)}, u32[]{:S(2)}) %collective-permute-start.2) | collective-permute-done | bytes 3145760 | tf_op jit(solution)/shard_map/ppermute | solution.py:275
  32.1 61.8 %all-to-all-done.rows_hbm = bf16[128,8,3072]{2,1,0:T(8,128)(2,1)} async-done(((bf16[128,8,3072]{2,1,0:T(8,128)(2,1)}), bf16[128,8,3072]{2,1,0:T(8,128)(2,1)}, u32[]{:S(2)}, u32[]{:S(2)}) %all-to-all-start) | async-done | bytes 6291488 | tf_op jit(solution)/shard_map/all_to_all | solution.py:271
  93.9 15.5 %expert.1 = bf16[128,8,3072]{2,1,0:T(8,128)(2,1)} custom-call(s32[1]{0:T(128)} %bitcast.2.mode_ref, bf16[128,8,3072]{2,1,0:T(8,128)(2,1)} %all-to-all-done.rows_hbm, bf16[1,2048,768]{2,1,0:T(8,128)(2,1)} %refs_0_.1, bf16[1,2048,768]{2,1,0:T(8,128)(2,1)} %refs_1_.1, bf16[1,768,2048]{2,1,0:T(8,128)(2,1)} %refs_2_.1, ...), custom_call_target="tpu_custom_call" | custom-call | flops 14495514624 | bytes 31457280 | tf_op jit(solution)/shard_map/expert/pallas_call | solution.py:282
  109.4 0.0 copy-start.3
  109.4 13.2 %all-to-all-start.1 = ((bf16[128,8,3072]{2,1,0:T(8,128)(2,1)}), bf16[128,8,3072]{2,1,0:T(8,128)(2,1)}, u32[]{:S(2)}, u32[]{:S(2)}) async-start(bf16[128,8,3072]{2,1,0:T(8,128)(2,1)} %expert.1), calls=%async_computation.1 | async-start | bytes 12582912 | tf_op jit(solution)/shard_map/all_to_all | solution.py:271
  122.7 0.0 copy-done.3
  122.7 0.7 combine_weights.1
  123.4 0.0 copy-start
  123.4 0.8 copy-done
  124.2 0.7 copy-done.1
  125.0 74.6 %all-to-all-done.1 = bf16[128,8,3072]{2,1,0:T(8,128)(2,1)} async-done(((bf16[128,8,3072]{2,1,0:T(8,128)(2,1)}), bf16[128,8,3072]{2,1,0:T(8,128)(2,1)}, u32[]{:S(2)}, u32[]{:S(2)}) %all-to-all-start.1) | async-done | bytes 6291488 | tf_op jit(solution)/shard_map/all_to_all | solution.py:271
  199.6 5.8 %combine.1 = bf16[128,2048]{1,0:T(8,128)(2,1)} custom-call(bf16[1024,128]{1,0:T(8,128)(2,1)} %copy-done.1, bf16[2,1024,128]{2,1,0:T(8,128)(2,1)} %copy-done, bf16[1024,3072]{1,0:T(8,128)(2,1)} %bitcast.3.main_ref.extra_ref, bf16[1024,3072]{1,0:T(8,128)(2,1)} %bitcast.3.main_ref.extra_ref), custom_call_target="tpu_custom_call" | custom-call | tf_op jit(solution)/shard_map/combine/pallas_call | solution.py:316
  (1 shorter events, 0.0 us)
Async XLA Ops:
  6.1 10.9 %copy-start.4 = (bf16[1,2048,768]{2,1,0:T(8,128)(2,1)S(1)}, bf16[1,2048,768]{2,1,0:T(8,128)(2,1)}, u32[]{:S(2)}) copy-start(bf16[1,2048,768]{2,1,0:T(8,128)(2,1)} %refs_0_.1) | copy-start | bytes 9437188
  6.1 11.7 %copy-start.2 = (s32[128,8]{0,1:T(8,128)S(1)}, s32[128,8]{0,1:T(8,128)}, u32[]{:S(2)}) copy-start(s32[128,8]{0,1:T(8,128)} %param.7) | copy-start | bytes 12292
  6.1 87.9 %all-to-all-start = ((bf16[128,8,3072]{2,1,0:T(8,128)(2,1)}), bf16[128,8,3072]{2,1,0:T(8,128)(2,1)}, u32[]{:S(2)}, u32[]{:S(2)}) async-start(bf16[128,8,3072]{2,1,0:T(8,128)(2,1)} %send_rows.1), calls=%async_computation | async-start | bytes 12582912 | tf_op jit(solution)/shard_map/all_to_all | solution.py:271
  17.0 8.9 %collective-permute-start = (bf16[1,2048,768]{2,1,0:T(8,128)(2,1)S(1)}, bf16[1,2048,768]{2,1,0:T(8,128)(2,1)}, u32[]{:S(2)}, u32[]{:S(2)}) collective-permute-start(bf16[1,2048,768]{2,1,0:T(8,128)(2,1)S(1)} %copy-done.4), channel_id=1, source_target_pairs={{0,1},{1,0},{2,3},{3,2},{4,5},{5,4},{6,7},{7,6},{8,9},{9,8},{10,11... | collective-permute-start | bytes 9437192 | tf_op jit(solution)/shard_map/ppermute | solution.py:275
  17.2 10.4 %collective-permute-start.1 = (bf16[1,2048,768]{2,1,0:T(8,128)(2,1)}, bf16[1,2048,768]{2,1,0:T(8,128)(2,1)}, u32[]{:S(2)}, u32[]{:S(2)}) collective-permute-start(bf16[1,2048,768]{2,1,0:T(8,128)(2,1)} %refs_1_.1), channel_id=1, source_target_pairs={{0,1},{1,0},{2,3},{3,2},{4,5},{5,4},{6,7},{7,6},{8,9},{9,8},{10,11... | collective-permute-start | bytes 9437192 | tf_op jit(solution)/shard_map/ppermute | solution.py:275
  17.6 14.5 %collective-permute-start.2 = (bf16[1,768,2048]{2,1,0:T(8,128)(2,1)}, bf16[1,768,2048]{2,1,0:T(8,128)(2,1)}, u32[]{:S(2)}, u32[]{:S(2)}) collective-permute-start(bf16[1,768,2048]{2,1,0:T(8,128)(2,1)} %refs_2_.1), channel_id=1, source_target_pairs={{0,1},{1,0},{2,3},{3,2},{4,5},{5,4},{6,7},{7,6},{8,9},{9,8},{10,11... | collective-permute-start | bytes 9437192 | tf_op jit(solution)/shard_map/ppermute | solution.py:275
  109.4 13.2 %copy-start.3 = (bf16[128,8]{0,1:T(8,128)(2,1)S(1)}, bf16[128,8]{0,1:T(8,128)(2,1)}, u32[]{:S(2)}) copy-start(bf16[128,8]{0,1:T(8,128)(2,1)} %param.8) | copy-start | bytes 6148
  109.4 90.1 %all-to-all-start.1 = ((bf16[128,8,3072]{2,1,0:T(8,128)(2,1)}), bf16[128,8,3072]{2,1,0:T(8,128)(2,1)}, u32[]{:S(2)}, u32[]{:S(2)}) async-start(bf16[128,8,3072]{2,1,0:T(8,128)(2,1)} %expert.1), calls=%async_computation.1 | async-start | bytes 12582912 | tf_op jit(solution)/shard_map/all_to_all | solution.py:271
  123.4 0.8 copy-start
  124.2 0.7 copy-start.1

commit v7 on v6

--- a/solution.py
+++ b/solution.py
@@ -58,34 +58,36 @@
     return (iota(shape, 0) & EXTRA) == 0
 
 
-def send_kernel(ids_ref, acts_ref, out_ref, ranks):
+def send_kernel(ids_ref, acts_ref, out_ref, main_picks, extra_picks, stacked):
     tokens, width = acts_ref.shape
-    experts = ranks.shape[0]
+    count = main_picks.shape[0]
     block = out_ref.shape[0]
     half = width // 2
 
     @pl.when(pl.program_id(0) == 0)
     def _():
-        named = marks_of(ids_ref, iota((experts, tokens), 0))
-        ranks[...] = jnp.where(named > 0.0, ranks_of(named), 99.0)
-
-    mine = ranks[pl.ds(pl.multiple_of(pl.program_id(0) * block, block), block)]
-    own = spread(mine, 0)
-    other = spread(mine, 1)
-    main = indicator(own == slot_of(own.shape)).astype(BF16)
-    place = extra_of(own.shape)
-    extra = jnp.maximum(indicator(own == place + SLOTS), indicator(other == place + (SLOTS + EXTRA)))
-    low = jnp.where(first_half(own.shape), extra, 0.0).astype(BF16)
-    high = jnp.where(first_half(own.shape), 0.0, extra).astype(BF16)
-    rows = dot(main, acts_ref[...])
+        named = marks_of(ids_ref, iota((count // SLOTS, tokens), 0))
+        ranks = jnp.where(named > 0.0, ranks_of(named), 99.0)
+        own = spread(ranks, 0)
+        other = spread(ranks, 1)
+        main_picks[...] = indicator(own == slot_of(own.shape)).astype(BF16)
+        place = extra_of(own.shape)
+        extra = jnp.maximum(indicator(own == place + SLOTS), indicator(other == place + (SLOTS + EXTRA)))
+        extra_picks[:, :tokens] = jnp.where(first_half(own.shape), extra, 0.0).astype(BF16)
+        extra_picks[:, tokens:] = jnp.where(first_half(own.shape), 0.0, extra).astype(BF16)
+        stacked[:tokens] = acts_ref[:, :half]
+        stacked[tokens:] = acts_ref[:, half:]
+
+    here = pl.ds(pl.multiple_of(pl.program_id(0) * block * SLOTS, block * SLOTS), block * SLOTS)
+    rows = dot(main_picks[here], acts_ref[...])
     out_ref[:, :, :width] = rows.reshape(block, SLOTS, width).astype(BF16)
-    folded = dot(low, acts_ref[:, :half]) + dot(high, acts_ref[:, half:])
+    folded = dot(extra_picks[here], stacked[...])
     out_ref[:, :, width:] = folded.reshape(block, SLOTS, half).astype(BF16)
 
 
 def weight_kernel(ids_ref, gates_ref, main_ref, extra_ref):
     tokens = ids_ref.shape[1]
-    experts = main_ref.shape[0] // SLOTS
+    experts = main_ref.shape[1] // SLOTS
     labels = iota((experts, tokens), 0)
     named = marks_of(ids_ref, labels)
     gates = jnp.zeros((experts, tokens), F32)
@@ -95,12 +97,12 @@
     ranks = jnp.where(named > 0.0, ranks_of(named), 99.0)
     own = spread(ranks, 0)
     own_gates = spread(gates, 0)
-    main_ref[...] = jnp.where(own == slot_of(own.shape), own_gates, 0.0).astype(BF16)
+    main_ref[...] = jnp.where(own == slot_of(own.shape), own_gates, 0.0).T.astype(BF16)
     place = extra_of(own.shape)
     extra = jnp.where(own == place + SLOTS, own_gates, 0.0)
     extra += jnp.where(spread(ranks, 1) == place + (SLOTS + EXTRA), spread(gates, 1), 0.0)
-    extra_ref[0] = jnp.where(first_half(own.shape), extra, 0.0).astype(BF16)
-    extra_ref[1] = jnp.where(first_half(own.shape), 0.0, extra).astype(BF16)
+    extra_ref[0] = jnp.where(first_half(own.shape), extra, 0.0).T.astype(BF16)
+    extra_ref[1] = jnp.where(first_half(own.shape), 0.0, extra).T.astype(BF16)
 
 
 def wait_all(copies):
@@ -221,9 +223,7 @@
 
 
 def combine_kernel(main_w_ref, extra_w_ref, main_ref, extra_ref, out_ref):
-    over_rows = (((0,), (0,)), ((), ()))
-    total = lax.dot_general(main_w_ref[...], main_ref[...], over_rows, preferred_element_type=F32)
-    total += lax.dot_general(extra_w_ref[0], extra_ref[...], over_rows, preferred_element_type=F32)
+    total = dot(main_w_ref[...], main_ref[...]) + dot(extra_w_ref[0], extra_ref[...])
     out_ref[...] = total.astype(BF16)
 
 
@@ -262,7 +262,11 @@
         ],
         out_specs=pl.BlockSpec((block, SLOTS, full), lambda i: (i, 0, 0)),
         out_shape=jax.ShapeDtypeStruct((experts, SLOTS, full), BF16),
-        scratch_shapes=[pltpu.VMEM((experts, tokens), F32)],
+        scratch_shapes=[
+            pltpu.VMEM((experts * SLOTS, tokens), BF16),
+            pltpu.VMEM((experts * SLOTS, 2 * tokens), BF16),
+            pltpu.VMEM((2 * tokens, half), BF16),
+        ],
         compiler_params=params(60),
         name="send_rows",
     )(id_rows, activations)
@@ -305,8 +309,8 @@
         in_specs=[whole(), whole()],
         out_specs=[whole(), whole()],
         out_shape=[
-            jax.ShapeDtypeStruct((count, tokens), BF16),
-            jax.ShapeDtypeStruct((2, count, tokens), BF16),
+            jax.ShapeDtypeStruct((tokens, count), BF16),
+            jax.ShapeDtypeStruct((2, tokens, count), BF16),
         ],
         compiler_params=params(24),
         name="combine_weights",
@@ -317,8 +321,8 @@
         combine_kernel,
         grid=(2, 2),
         in_specs=[
-            pl.BlockSpec((count, tokens), lambda j, side: (0, 0)),
-            pl.BlockSpec((1, count, tokens), lambda j, side: (side, 0, 0)),
+            pl.BlockSpec((tokens, count), lambda j, side: (0, 0)),
+            pl.BlockSpec((1, tokens, count), lambda j, side: (side, 0, 0)),
             pl.BlockSpec((count, half // 2), lambda j, side: (0, 2 * side + j)),
             pl.BlockSpec((count, half // 2), lambda j, side: (0, 4 + j)),
         ],

time: 206 us -> 206 us (level)
  no operation moved by 1% of the time
where the time goes in v7:
time: 206 us; the launch traced here: 205 us
  waiting for transfers between devices  149 us (72%)
  Pallas kernels  28.1 us (14%)
  starting transfers between devices  25 us (12%)
    all_to_all x2, waiting for transfers between devices, exchange(): lax.all_to_all(rows, ('node', 'local'), split_axis=0, concat_axis=0, tile...  136 us
    all_to_all x2, starting transfers between devices, exchange(): lax.all_to_all(rows, ('node', 'local'), split_axis=0, concat_axis=0, tile...  24.3 us
    pallas_call x1, Pallas kernels, shards(): pl.pallas_call(expert_kernel, in_specs=[pl.BlockSpec(memory_space=pltpu.S...  15.5 us
    ppermute x3, waiting for transfers between devices, shards(): lax.ppermute(weight, 'local', cores)  12.5 us
    pallas_call x1, Pallas kernels, shards(): pl.pallas_call(send_kernel, grid=(experts // block,), in_specs=[pl.BlockS...  5.84 us
    pallas_call x1, Pallas kernels, shards(): pl.pallas_call(combine_kernel, grid=(2, 2), in_specs=[pl.BlockSpec((token...  5.8 us
  transfers between devices with their start and end apart: 5, of which 5 were waited for; matrix products, arithmetic and copies ran while one was open for 0% of the time, Pallas kernels for 0%

profile of v7, /device:TPU:2, one launch (start us, length us, event | category | flops | bytes accessed | tf_op | source)
XLA Modules:
  0.0 205.3 jit_solution(2933515520062751264)
XLA Ops:
  0.0 5.8 %send_rows.1 = bf16[128,8,3072]{2,1,0:T(8,128)(2,1)} custom-call(s32[8,128]{1,0:T(8,128)} %bitcast.4, bf16[128,2048]{1,0:T(8,128)(2,1)} %acts_ref.1), custom_call_target="tpu_custom_call" | custom-call | tf_op jit(solution)/shard_map/send_rows/pallas_call | solution.py:256
  5.8 0.0 copy-start.4
  5.8 0.0 copy-start.2
  5.8 10.9 %all-to-all-start = ((bf16[128,8,3072]{2,1,0:T(8,128)(2,1)}), bf16[128,8,3072]{2,1,0:T(8,128)(2,1)}, u32[]{:S(2)}, u32[]{:S(2)}) async-start(bf16[128,8,3072]{2,1,0:T(8,128)(2,1)} %send_rows.1), calls=%async_computation | async-start | bytes 12582912 | tf_op jit(solution)/shard_map/all_to_all | solution.py:275
  16.8 0.0 copy-done.4
  16.8 0.2 collective-permute-start
  17.0 0.4 collective-permute-start.1
  17.4 0.1 collective-permute-start.2
  17.5 0.0 copy-done.2
  17.5 0.6 convert_reduce_fusion
  19.4 6.3 %collective-permute-done.refs_3_ = bf16[1,2048,768]{2,1,0:T(8,128)(2,1)} collective-permute-done((bf16[1,2048,768]{2,1,0:T(8,128)(2,1)S(1)}, bf16[1,2048,768]{2,1,0:T(8,128)(2,1)}, u32[]{:S(2)}, u32[]{:S(2)}) %collective-permute-start) | collective-permute-done | bytes 3145760 | tf_op jit(solution)/shard_map/ppermute | solution.py:279
  25.7 1.7 collective-permute-done.1.refs_4_
  27.4 4.5 %collective-permute-done.2.refs_5_ = bf16[1,768,2048]{2,1,0:T(8,128)(2,1)} collective-permute-done((bf16[1,768,2048]{2,1,0:T(8,128)(2,1)}, bf16[1,768,2048]{2,1,0:T(8,128)(2,1)}, u32[]{:S(2)}, u32[]{:S(2)}) %collective-permute-start.2) | collective-permute-done | bytes 3145760 | tf_op jit(solution)/shard_map/ppermute | solution.py:279
  31.9 61.8 %all-to-all-done.rows_hbm = bf16[128,8,3072]{2,1,0:T(8,128)(2,1)} async-done(((bf16[128,8,3072]{2,1,0:T(8,128)(2,1)}), bf16[128,8,3072]{2,1,0:T(8,128)(2,1)}, u32[]{:S(2)}, u32[]{:S(2)}) %all-to-all-start) | async-done | bytes 6291488 | tf_op jit(solution)/shard_map/all_to_all | solution.py:275
  93.7 15.5 %expert.1 = bf16[128,8,3072]{2,1,0:T(8,128)(2,1)} custom-call(s32[1]{0:T(128)} %bitcast.2.mode_ref, bf16[128,8,3072]{2,1,0:T(8,128)(2,1)} %all-to-all-done.rows_hbm, bf16[1,2048,768]{2,1,0:T(8,128)(2,1)} %refs_0_.1, bf16[1,2048,768]{2,1,0:T(8,128)(2,1)} %refs_1_.1, bf16[1,768,2048]{2,1,0:T(8,128)(2,1)} %refs_2_.1, ...), custom_call_target="tpu_custom_call" | custom-call | flops 14495514624 | bytes 31457280 | tf_op jit(solution)/shard_map/expert/pallas_call | solution.py:286
  109.2 0.0 copy-start.3
  109.2 13.3 %all-to-all-start.1 = ((bf16[128,8,3072]{2,1,0:T(8,128)(2,1)}), bf16[128,8,3072]{2,1,0:T(8,128)(2,1)}, u32[]{:S(2)}, u32[]{:S(2)}) async-start(bf16[128,8,3072]{2,1,0:T(8,128)(2,1)} %expert.1), calls=%async_computation.1 | async-start | bytes 12582912 | tf_op jit(solution)/shard_map/all_to_all | solution.py:275
  122.6 0.0 copy-done.3
  122.6 0.9 combine_weights.1
  123.5 0.0 copy-start
  123.5 0.8 copy-done
  124.3 0.7 copy-done.1
  125.0 74.5 %all-to-all-done.1 = bf16[128,8,3072]{2,1,0:T(8,128)(2,1)} async-done(((bf16[128,8,3072]{2,1,0:T(8,128)(2,1)}), bf16[128,8,3072]{2,1,0:T(8,128)(2,1)}, u32[]{:S(2)}, u32[]{:S(2)}) %all-to-all-start.1) | async-done | bytes 6291488 | tf_op jit(solution)/shard_map/all_to_all | solution.py:275
  199.5 5.8 %combine.1 = bf16[128,2048]{1,0:T(8,128)(2,1)} custom-call(bf16[128,1024]{1,0:T(8,128)(2,1)} %copy-done.1, bf16[2,128,1024]{2,1,0:T(8,128)(2,1)} %copy-done, bf16[1024,3072]{1,0:T(8,128)(2,1)} %bitcast.3.main_ref.extra_ref, bf16[1024,3072]{1,0:T(8,128)(2,1)} %bitcast.3.main_ref.extra_ref), custom_call_target="tpu_custom_call" | custom-call | tf_op jit(solution)/shard_map/combine/pallas_call | solution.py:320
  (1 shorter events, 0.0 us)
Async XLA Ops:
  5.8 10.9 %copy-start.4 = (bf16[1,2048,768]{2,1,0:T(8,128)(2,1)S(1)}, bf16[1,2048,768]{2,1,0:T(8,128)(2,1)}, u32[]{:S(2)}) copy-start(bf16[1,2048,768]{2,1,0:T(8,128)(2,1)} %refs_0_.1) | copy-start | bytes 9437188
  5.8 11.7 %copy-start.2 = (s32[128,8]{0,1:T(8,128)S(1)}, s32[128,8]{0,1:T(8,128)}, u32[]{:S(2)}) copy-start(s32[128,8]{0,1:T(8,128)} %param.7) | copy-start | bytes 12292
  5.8 87.9 %all-to-all-start = ((bf16[128,8,3072]{2,1,0:T(8,128)(2,1)}), bf16[128,8,3072]{2,1,0:T(8,128)(2,1)}, u32[]{:S(2)}, u32[]{:S(2)}) async-start(bf16[128,8,3072]{2,1,0:T(8,128)(2,1)} %send_rows.1), calls=%async_computation | async-start | bytes 12582912 | tf_op jit(solution)/shard_map/all_to_all | solution.py:275
  16.8 8.9 %collective-permute-start = (bf16[1,2048,768]{2,1,0:T(8,128)(2,1)S(1)}, bf16[1,2048,768]{2,1,0:T(8,128)(2,1)}, u32[]{:S(2)}, u32[]{:S(2)}) collective-permute-start(bf16[1,2048,768]{2,1,0:T(8,128)(2,1)S(1)} %copy-done.4), channel_id=1, source_target_pairs={{0,1},{1,0},{2,3},{3,2},{4,5},{5,4},{6,7},{7,6},{8,9},{9,8},{10,11... | collective-permute-start | bytes 9437192 | tf_op jit(solution)/shard_map/ppermute | solution.py:279
  17.0 10.4 %collective-permute-start.1 = (bf16[1,2048,768]{2,1,0:T(8,128)(2,1)}, bf16[1,2048,768]{2,1,0:T(8,128)(2,1)}, u32[]{:S(2)}, u32[]{:S(2)}) collective-permute-start(bf16[1,2048,768]{2,1,0:T(8,128)(2,1)} %refs_1_.1), channel_id=1, source_target_pairs={{0,1},{1,0},{2,3},{3,2},{4,5},{5,4},{6,7},{7,6},{8,9},{9,8},{10,11... | collective-permute-start | bytes 9437192 | tf_op jit(solution)/shard_map/ppermute | solution.py:279
  17.4 14.5 %collective-permute-start.2 = (bf16[1,768,2048]{2,1,0:T(8,128)(2,1)}, bf16[1,768,2048]{2,1,0:T(8,128)(2,1)}, u32[]{:S(2)}, u32[]{:S(2)}) collective-permute-start(bf16[1,768,2048]{2,1,0:T(8,128)(2,1)} %refs_2_.1), channel_id=1, source_target_pairs={{0,1},{1,0},{2,3},{3,2},{4,5},{5,4},{6,7},{7,6},{8,9},{9,8},{10,11... | collective-permute-start | bytes 9437192 | tf_op jit(solution)/shard_map/ppermute | solution.py:279
  109.2 13.4 %copy-start.3 = (bf16[128,8]{0,1:T(8,128)(2,1)S(1)}, bf16[128,8]{0,1:T(8,128)(2,1)}, u32[]{:S(2)}) copy-start(bf16[128,8]{0,1:T(8,128)(2,1)} %param.8) | copy-start | bytes 6148
  109.2 90.3 %all-to-all-start.1 = ((bf16[128,8,3072]{2,1,0:T(8,128)(2,1)}), bf16[128,8,3072]{2,1,0:T(8,128)(2,1)}, u32[]{:S(2)}, u32[]{:S(2)}) async-start(bf16[128,8,3072]{2,1,0:T(8,128)(2,1)} %expert.1), calls=%async_computation.1 | async-start | bytes 12582912 | tf_op jit(solution)/shard_map/all_to_all | solution.py:275
  123.5 0.8 copy-start
  124.3 0.7 copy-start.1

commit v8 on v7

--- a/solution.py
+++ b/solution.py
@@ -58,31 +58,47 @@
     return (iota(shape, 0) & EXTRA) == 0
 
 
-def send_kernel(ids_ref, acts_ref, out_ref, main_picks, extra_picks, stacked):
+def wait_all(copies):
+    for copy in copies:
+        copy.wait()
+
+
+def send_kernel(ids_hbm, acts_hbm, out_hbm, ids_ref, acts_ref, held, in_sems, out_sems):
     tokens, width = acts_ref.shape
-    count = main_picks.shape[0]
-    block = out_ref.shape[0]
+    experts = held.shape[0]
     half = width // 2
-
-    @pl.when(pl.program_id(0) == 0)
-    def _():
-        named = marks_of(ids_ref, iota((count // SLOTS, tokens), 0))
-        ranks = jnp.where(named > 0.0, ranks_of(named), 99.0)
-        own = spread(ranks, 0)
-        other = spread(ranks, 1)
-        main_picks[...] = indicator(own == slot_of(own.shape)).astype(BF16)
-        place = extra_of(own.shape)
-        extra = jnp.maximum(indicator(own == place + SLOTS), indicator(other == place + (SLOTS + EXTRA)))
-        extra_picks[:, :tokens] = jnp.where(first_half(own.shape), extra, 0.0).astype(BF16)
-        extra_picks[:, tokens:] = jnp.where(first_half(own.shape), 0.0, extra).astype(BF16)
-        stacked[:tokens] = acts_ref[:, :half]
-        stacked[tokens:] = acts_ref[:, half:]
-
-    here = pl.ds(pl.multiple_of(pl.program_id(0) * block * SLOTS, block * SLOTS), block * SLOTS)
-    rows = dot(main_picks[here], acts_ref[...])
-    out_ref[:, :, :width] = rows.reshape(block, SLOTS, width).astype(BF16)
-    folded = dot(extra_picks[here], stacked[...])
-    out_ref[:, :, width:] = folded.reshape(block, SLOTS, half).astype(BF16)
+    runs = out_sems.shape[0]
+    run = experts // runs
+    ids_copy = pltpu.make_async_copy(ids_hbm, ids_ref, in_sems.at[0])
+    acts_copy = pltpu.make_async_copy(acts_hbm, acts_ref, in_sems.at[1])
+    ids_copy.start()
+    acts_copy.start()
+    ids_copy.wait()
+    named = marks_of(ids_ref, iota((experts, tokens), 0))
+    ranks = jnp.where(named > 0.0, ranks_of(named), 99.0)
+    own = spread(ranks, 0)
+    other = spread(ranks, 1)
+    main = indicator(own == slot_of(own.shape)).astype(BF16)
+    place = extra_of(own.shape)
+    extra = jnp.maximum(indicator(own == place + SLOTS), indicator(other == place + (SLOTS + EXTRA)))
+    low = jnp.where(first_half(own.shape), extra, 0.0)
+    high = jnp.where(first_half(own.shape), 0.0, extra)
+    folds = jnp.concatenate([low, high], axis=1).astype(BF16)
+    acts_copy.wait()
+    acts = acts_ref[...]
+    stacked = jnp.concatenate([acts[:, :half], acts[:, half:]], axis=0)
+    copies = []
+    for pair in range(0, runs, 2):
+        start, stop = pair * run, (pair + 2) * run
+        rows = dot(main[start * SLOTS : stop * SLOTS], acts)
+        held[start:stop, :, :width] = rows.reshape(2 * run, SLOTS, width).astype(BF16)
+        folded = dot(folds[start * SLOTS : stop * SLOTS], stacked)
+        held[start:stop, :, width:] = folded.reshape(2 * run, SLOTS, half).astype(BF16)
+        for part in (pair, pair + 1):
+            there = pl.ds(part * run, run)
+            copies.append(pltpu.make_async_copy(held.at[there], out_hbm.at[there], out_sems.at[part]))
+            copies[-1].start()
+    wait_all(copies)
 
 
 def weight_kernel(ids_ref, gates_ref, main_ref, extra_ref):
@@ -105,11 +121,6 @@
     extra_ref[1] = jnp.where(first_half(own.shape), 0.0, extra).T.astype(BF16)
 
 
-def wait_all(copies):
-    for copy in copies:
-        copy.wait()
-
-
 CHUNKS = 4
 
 
@@ -222,9 +233,38 @@
     wait_all(stores + extra_stores)
 
 
-def combine_kernel(main_w_ref, extra_w_ref, main_ref, extra_ref, out_ref):
-    total = dot(main_w_ref[...], main_ref[...]) + dot(extra_w_ref[0], extra_ref[...])
-    out_ref[...] = total.astype(BF16)
+def combine_kernel(main_w_hbm, extra_w_hbm, rows_hbm, out_hbm, main_w, extra_w, held, out_ref, w_sems, sems, out_sems):
+    tokens, width = out_ref.shape
+    half = width // 2
+    runs = sems.shape[0]
+    run = held.shape[0] // runs
+    w_copies = [
+        pltpu.make_async_copy(main_w_hbm, main_w, w_sems.at[0]),
+        pltpu.make_async_copy(extra_w_hbm, extra_w, w_sems.at[1]),
+    ]
+    copies = [
+        pltpu.make_async_copy(rows_hbm.at[pl.ds(part * run, run)], held.at[pl.ds(part * run, run)], sems.at[part])
+        for part in range(runs)
+    ]
+    for copy in w_copies + copies:
+        copy.start()
+    wait_all(w_copies)
+    totals = [None, None]
+    for pair in range(0, runs, 2):
+        wait_all(copies[pair : pair + 2])
+        here = slice(pair * run, (pair + 2) * run)
+        extra = held[here, width:]
+        for side in range(2):
+            rows = held[here, side * half : (side + 1) * half]
+            part = dot(main_w[:, here], rows) + dot(extra_w[side, :, here], extra)
+            totals[side] = part if totals[side] is None else totals[side] + part
+    stores = []
+    for side in range(2):
+        columns = pl.ds(side * half, half)
+        out_ref[:, side * half : (side + 1) * half] = totals[side].astype(BF16)
+        stores.append(pltpu.make_async_copy(out_ref.at[:, columns], out_hbm.at[:, columns], out_sems.at[side]))
+        stores[-1].start()
+    wait_all(stores)
 
 
 def params(megabytes):
@@ -252,20 +292,17 @@
     id_rows = expert_ids.T
     gate_rows = route_gates.T
 
-    block = experts // 4
     sent = pl.pallas_call(
         send_kernel,
-        grid=(experts // block,),
-        in_specs=[
-            pl.BlockSpec((top, tokens), lambda i: (0, 0)),
-            pl.BlockSpec((tokens, width), lambda i: (0, 0)),
-        ],
-        out_specs=pl.BlockSpec((block, SLOTS, full), lambda i: (i, 0, 0)),
+        in_specs=[hbm(), hbm()],
+        out_specs=hbm(),
         out_shape=jax.ShapeDtypeStruct((experts, SLOTS, full), BF16),
         scratch_shapes=[
-            pltpu.VMEM((experts * SLOTS, tokens), BF16),
-            pltpu.VMEM((experts * SLOTS, 2 * tokens), BF16),
-            pltpu.VMEM((2 * tokens, half), BF16),
+            pltpu.VMEM((top, tokens), jnp.int32),
+            pltpu.VMEM((tokens, width), BF16),
+            pltpu.VMEM((experts, SLOTS, full), BF16),
+            pltpu.SemaphoreType.DMA((2,)),
+            pltpu.SemaphoreType.DMA((8,)),
         ],
         compiler_params=params(60),
         name="send_rows",
@@ -319,18 +356,21 @@
     returned = exchange(results).reshape(count, full)
     return pl.pallas_call(
         combine_kernel,
-        grid=(2, 2),
-        in_specs=[
-            pl.BlockSpec((tokens, count), lambda j, side: (0, 0)),
-            pl.BlockSpec((1, tokens, count), lambda j, side: (side, 0, 0)),
-            pl.BlockSpec((count, half // 2), lambda j, side: (0, 2 * side + j)),
-            pl.BlockSpec((count, half // 2), lambda j, side: (0, 4 + j)),
+        in_specs=[hbm()] * 3,
+        out_specs=hbm(),
+        out_shape=jax.ShapeDtypeStruct((tokens, width), BF16),
+        scratch_shapes=[
+            pltpu.VMEM((tokens, count), BF16),
+            pltpu.VMEM((2, tokens, count), BF16),
+            pltpu.VMEM((count, full), BF16),
+            pltpu.VMEM((tokens, width), BF16),
+            pltpu.SemaphoreType.DMA((2,)),
+            pltpu.SemaphoreType.DMA((8,)),
+            pltpu.SemaphoreType.DMA((2,)),
         ],
-        out_specs=pl.BlockSpec((tokens, half // 2), lambda j, side: (0, 2 * side + j)),
-        out_shape=jax.ShapeDtypeStruct((tokens, width), BF16),
         compiler_params=params(60),
         name="combine",
-    )(main_w, extra_w, returned, returned)
+    )(main_w, extra_w, returned)
 
 
 def solution(mesh):

time: 206 us -> 203 us (0.985)
  Pallas kernels: 28.1 us -> 26 us
    pallas_call x2, Pallas kernels: 11.6 us -> 9.56 us  [the longest x1 5.03 us: shards(): pl.pallas_call(combine_kernel, in_specs=[hbm()] * 3, out_specs=hbm(), out...]
where the time goes in v8:
time: 203 us; the launch traced here: 202 us
  waiting for transfers between devices  149 us (73%)
  Pallas kernels  26 us (13%)
  starting transfers between devices  23.9 us (12%)
    all_to_all x2, waiting for transfers between devices, exchange(): lax.all_to_all(rows, ('node', 'local'), split_axis=0, concat_axis=0, tile...  136 us
    all_to_all x2, starting transfers between devices, exchange(): lax.all_to_all(rows, ('node', 'local'), split_axis=0, concat_axis=0, tile...  23.2 us
    pallas_call x1, Pallas kernels, shards(): pl.pallas_call(expert_kernel, in_specs=[pl.BlockSpec(memory_space=pltpu.S...  15.5 us
    ppermute x3, waiting for transfers between devices, shards(): lax.ppermute(weight, 'local', cores)  12.5 us
    pallas_call x1, Pallas kernels, shards(): pl.pallas_call(combine_kernel, in_specs=[hbm()] * 3, out_specs=hbm(), out...  5.03 us
    pallas_call x1, Pallas kernels, shards(): pl.pallas_call(send_kernel, in_specs=[hbm(), hbm()], out_specs=hbm(), out...  4.52 us
  transfers between devices with their start and end apart: 5, of which 5 were waited for; matrix products, arithmetic and copies ran while one was open for 0% of the time, Pallas kernels for 0%

profile of v8, /device:TPU:2, one launch (start us, length us, event | category | flops | bytes accessed | tf_op | source)
XLA Modules:
  0.0 202.3 jit_solution(11022808141629318986)
XLA Ops:
  0.0 4.5 %send_rows.1 = bf16[128,8,3072]{2,1,0:T(8,128)(2,1)} custom-call(s32[8,128]{1,0:T(8,128)} %bitcast.4, bf16[128,2048]{1,0:T(8,128)(2,1)} %acts_hbm.1), custom_call_target="tpu_custom_call" | custom-call | tf_op jit(solution)/shard_map/send_rows/pallas_call | solution.py:295
  4.5 0.0 copy-start.4
  4.5 0.0 copy-start.2
  4.6 10.9 %all-to-all-start = ((bf16[128,8,3072]{2,1,0:T(8,128)(2,1)}), bf16[128,8,3072]{2,1,0:T(8,128)(2,1)}, u32[]{:S(2)}, u32[]{:S(2)}) async-start(bf16[128,8,3072]{2,1,0:T(8,128)(2,1)} %send_rows.1), calls=%async_computation | async-start | bytes 12582912 | tf_op jit(solution)/shard_map/all_to_all | solution.py:312
  15.5 0.0 copy-done.4
  15.5 0.2 collective-permute-start
  15.7 0.4 collective-permute-start.1
  16.1 0.1 collective-permute-start.2
  16.2 0.0 copy-done.2
  16.3 0.6 convert_reduce_fusion
  18.1 6.3 %collective-permute-done.refs_3_ = bf16[1,2048,768]{2,1,0:T(8,128)(2,1)} collective-permute-done((bf16[1,2048,768]{2,1,0:T(8,128)(2,1)S(1)}, bf16[1,2048,768]{2,1,0:T(8,128)(2,1)}, u32[]{:S(2)}, u32[]{:S(2)}) %collective-permute-start) | collective-permute-done | bytes 3145760 | tf_op jit(solution)/shard_map/ppermute | solution.py:316
  24.4 1.7 collective-permute-done.1.refs_4_
  26.1 4.5 %collective-permute-done.2.refs_5_ = bf16[1,768,2048]{2,1,0:T(8,128)(2,1)} collective-permute-done((bf16[1,768,2048]{2,1,0:T(8,128)(2,1)}, bf16[1,768,2048]{2,1,0:T(8,128)(2,1)}, u32[]{:S(2)}, u32[]{:S(2)}) %collective-permute-start.2) | collective-permute-done | bytes 3145760 | tf_op jit(solution)/shard_map/ppermute | solution.py:316
  30.6 61.8 %all-to-all-done.rows_hbm = bf16[128,8,3072]{2,1,0:T(8,128)(2,1)} async-done(((bf16[128,8,3072]{2,1,0:T(8,128)(2,1)}), bf16[128,8,3072]{2,1,0:T(8,128)(2,1)}, u32[]{:S(2)}, u32[]{:S(2)}) %all-to-all-start) | async-done | bytes 6291488 | tf_op jit(solution)/shard_map/all_to_all | solution.py:312
  92.4 15.5 %expert.1 = bf16[128,8,3072]{2,1,0:T(8,128)(2,1)} custom-call(s32[1]{0:T(128)} %bitcast.2.mode_ref, bf16[128,8,3072]{2,1,0:T(8,128)(2,1)} %all-to-all-done.rows_hbm, bf16[1,2048,768]{2,1,0:T(8,128)(2,1)} %refs_0_.1, bf16[1,2048,768]{2,1,0:T(8,128)(2,1)} %refs_1_.1, bf16[1,768,2048]{2,1,0:T(8,128)(2,1)} %refs_2_.1, ...), custom_call_target="tpu_custom_call" | custom-call | flops 14495514624 | bytes 31457280 | tf_op jit(solution)/shard_map/expert/pallas_call | solution.py:323
  107.9 0.0 copy-start.3
  107.9 12.2 %all-to-all-start.1 = ((bf16[128,8,3072]{2,1,0:T(8,128)(2,1)}), bf16[128,8,3072]{2,1,0:T(8,128)(2,1)}, u32[]{:S(2)}, u32[]{:S(2)}) async-start(bf16[128,8,3072]{2,1,0:T(8,128)(2,1)} %expert.1), calls=%async_computation.1 | async-start | bytes 12582912 | tf_op jit(solution)/shard_map/all_to_all | solution.py:312
  120.2 0.0 copy-done.3
  120.2 0.9 combine_weights.1
  121.1 0.0 copy-start
  121.1 0.8 copy-done
  121.9 0.7 copy-done.1
  122.6 74.5 %all-to-all-done.1 = bf16[128,8,3072]{2,1,0:T(8,128)(2,1)} async-done(((bf16[128,8,3072]{2,1,0:T(8,128)(2,1)}), bf16[128,8,3072]{2,1,0:T(8,128)(2,1)}, u32[]{:S(2)}, u32[]{:S(2)}) %all-to-all-start.1) | async-done | bytes 6291488 | tf_op jit(solution)/shard_map/all_to_all | solution.py:312
  197.1 5.0 %combine.1 = bf16[128,2048]{1,0:T(8,128)(2,1)} custom-call(bf16[128,1024]{1,0:T(8,128)(2,1)} %copy-done.1, bf16[2,128,1024]{2,1,0:T(8,128)(2,1)} %copy-done, bf16[1024,3072]{1,0:T(8,128)(2,1)} %bitcast.3.rows_hbm), custom_call_target="tpu_custom_call" | custom-call | tf_op jit(solution)/shard_map/combine/pallas_call | solution.py:357
  (1 shorter events, 0.0 us)
Async XLA Ops:
  4.5 11.0 %copy-start.4 = (bf16[1,2048,768]{2,1,0:T(8,128)(2,1)S(1)}, bf16[1,2048,768]{2,1,0:T(8,128)(2,1)}, u32[]{:S(2)}) copy-start(bf16[1,2048,768]{2,1,0:T(8,128)(2,1)} %refs_0_.1) | copy-start | bytes 9437188
  4.5 11.7 %copy-start.2 = (s32[128,8]{0,1:T(8,128)S(1)}, s32[128,8]{0,1:T(8,128)}, u32[]{:S(2)}) copy-start(s32[128,8]{0,1:T(8,128)} %param.7) | copy-start | bytes 12292
  4.6 87.9 %all-to-all-start = ((bf16[128,8,3072]{2,1,0:T(8,128)(2,1)}), bf16[128,8,3072]{2,1,0:T(8,128)(2,1)}, u32[]{:S(2)}, u32[]{:S(2)}) async-start(bf16[128,8,3072]{2,1,0:T(8,128)(2,1)} %send_rows.1), calls=%async_computation | async-start | bytes 12582912 | tf_op jit(solution)/shard_map/all_to_all | solution.py:312
  15.5 8.9 %collective-permute-start = (bf16[1,2048,768]{2,1,0:T(8,128)(2,1)S(1)}, bf16[1,2048,768]{2,1,0:T(8,128)(2,1)}, u32[]{:S(2)}, u32[]{:S(2)}) collective-permute-start(bf16[1,2048,768]{2,1,0:T(8,128)(2,1)S(1)} %copy-done.4), channel_id=1, source_target_pairs={{0,1},{1,0},{2,3},{3,2},{4,5},{5,4},{6,7},{7,6},{8,9},{9,8},{10,11... | collective-permute-start | bytes 9437192 | tf_op jit(solution)/shard_map/ppermute | solution.py:316
  15.7 10.4 %collective-permute-start.1 = (bf16[1,2048,768]{2,1,0:T(8,128)(2,1)}, bf16[1,2048,768]{2,1,0:T(8,128)(2,1)}, u32[]{:S(2)}, u32[]{:S(2)}) collective-permute-start(bf16[1,2048,768]{2,1,0:T(8,128)(2,1)} %refs_1_.1), channel_id=1, source_target_pairs={{0,1},{1,0},{2,3},{3,2},{4,5},{5,4},{6,7},{7,6},{8,9},{9,8},{10,11... | collective-permute-start | bytes 9437192 | tf_op jit(solution)/shard_map/ppermute | solution.py:316
  16.1 14.5 %collective-permute-start.2 = (bf16[1,768,2048]{2,1,0:T(8,128)(2,1)}, bf16[1,768,2048]{2,1,0:T(8,128)(2,1)}, u32[]{:S(2)}, u32[]{:S(2)}) collective-permute-start(bf16[1,768,2048]{2,1,0:T(8,128)(2,1)} %refs_2_.1), channel_id=1, source_target_pairs={{0,1},{1,0},{2,3},{3,2},{4,5},{5,4},{6,7},{7,6},{8,9},{9,8},{10,11... | collective-permute-start | bytes 9437192 | tf_op jit(solution)/shard_map/ppermute | solution.py:316
  107.9 12.3 %copy-start.3 = (bf16[128,8]{0,1:T(8,128)(2,1)S(1)}, bf16[128,8]{0,1:T(8,128)(2,1)}, u32[]{:S(2)}) copy-start(bf16[128,8]{0,1:T(8,128)(2,1)} %param.8) | copy-start | bytes 6148
  107.9 89.2 %all-to-all-start.1 = ((bf16[128,8,3072]{2,1,0:T(8,128)(2,1)}), bf16[128,8,3072]{2,1,0:T(8,128)(2,1)}, u32[]{:S(2)}, u32[]{:S(2)}) async-start(bf16[128,8,3072]{2,1,0:T(8,128)(2,1)} %expert.1), calls=%async_computation.1 | async-start | bytes 12582912 | tf_op jit(solution)/shard_map/all_to_all | solution.py:312
  121.1 0.8 copy-start
  121.9 0.7 copy-start.1

commit v9 on v8

--- a/solution.py
+++ b/solution.py
@@ -121,7 +121,7 @@
     extra_ref[1] = jnp.where(first_half(own.shape), 0.0, extra).T.astype(BF16)
 
 
-CHUNKS = 4
+CHUNKS = 8
 
 
 def expert_loads(sources, weights, sems):
@@ -134,14 +134,26 @@
     return loads
 
 
+def arriving(blocks, weight, loads):
+    parts = 2
+    run = weight.shape[0] // parts
+    totals = [None] * len(blocks)
+    for part in range(parts):
+        wait_all(loads[part * CHUNKS // parts : (part + 1) * CHUNKS // parts])
+        here = slice(part * run, (part + 1) * run)
+        outs = [dot(rows[:, here], weight[here]) for rows in blocks]
+        totals = [out if total is None else total + out for total, out in zip(totals, outs)]
+    return totals
+
+
 def expert_rows(blocks, weights, loads=None):
     gate_w, up_w, down_w = weights
     if loads:
-        wait_all(loads[:CHUNKS])
-    gates = [dot(rows, gate_w[...]) for rows in blocks]
-    if loads:
-        wait_all(loads[CHUNKS : 2 * CHUNKS])
-    ups = [dot(rows, up_w[...]) for rows in blocks]
+        gates = arriving(blocks, gate_w, loads[:CHUNKS])
+        ups = arriving(blocks, up_w, loads[CHUNKS : 2 * CHUNKS])
+    else:
+        gates = [dot(rows, gate_w[...]) for rows in blocks]
+        ups = [dot(rows, up_w[...]) for rows in blocks]
     hidden = [(g / (1.0 + jnp.exp(-g)) * u).astype(BF16) for g, u in zip(gates, ups)]
     if loads:
         wait_all(loads[2 * CHUNKS :])
@@ -250,9 +262,9 @@
         copy.start()
     wait_all(w_copies)
     totals = [None, None]
-    for pair in range(0, runs, 2):
-        wait_all(copies[pair : pair + 2])
-        here = slice(pair * run, (pair + 2) * run)
+    for first in range(0, runs, 4):
+        wait_all(copies[first : first + 4])
+        here = slice(first * run, (first + 4) * run)
         extra = held[here, width:]
         for side in range(2):
             rows = held[here, side * half : (side + 1) * half]
@@ -365,7 +377,7 @@
             pltpu.VMEM((count, full), BF16),
             pltpu.VMEM((tokens, width), BF16),
             pltpu.SemaphoreType.DMA((2,)),
-            pltpu.SemaphoreType.DMA((8,)),
+            pltpu.SemaphoreType.DMA((16,)),
             pltpu.SemaphoreType.DMA((2,)),
         ],
         compiler_params=params(60),

time: 203 us -> 205 us (level)
  no operation moved by 1% of the time
where the time goes in v9:
time: 205 us
  waiting for transfers between devices  149 us (73%)
  Pallas kernels  27.4 us (13%)
  starting transfers between devices  24.9 us (12%)
    all_to_all x2, waiting for transfers between devices, exchange(): lax.all_to_all(rows, ('node', 'local'), split_axis=0, concat_axis=0, tile...  136 us
    all_to_all x2, starting transfers between devices, exchange(): lax.all_to_all(rows, ('node', 'local'), split_axis=0, concat_axis=0, tile...  24.2 us
    pallas_call x1, Pallas kernels, shards(): pl.pallas_call(expert_kernel, in_specs=[pl.BlockSpec(memory_space=pltpu.S...  16.7 us
    ppermute x3, waiting for transfers between devices, shards(): lax.ppermute(weight, 'local', cores)  12.5 us
    pallas_call x1, Pallas kernels, shards(): pl.pallas_call(combine_kernel, in_specs=[hbm()] * 3, out_specs=hbm(), out...  5.23 us
    pallas_call x1, Pallas kernels, shards(): pl.pallas_call(send_kernel, in_specs=[hbm(), hbm()], out_specs=hbm(), out...  4.52 us
  transfers between devices with their start and end apart: 5, of which 5 were waited for; matrix products, arithmetic and copies ran while one was open for 0% of the time, Pallas kernels for 0%

profile of v9, /device:TPU:2, one launch (start us, length us, event | category | flops | bytes accessed | tf_op | source)
XLA Modules:
  0.0 204.7 jit_solution(2738613877361542142)
XLA Ops:
  0.0 4.5 %send_rows.1 = bf16[128,8,3072]{2,1,0:T(8,128)(2,1)} custom-call(s32[8,128]{1,0:T(8,128)} %bitcast.4, bf16[128,2048]{1,0:T(8,128)(2,1)} %acts_hbm.1), custom_call_target="tpu_custom_call" | custom-call | tf_op jit(solution)/shard_map/send_rows/pallas_call | solution.py:307
  4.5 0.0 copy-start.4
  4.5 0.0 copy-start.2
  4.6 10.9 %all-to-all-start = ((bf16[128,8,3072]{2,1,0:T(8,128)(2,1)}), bf16[128,8,3072]{2,1,0:T(8,128)(2,1)}, u32[]{:S(2)}, u32[]{:S(2)}) async-start(bf16[128,8,3072]{2,1,0:T(8,128)(2,1)} %send_rows.1), calls=%async_computation | async-start | bytes 12582912 | tf_op jit(solution)/shard_map/all_to_all | solution.py:324
  15.5 0.0 copy-done.4
  15.5 0.2 collective-permute-start
  15.7 0.4 collective-permute-start.1
  16.1 0.1 collective-permute-start.2
  16.2 0.0 copy-done.2
  16.3 0.6 convert_reduce_fusion
  18.1 6.3 %collective-permute-done.refs_3_ = bf16[1,2048,768]{2,1,0:T(8,128)(2,1)} collective-permute-done((bf16[1,2048,768]{2,1,0:T(8,128)(2,1)S(1)}, bf16[1,2048,768]{2,1,0:T(8,128)(2,1)}, u32[]{:S(2)}, u32[]{:S(2)}) %collective-permute-start) | collective-permute-done | bytes 3145760 | tf_op jit(solution)/shard_map/ppermute | solution.py:328
  24.4 1.7 collective-permute-done.1.refs_4_
  26.1 4.5 %collective-permute-done.2.refs_5_ = bf16[1,768,2048]{2,1,0:T(8,128)(2,1)} collective-permute-done((bf16[1,768,2048]{2,1,0:T(8,128)(2,1)}, bf16[1,768,2048]{2,1,0:T(8,128)(2,1)}, u32[]{:S(2)}, u32[]{:S(2)}) %collective-permute-start.2) | collective-permute-done | bytes 3145760 | tf_op jit(solution)/shard_map/ppermute | solution.py:328
  30.6 61.8 %all-to-all-done.rows_hbm = bf16[128,8,3072]{2,1,0:T(8,128)(2,1)} async-done(((bf16[128,8,3072]{2,1,0:T(8,128)(2,1)}), bf16[128,8,3072]{2,1,0:T(8,128)(2,1)}, u32[]{:S(2)}, u32[]{:S(2)}) %all-to-all-start) | async-done | bytes 6291488 | tf_op jit(solution)/shard_map/all_to_all | solution.py:324
  92.4 16.7 %expert.1 = bf16[128,8,3072]{2,1,0:T(8,128)(2,1)} custom-call(s32[1]{0:T(128)} %bitcast.2.mode_ref, bf16[128,8,3072]{2,1,0:T(8,128)(2,1)} %all-to-all-done.rows_hbm, bf16[1,2048,768]{2,1,0:T(8,128)(2,1)} %refs_0_.1, bf16[1,2048,768]{2,1,0:T(8,128)(2,1)} %refs_1_.1, bf16[1,768,2048]{2,1,0:T(8,128)(2,1)} %refs_2_.1, ...), custom_call_target="tpu_custom_call" | custom-call | flops 14495514624 | bytes 31457280 | tf_op jit(solution)/shard_map/expert/pallas_call | solution.py:335
  109.1 0.0 copy-start.3
  109.2 13.2 %all-to-all-start.1 = ((bf16[128,8,3072]{2,1,0:T(8,128)(2,1)}), bf16[128,8,3072]{2,1,0:T(8,128)(2,1)}, u32[]{:S(2)}, u32[]{:S(2)}) async-start(bf16[128,8,3072]{2,1,0:T(8,128)(2,1)} %expert.1), calls=%async_computation.1 | async-start | bytes 12582912 | tf_op jit(solution)/shard_map/all_to_all | solution.py:324
  122.4 0.0 copy-done.3
  122.4 0.9 combine_weights.1
  123.3 0.0 copy-start
  123.3 0.8 copy-done
  124.1 0.7 copy-done.1
  124.8 74.5 %all-to-all-done.1 = bf16[128,8,3072]{2,1,0:T(8,128)(2,1)} async-done(((bf16[128,8,3072]{2,1,0:T(8,128)(2,1)}), bf16[128,8,3072]{2,1,0:T(8,128)(2,1)}, u32[]{:S(2)}, u32[]{:S(2)}) %all-to-all-start.1) | async-done | bytes 6291488 | tf_op jit(solution)/shard_map/all_to_all | solution.py:324
  199.3 5.2 %combine.1 = bf16[128,2048]{1,0:T(8,128)(2,1)} custom-call(bf16[128,1024]{1,0:T(8,128)(2,1)} %copy-done.1, bf16[2,128,1024]{2,1,0:T(8,128)(2,1)} %copy-done, bf16[1024,3072]{1,0:T(8,128)(2,1)} %bitcast.3.rows_hbm), custom_call_target="tpu_custom_call" | custom-call | tf_op jit(solution)/shard_map/combine/pallas_call | solution.py:369
  (1 shorter events, 0.0 us)
Async XLA Ops:
  4.5 11.0 %copy-start.4 = (bf16[1,2048,768]{2,1,0:T(8,128)(2,1)S(1)}, bf16[1,2048,768]{2,1,0:T(8,128)(2,1)}, u32[]{:S(2)}) copy-start(bf16[1,2048,768]{2,1,0:T(8,128)(2,1)} %refs_0_.1) | copy-start | bytes 9437188
  4.5 11.7 %copy-start.2 = (s32[128,8]{0,1:T(8,128)S(1)}, s32[128,8]{0,1:T(8,128)}, u32[]{:S(2)}) copy-start(s32[128,8]{0,1:T(8,128)} %param.7) | copy-start | bytes 12292
  4.6 87.9 %all-to-all-start = ((bf16[128,8,3072]{2,1,0:T(8,128)(2,1)}), bf16[128,8,3072]{2,1,0:T(8,128)(2,1)}, u32[]{:S(2)}, u32[]{:S(2)}) async-start(bf16[128,8,3072]{2,1,0:T(8,128)(2,1)} %send_rows.1), calls=%async_computation | async-start | bytes 12582912 | tf_op jit(solution)/shard_map/all_to_all | solution.py:324
  15.5 8.9 %collective-permute-start = (bf16[1,2048,768]{2,1,0:T(8,128)(2,1)S(1)}, bf16[1,2048,768]{2,1,0:T(8,128)(2,1)}, u32[]{:S(2)}, u32[]{:S(2)}) collective-permute-start(bf16[1,2048,768]{2,1,0:T(8,128)(2,1)S(1)} %copy-done.4), channel_id=1, source_target_pairs={{0,1},{1,0},{2,3},{3,2},{4,5},{5,4},{6,7},{7,6},{8,9},{9,8},{10,11... | collective-permute-start | bytes 9437192 | tf_op jit(solution)/shard_map/ppermute | solution.py:328
  15.7 10.4 %collective-permute-start.1 = (bf16[1,2048,768]{2,1,0:T(8,128)(2,1)}, bf16[1,2048,768]{2,1,0:T(8,128)(2,1)}, u32[]{:S(2)}, u32[]{:S(2)}) collective-permute-start(bf16[1,2048,768]{2,1,0:T(8,128)(2,1)} %refs_1_.1), channel_id=1, source_target_pairs={{0,1},{1,0},{2,3},{3,2},{4,5},{5,4},{6,7},{7,6},{8,9},{9,8},{10,11... | collective-permute-start | bytes 9437192 | tf_op jit(solution)/shard_map/ppermute | solution.py:328
  16.1 14.5 %collective-permute-start.2 = (bf16[1,768,2048]{2,1,0:T(8,128)(2,1)}, bf16[1,768,2048]{2,1,0:T(8,128)(2,1)}, u32[]{:S(2)}, u32[]{:S(2)}) collective-permute-start(bf16[1,768,2048]{2,1,0:T(8,128)(2,1)} %refs_2_.1), channel_id=1, source_target_pairs={{0,1},{1,0},{2,3},{3,2},{4,5},{5,4},{6,7},{7,6},{8,9},{9,8},{10,11... | collective-permute-start | bytes 9437192 | tf_op jit(solution)/shard_map/ppermute | solution.py:328
  109.1 13.2 %copy-start.3 = (bf16[128,8]{0,1:T(8,128)(2,1)S(1)}, bf16[128,8]{0,1:T(8,128)(2,1)}, u32[]{:S(2)}) copy-start(bf16[128,8]{0,1:T(8,128)(2,1)} %param.8) | copy-start | bytes 6148
  109.2 90.2 %all-to-all-start.1 = ((bf16[128,8,3072]{2,1,0:T(8,128)(2,1)}), bf16[128,8,3072]{2,1,0:T(8,128)(2,1)}, u32[]{:S(2)}, u32[]{:S(2)}) async-start(bf16[128,8,3072]{2,1,0:T(8,128)(2,1)} %expert.1), calls=%async_computation.1 | async-start | bytes 12582912 | tf_op jit(solution)/shard_map/all_to_all | solution.py:324
  123.3 0.8 copy-start
  124.1 0.7 copy-start.1

commit v10 on v8

--- a/solution.py
+++ b/solution.py
@@ -121,7 +121,7 @@
     extra_ref[1] = jnp.where(first_half(own.shape), 0.0, extra).T.astype(BF16)
 
 
-CHUNKS = 4
+CHUNKS = 2
 
 
 def expert_loads(sources, weights, sems):

time: 203 us -> 204 us (level)
  no operation moved by 1% of the time
where the time goes in v10:
time: 204 us; the launch traced here: 203 us
  waiting for transfers between devices  149 us (73%)
  Pallas kernels  25.8 us (13%)
  starting transfers between devices  25.1 us (12%)
    all_to_all x2, waiting for transfers between devices, exchange(): lax.all_to_all(rows, ('node', 'local'), split_axis=0, concat_axis=0, tile...  136 us
    all_to_all x2, starting transfers between devices, exchange(): lax.all_to_all(rows, ('node', 'local'), split_axis=0, concat_axis=0, tile...  24.3 us
    pallas_call x1, Pallas kernels, shards(): pl.pallas_call(expert_kernel, in_specs=[pl.BlockSpec(memory_space=pltpu.S...  15.4 us
    ppermute x3, waiting for transfers between devices, shards(): lax.ppermute(weight, 'local', cores)  12.5 us
    pallas_call x1, Pallas kernels, shards(): pl.pallas_call(combine_kernel, in_specs=[hbm()] * 3, out_specs=hbm(), out...  5.04 us
    pallas_call x1, Pallas kernels, shards(): pl.pallas_call(send_kernel, in_specs=[hbm(), hbm()], out_specs=hbm(), out...  4.52 us
  transfers between devices with their start and end apart: 5, of which 5 were waited for; matrix products, arithmetic and copies ran while one was open for 0% of the time, Pallas kernels for 0%

profile of v10, /device:TPU:2, one launch (start us, length us, event | category | flops | bytes accessed | tf_op | source)
XLA Modules:
  0.0 203.3 jit_solution(7295373719569766808)
XLA Ops:
  0.0 4.5 %send_rows.1 = bf16[128,8,3072]{2,1,0:T(8,128)(2,1)} custom-call(s32[8,128]{1,0:T(8,128)} %bitcast.4, bf16[128,2048]{1,0:T(8,128)(2,1)} %acts_hbm.1), custom_call_target="tpu_custom_call" | custom-call | tf_op jit(solution)/shard_map/send_rows/pallas_call | solution.py:295
  4.5 0.0 copy-start.4
  4.5 0.0 copy-start.2
  4.6 10.9 %all-to-all-start = ((bf16[128,8,3072]{2,1,0:T(8,128)(2,1)}), bf16[128,8,3072]{2,1,0:T(8,128)(2,1)}, u32[]{:S(2)}, u32[]{:S(2)}) async-start(bf16[128,8,3072]{2,1,0:T(8,128)(2,1)} %send_rows.1), calls=%async_computation | async-start | bytes 12582912 | tf_op jit(solution)/shard_map/all_to_all | solution.py:312
  15.5 0.0 copy-done.4
  15.5 0.2 collective-permute-start
  15.7 0.4 collective-permute-start.1
  16.1 0.1 collective-permute-start.2
  16.2 0.0 copy-done.2
  16.3 0.6 convert_reduce_fusion
  18.1 6.3 %collective-permute-done.refs_3_ = bf16[1,2048,768]{2,1,0:T(8,128)(2,1)} collective-permute-done((bf16[1,2048,768]{2,1,0:T(8,128)(2,1)S(1)}, bf16[1,2048,768]{2,1,0:T(8,128)(2,1)}, u32[]{:S(2)}, u32[]{:S(2)}) %collective-permute-start) | collective-permute-done | bytes 3145760 | tf_op jit(solution)/shard_map/ppermute | solution.py:316
  24.4 1.7 collective-permute-done.1.refs_4_
  26.1 4.5 %collective-permute-done.2.refs_5_ = bf16[1,768,2048]{2,1,0:T(8,128)(2,1)} collective-permute-done((bf16[1,768,2048]{2,1,0:T(8,128)(2,1)}, bf16[1,768,2048]{2,1,0:T(8,128)(2,1)}, u32[]{:S(2)}, u32[]{:S(2)}) %collective-permute-start.2) | collective-permute-done | bytes 3145760 | tf_op jit(solution)/shard_map/ppermute | solution.py:316
  30.6 61.8 %all-to-all-done.rows_hbm = bf16[128,8,3072]{2,1,0:T(8,128)(2,1)} async-done(((bf16[128,8,3072]{2,1,0:T(8,128)(2,1)}), bf16[128,8,3072]{2,1,0:T(8,128)(2,1)}, u32[]{:S(2)}, u32[]{:S(2)}) %all-to-all-start) | async-done | bytes 6291488 | tf_op jit(solution)/shard_map/all_to_all | solution.py:312
  92.4 15.4 %expert.1 = bf16[128,8,3072]{2,1,0:T(8,128)(2,1)} custom-call(s32[1]{0:T(128)} %bitcast.2.mode_ref, bf16[128,8,3072]{2,1,0:T(8,128)(2,1)} %all-to-all-done.rows_hbm, bf16[1,2048,768]{2,1,0:T(8,128)(2,1)} %refs_0_.1, bf16[1,2048,768]{2,1,0:T(8,128)(2,1)} %refs_1_.1, bf16[1,768,2048]{2,1,0:T(8,128)(2,1)} %refs_2_.1, ...), custom_call_target="tpu_custom_call" | custom-call | flops 14495514624 | bytes 31457280 | tf_op jit(solution)/shard_map/expert/pallas_call | solution.py:323
  107.8 0.0 copy-start.3
  107.8 13.4 %all-to-all-start.1 = ((bf16[128,8,3072]{2,1,0:T(8,128)(2,1)}), bf16[128,8,3072]{2,1,0:T(8,128)(2,1)}, u32[]{:S(2)}, u32[]{:S(2)}) async-start(bf16[128,8,3072]{2,1,0:T(8,128)(2,1)} %expert.1), calls=%async_computation.1 | async-start | bytes 12582912 | tf_op jit(solution)/shard_map/all_to_all | solution.py:312
  121.2 0.0 copy-done.3
  121.2 0.9 combine_weights.1
  122.1 0.0 copy-start
  122.1 0.8 copy-done
  122.9 0.7 copy-done.1
  123.6 74.5 %all-to-all-done.1 = bf16[128,8,3072]{2,1,0:T(8,128)(2,1)} async-done(((bf16[128,8,3072]{2,1,0:T(8,128)(2,1)}), bf16[128,8,3072]{2,1,0:T(8,128)(2,1)}, u32[]{:S(2)}, u32[]{:S(2)}) %all-to-all-start.1) | async-done | bytes 6291488 | tf_op jit(solution)/shard_map/all_to_all | solution.py:312
  198.1 5.0 %combine.1 = bf16[128,2048]{1,0:T(8,128)(2,1)} custom-call(bf16[128,1024]{1,0:T(8,128)(2,1)} %copy-done.1, bf16[2,128,1024]{2,1,0:T(8,128)(2,1)} %copy-done, bf16[1024,3072]{1,0:T(8,128)(2,1)} %bitcast.3.rows_hbm), custom_call_target="tpu_custom_call" | custom-call | tf_op jit(solution)/shard_map/combine/pallas_call | solution.py:357
  (1 shorter events, 0.0 us)
Async XLA Ops:
  4.5 11.0 %copy-start.4 = (bf16[1,2048,768]{2,1,0:T(8,128)(2,1)S(1)}, bf16[1,2048,768]{2,1,0:T(8,128)(2,1)}, u32[]{:S(2)}) copy-start(bf16[1,2048,768]{2,1,0:T(8,128)(2,1)} %refs_0_.1) | copy-start | bytes 9437188
  4.5 11.7 %copy-start.2 = (s32[128,8]{0,1:T(8,128)S(1)}, s32[128,8]{0,1:T(8,128)}, u32[]{:S(2)}) copy-start(s32[128,8]{0,1:T(8,128)} %param.7) | copy-start | bytes 12292
  4.6 87.9 %all-to-all-start = ((bf16[128,8,3072]{2,1,0:T(8,128)(2,1)}), bf16[128,8,3072]{2,1,0:T(8,128)(2,1)}, u32[]{:S(2)}, u32[]{:S(2)}) async-start(bf16[128,8,3072]{2,1,0:T(8,128)(2,1)} %send_rows.1), calls=%async_computation | async-start | bytes 12582912 | tf_op jit(solution)/shard_map/all_to_all | solution.py:312
  15.5 8.9 %collective-permute-start = (bf16[1,2048,768]{2,1,0:T(8,128)(2,1)S(1)}, bf16[1,2048,768]{2,1,0:T(8,128)(2,1)}, u32[]{:S(2)}, u32[]{:S(2)}) collective-permute-start(bf16[1,2048,768]{2,1,0:T(8,128)(2,1)S(1)} %copy-done.4), channel_id=1, source_target_pairs={{0,1},{1,0},{2,3},{3,2},{4,5},{5,4},{6,7},{7,6},{8,9},{9,8},{10,11... | collective-permute-start | bytes 9437192 | tf_op jit(solution)/shard_map/ppermute | solution.py:316
  15.7 10.4 %collective-permute-start.1 = (bf16[1,2048,768]{2,1,0:T(8,128)(2,1)}, bf16[1,2048,768]{2,1,0:T(8,128)(2,1)}, u32[]{:S(2)}, u32[]{:S(2)}) collective-permute-start(bf16[1,2048,768]{2,1,0:T(8,128)(2,1)} %refs_1_.1), channel_id=1, source_target_pairs={{0,1},{1,0},{2,3},{3,2},{4,5},{5,4},{6,7},{7,6},{8,9},{9,8},{10,11... | collective-permute-start | bytes 9437192 | tf_op jit(solution)/shard_map/ppermute | solution.py:316
  16.1 14.5 %collective-permute-start.2 = (bf16[1,768,2048]{2,1,0:T(8,128)(2,1)}, bf16[1,768,2048]{2,1,0:T(8,128)(2,1)}, u32[]{:S(2)}, u32[]{:S(2)}) collective-permute-start(bf16[1,768,2048]{2,1,0:T(8,128)(2,1)} %refs_2_.1), channel_id=1, source_target_pairs={{0,1},{1,0},{2,3},{3,2},{4,5},{5,4},{6,7},{7,6},{8,9},{9,8},{10,11... | collective-permute-start | bytes 9437192 | tf_op jit(solution)/shard_map/ppermute | solution.py:316
  107.8 13.4 %copy-start.3 = (bf16[128,8]{0,1:T(8,128)(2,1)S(1)}, bf16[128,8]{0,1:T(8,128)(2,1)}, u32[]{:S(2)}) copy-start(bf16[128,8]{0,1:T(8,128)(2,1)} %param.8) | copy-start | bytes 6148
  107.8 90.3 %all-to-all-start.1 = ((bf16[128,8,3072]{2,1,0:T(8,128)(2,1)}), bf16[128,8,3072]{2,1,0:T(8,128)(2,1)}, u32[]{:S(2)}, u32[]{:S(2)}) async-start(bf16[128,8,3072]{2,1,0:T(8,128)(2,1)} %expert.1), calls=%async_computation.1 | async-start | bytes 12582912 | tf_op jit(solution)/shard_map/all_to_all | solution.py:312
  122.1 0.8 copy-start
  122.9 0.7 copy-start.1
